TPU v7x, 32 devices: a whole 2x2x4 slice. The times are simulated.
32 devices in a mesh: seq: 16 (over z, y, x), rep: 2 (over core).
Axes of the slice: x: 2, y: 2, z: 4, core: 2. Of those that a mesh axis runs over, the one named last changes fastest.
Arguments:
- series: float32 [2, 160, 1440], P('rep', None, 'seq'), may hold values from -60 to 60
- group_ids: int32 [160], replicated, may hold values from 0 to 3
- rev_gain: float32 [160], replicated, may hold values from 0.5 to 1.5
- rev_bias: float32 [160], replicated, may hold values from -4 to 4
- mode_in: float32 [256, 4], replicated, may hold values from -0.375 to 0.375
- mode_out: float32 [256, 4], replicated, may hold values from -0.375 to 0.375
- mode_re: float32 [4, 32], replicated, may hold values from -24 to 24
- mode_im: float32 [4, 32], replicated, may hold values from -24 to 24
- mixing: float32 [160, 160], replicated, may hold values from -1 to 1
- out_bias: float32 [160], replicated, may hold values from -6 to 6
- cotangent: float32 [2, 160, 1440], P('rep', None, 'seq'), may hold values from -6 to 6
Outputs:
- layer_out: float32 [2, 160, 1440], P('rep', None, 'seq')
- series_grad: float32 [2, 160, 1440], P('rep', None, 'seq')
- rev_gain_grad: float32 [160], replicated
- rev_bias_grad: float32 [160], replicated
- mode_in_grad: float32 [256, 4], replicated
- mode_out_grad: float32 [256, 4], replicated
- mode_re_grad: float32 [4, 32], replicated
- mode_im_grad: float32 [4, 32], replicated
- mixing_grad: float32 [160, 160], replicated
- out_bias_grad: float32 [160], replicated
All inputs are finite; a program needn't handle non-finite values.
Results may differ from a plain program's by a relative error of at most 0.0003.
Values sent between devices are 32-bit elements; how exact they have to be, the bound alone decides.
No kernel may reach another device: no remote copies, remote signals or barrier semaphores. Data moves between devices by JAX's collectives and lax.ppermute only.
A program may use at most 192 MiB of HBM per device.

v0:
```python
import math

import jax
import jax.numpy as jnp
from jax import lax
from jax.sharding import PartitionSpec as P

ORDER = 256
MODES = 32
RANK = 4
WINDOW = 720


epsilon = 1e-05
precise = lax.Precision.HIGHEST


def entering(shard, axis, combine, identity, reverse):
    size, place = (lax.axis_size(axis), lax.axis_index(axis))
    everything = jax.tree.map(lambda part: lax.all_gather(part, axis), shard)
    start = jax.tree.map(
        lambda part, zero: jnp.broadcast_to(jnp.asarray(zero, part.dtype), part.shape),
        shard,
        identity,
    )

    def turn(k, before):
        at = size - 1 - k if reverse else k
        reached = at > place if reverse else at < place
        new = combine(before, jax.tree.map(lambda part: part[at], everything))
        return jax.tree.map(lambda a, b: jnp.where(reached, a, b), new, before)

    return lax.fori_loop(0, size, turn, start)


def legendre_rows(degrees, window):
    lag_index = jnp.arange(window).astype(jnp.float32)
    points = 1.0 - 2.0 * (lag_index + 0.5) / window

    def advance(state_pair, degree):
        lower_poly, this_poly = state_pair
        upper_poly = ((2.0 * degree + 1.0) * points * this_poly - degree * lower_poly) / (
            degree + 1.0
        )
        return ((this_poly, upper_poly), this_poly)

    initial = (jnp.zeros_like(points), jnp.ones_like(points))
    unused, legendre = lax.scan(advance, initial, jnp.arange(degrees).astype(jnp.float32))
    return legendre


def wave_tables(mode_count, window):
    phase_index = jnp.arange(mode_count)[:, None] * jnp.arange(window)[None, :] % window
    angles = 2.0 * math.pi / window * phase_index.astype(jnp.float32)
    return (jnp.cos(angles), jnp.sin(angles))


def add_pairs(earlier, later):
    return (earlier[0] + later[0], earlier[1] + later[1])


def band_table(kernel, rows, cols, offset):
    row_index = jnp.arange(rows)[:, None]
    col_index = jnp.arange(cols)[None, :]
    lag = col_index + offset - row_index
    valid = (lag >= 0) & (lag < WINDOW)
    picked = kernel[:, jnp.clip(lag, 0, WINDOW - 1)]
    return jnp.where(valid[None], picked, 0.0)


def band_kernel_grad(kernel, rows, cols, offset, table_grad):
    unused, pullback = jax.vjp(lambda values: band_table(values, rows, cols, offset), kernel)
    return pullback(table_grad)[0]


def to_modes(signal, cosine, sine_table):
    framed = signal.reshape(signal.shape[:-1] + (-1, cosine.shape[1]))
    real_part = jnp.einsum("...kt,mt->...km", framed, cosine, precision=precise)
    imag_part = -jnp.einsum("...kt,mt->...km", framed, sine_table, precision=precise)
    return (real_part, imag_part)


def from_modes(real_part, imag_part, cosine, sine_table, mode_scale):
    framed = jnp.einsum("...km,mt->...kt", real_part * mode_scale, cosine, precision=precise)
    framed = framed - jnp.einsum(
        "...km,mt->...kt", imag_part * mode_scale, sine_table, precision=precise
    )
    return framed.reshape(framed.shape[:-2] + (-1,))


def body(
    series,
    group_ids,
    rev_gain,
    rev_bias,
    mode_in,
    mode_out,
    mode_re,
    mode_im,
    mixing,
    out_bias,
    cotangent,
):
    samples, channels, local_steps = series.shape
    legendre = legendre_rows(ORDER, WINDOW)
    degree = jnp.arange(ORDER).astype(jnp.float32)
    weights = legendre * ((2.0 * degree + 1.0) / WINDOW)[:, None]
    kernel = jnp.dot(mode_in.T, weights, precision=precise)
    endpoint = legendre[:, 0]
    recon_mix = jnp.dot(endpoint, mode_out, precision=precise)
    cosine, sine_table = wave_tables(MODES, WINDOW)
    mode_scale = jnp.where(jnp.arange(MODES) == 0, 1.0, 2.0) / WINDOW
    gain_re = mode_re[:, None, :]
    gain_im = mode_im[:, None, :]
    triangle = (jnp.arange(local_steps)[:, None] <= jnp.arange(local_steps)[None, :]).astype(
        jnp.float32
    )
    local_one = jnp.einsum("bct,ts->bcs", series, triangle, precision=precise)
    local_two = jnp.einsum("bct,ts->bcs", series * series, triangle, precision=precise)
    blank = jnp.zeros((samples, channels), jnp.float32)
    earlier = entering(
        (local_one[:, :, -1], local_two[:, :, -1]), "seq", add_pairs, (blank, blank), False
    )
    denominator = (
        lax.axis_index("seq") * local_steps + jnp.arange(local_steps) + 1 + WINDOW
    ).astype(jnp.float32)
    running_mean = (local_one + earlier[0][:, :, None]) / denominator
    variance = (
        local_two + earlier[1][:, :, None] + WINDOW
    ) / denominator - running_mean * running_mean
    spread = jnp.sqrt(variance + epsilon)
    centered = (series - running_mean) / spread
    normal = rev_gain[None, :, None] * centered + rev_bias[None, :, None]
    hop_count = (WINDOW - 2) // local_steps + 1
    span_rows = (hop_count + 1) * local_steps
    table = band_table(kernel, span_rows, local_steps, hop_count * local_steps)
    regrouped = lax.all_to_all(normal, "seq", split_axis=1, concat_axis=2, tiled=True)
    own_channels = regrouped.shape[1]
    block_count = regrouped.shape[2] // local_steps
    padded_in = jnp.pad(regrouped, ((0, 0), (0, 0), (hop_count * local_steps, 0)))
    blocked_in = padded_in.reshape(samples, own_channels, block_count + hop_count, local_steps)
    framed_in = jnp.concatenate(
        [blocked_in[:, :, offset : offset + block_count] for offset in range(hop_count + 1)], axis=3
    )
    coeffs = jnp.einsum("bcks,rst->bcrkt", framed_in, table, precision=precise).reshape(
        samples, own_channels, RANK, -1
    )
    coeff_re, coeff_im = to_modes(coeffs, cosine, sine_table)
    filtered_re = gain_re * coeff_re - gain_im * coeff_im
    filtered_im = gain_re * coeff_im + gain_im * coeff_re
    rebuilt = from_modes(filtered_re, filtered_im, cosine, sine_table, mode_scale)
    recon_local = jnp.einsum("bcrt,r->bct", rebuilt, recon_mix, precision=precise)
    recon_time = lax.all_to_all(recon_local, "seq", split_axis=2, concat_axis=1, tiled=True)
    same_group = (group_ids[:, None] == group_ids[None, :]).astype(jnp.float32)
    masked = mixing * same_group
    shifted = (recon_time - rev_bias[None, :, None]) / rev_gain[None, :, None]
    restored = shifted * spread + running_mean
    layer_out = (
        series
        + jnp.einsum("ij,bjt->bit", masked, restored, precision=precise)
        + out_bias[None, :, None]
    )
    bias_grad = jnp.sum(cotangent, axis=(0, 2))
    mixing_grad = same_group * jnp.einsum("bit,bjt->ij", cotangent, restored, precision=precise)
    restored_grad = jnp.einsum("ij,bit->bjt", masked, cotangent, precision=precise)
    recon_grad = restored_grad * spread / rev_gain[None, :, None]
    gain_grad = -jnp.sum(restored_grad * spread * shifted, axis=(0, 2)) / rev_gain
    offset_grad = -jnp.sum(restored_grad * spread, axis=(0, 2)) / rev_gain
    spread_grad = restored_grad * shifted
    mean_grad = restored_grad
    recon_grad_owned = lax.all_to_all(recon_grad, "seq", split_axis=1, concat_axis=2, tiled=True)
    wave_grad = recon_grad_owned[:, :, None, :] * recon_mix[None, None, :, None]
    recon_mix_grad = jnp.einsum("bct,bcrt->r", recon_grad_owned, rebuilt, precision=precise)
    sum_re, sum_im = to_modes(wave_grad, cosine, sine_table)
    grad_re = mode_scale * sum_re
    grad_im = mode_scale * sum_im
    mode_re_grad = jnp.sum(grad_re * coeff_re + grad_im * coeff_im, axis=(0, 1, 3))
    mode_im_grad = jnp.sum(grad_im * coeff_re - grad_re * coeff_im, axis=(0, 1, 3))
    back_re = gain_re * grad_re + gain_im * grad_im
    back_im = gain_re * grad_im - gain_im * grad_re
    coeff_grad = from_modes(back_re, back_im, cosine, sine_table, 1.0)
    blocked_grad = coeff_grad.reshape(samples, own_channels, RANK, block_count, local_steps)
    framed_grad = jnp.einsum("bcrkt,rst->bcks", blocked_grad, table, precision=precise)
    table_grad = jnp.einsum("bcks,bcrkt->rst", framed_in, blocked_grad, precision=precise)
    kernel_grad = band_kernel_grad(
        kernel, span_rows, local_steps, hop_count * local_steps, table_grad
    )
    folded = jnp.zeros((samples, own_channels, block_count + hop_count, local_steps), jnp.float32)
    for offset in range(hop_count + 1):
        piece = framed_grad[:, :, :, offset * local_steps : (offset + 1) * local_steps]
        folded = folded + jnp.pad(piece, ((0, 0), (0, 0), (offset, hop_count - offset), (0, 0)))
    owned_grad = folded[:, :, hop_count:].reshape(samples, own_channels, -1)
    normal_grad = lax.all_to_all(owned_grad, "seq", split_axis=2, concat_axis=1, tiled=True)
    gain_grad = gain_grad + jnp.sum(normal_grad * centered, axis=(0, 2))
    offset_grad = offset_grad + jnp.sum(normal_grad, axis=(0, 2))
    scaled = normal_grad * rev_gain[None, :, None] / spread
    mean_grad = mean_grad - scaled
    spread_grad = spread_grad - scaled * centered
    variance_grad = spread_grad / (2.0 * spread)
    first_grad = (mean_grad - 2.0 * running_mean * variance_grad) / denominator
    second_grad = variance_grad / denominator
    later_sums = entering(
        (jnp.sum(first_grad, axis=2), jnp.sum(second_grad, axis=2)),
        "seq",
        add_pairs,
        (blank, blank),
        True,
    )
    suffix_one = (
        jnp.einsum("bcs,ts->bct", first_grad, triangle, precision=precise)
        + later_sums[0][:, :, None]
    )
    suffix_two = (
        jnp.einsum("bcs,ts->bct", second_grad, triangle, precision=precise)
        + later_sums[1][:, :, None]
    )
    series_grad = cotangent + scaled + suffix_one + 2.0 * series * suffix_two
    mode_in_grad = jnp.dot(weights, kernel_grad.T, precision=precise)
    mode_out_grad = endpoint[:, None] * recon_mix_grad[None, :]
    totals = lax.psum(
        (
            gain_grad,
            offset_grad,
            mode_in_grad,
            mode_out_grad,
            mode_re_grad,
            mode_im_grad,
            mixing_grad,
            bias_grad,
        ),
        ("seq", "rep"),
    )
    return (
        layer_out,
        series_grad,
        totals[0],
        totals[1],
        totals[2],
        totals[3],
        totals[4],
        totals[5],
        totals[6],
        totals[7],
    )


def solution(mesh):
    in_specs = (
        P("rep", None, "seq"),
        P(),
        P(),
        P(),
        P(),
        P(),
        P(),
        P(),
        P(),
        P(),
        P("rep", None, "seq"),
    )
    out_specs = (
        P("rep", None, "seq"),
        P("rep", None, "seq"),
        P(),
        P(),
        P(),
        P(),
        P(),
        P(),
        P(),
        P(),
    )
    return jax.shard_map(body, mesh=mesh, in_specs=in_specs, out_specs=out_specs, check_vma=False)
```

profile of v0, /device:TPU:0, one launch (start us, length us, event | category | flops | bytes accessed | tf_op | source)
XLA Modules:
  0.0 1642.2 jit_solution(18320291348270196528)
XLA Ops:
  7.2 1.1 fusion.87
  8.3 1.1 fusion.84
  9.5 42.4 %all-gather = f32[16,160,1]{1,2,0:T(1,128)S(1)} all-gather(f32[1,160,1]{1,2,0:T(1,128)S(1)} %copy.152), channel_id=2, replica_groups=mesh['seq'=16,'rep'=2] {'seq'}, dimensions={0}, use_global_device_ids=true | all-gather | bytes 10880 | tf_op jit(solution)/shard_map/all_gather | solution.py:20
  52.1 35.5 %all-gather.1 = f32[16,160,1]{1,2,0:T(1,128)S(1)} all-gather(f32[1,160,1]{1,2,0:T(1,128)S(1)} %copy.153), channel_id=3, replica_groups=mesh['seq'=16,'rep'=2] {'seq'}, dimensions={0}, use_global_device_ids=true | all-gather | bytes 10880 | tf_op jit(solution)/shard_map/all_gather | solution.py:20
  88.3 1.0 copy.174
  89.3 2.0 broadcast_divide_fusion
  91.3 3.5 all-to-all-start.2
  95.2 684.1 %while.49 = (s32[]{:T(128)}, f32[720]{0:T(1024)S(1)}, f32[720]{0:T(1024)S(1)}, f32[256,720]{1,0:T(8,128)S(1)}, f32[256]{0:T(256)S(1)}, /*index=5*/s32[]{:T(128)}, f32[]{:T(128)}, f32[]{:T(128)}, s32[]{:T(128)}) while((s32[]{:T(128)}, f32[720]{0:T(1024)S(1)}, f32[720]{0:T(1024)S(1)}, f32[256,720]{1,0:T(8,128)S(1)}, ...), condition=%wide.region_1.2_spmd.clone, body=%wide.region_0.1_spmd.clone.sunk | while | flops 7206 | bytes 23215 | solution.py:48
  781.4 133.9 %gather_fusion = f32[72900,4]{1,0:T(8,128)} fusion(f32[4,720]{0,1:T(8,128)S(1)} %copy.150, s32[73728]{0:T(1024)S(1)} %pad_clamp_fusion), kind=kCustom, calls=%fused_computation | custom fusion | bytes 2624400 | tf_op jit(solution)/shard_map/gather | solution.py:67
  915.4 19.7 %copy.151 = f32[72900,4]{0,1:T(4,128)S(1)} copy(f32[72900,4]{1,0:T(8,128)} %gather_fusion) | data formatting | bytes 2332800 | tf_op jit(solution)/shard_map/gather | solution.py:67
  935.2 1.7 reshape.356
  939.5 0.9 convolution_multiply_fusion
  940.3 0.9 fusion.22
  941.2 0.8 fusion.53
  942.1 0.8 convolution_subtract_fusion
  943.4 1.9 fusion.11
  945.9 0.9 copy.180
  947.4 8.0 reduce.14
  955.4 2.4 reshape.410
  957.8 7.0 all-to-all-start.3
  966.2 6.1 all-to-all-done.3
  972.4 0.8 reduce.15
  973.2 0.8 reshape.411
  976.1 3.5 all-to-all-start
  981.1 6.1 all-to-all-done
  988.5 1.3 concatenate.3
  989.8 1.5 fusion.14
  991.4 1.5 select_bitcast_fusion
  993.3 0.9 fusion.38
  994.1 1.4 subtract_reduce_fusion
  995.6 0.8 fusion.56
  998.3 0.9 copy.171
  999.2 6.8 reduce.16
  1006.0 1.3 reshape.408
  1007.2 3.7 all-to-all-start.1
  1011.5 1.6 reshape.363
  1013.2 17.8 %copy.189 = f32[72900,4]{1,0:T(8,128)} copy(f32[72900,4]{0,1:T(4,128)S(1)} %reshape.363) | data formatting | bytes 2332800 | tf_op jit(solution)/shard_map/transpose(jvp(jit(_where)))/select_n | solution.py:68
  1031.0 398.7 %scatter_custom_fusion = f32[4,720]{0,1:T(8,128)S(1)} fusion(s32[72900]{0:T(1024)} %copy-done.7, f32[72900,4]{1,0:T(8,128)} %copy.189, f32[]{:T(128)} %constant.129.clone.1), kind=kCustom, calls=%fused_computation.74 | custom fusion | flops 291600 | bytes 12032 | tf_op jit(solution)/shard_map/transpose(jvp())/scatter-add | solution.py:67
  1430.6 1.2 convolution_bitcast_fusion.5
  1431.9 0.9 reduce.17
  1432.8 0.8 reshape.409
  1434.5 1.0 fusion.17
  1435.4 1.2 fusion.21
  1437.6 77.0 %all-reduce.13 = (f32[2560]{0:T(1024)S(1)}, f32[2560]{0:T(1024)S(1)}) all-reduce(f32[2560]{0:T(1024)S(1)} %dynamic-update-slice, f32[2560]{0:T(1024)S(1)} %dynamic-update-slice.1), channel_id=4, replica_groups=mesh['seq'=16,'rep'=2] {'seq'}, use_global_device_ids=true, to_apply=%add.10 | all-reduce | flops 5120 | bytes 40960
  1515.8 0.8 fusion.24
  1516.6 37.2 %all-reduce.12 = (f32[160]{0:T(256)}, f32[160]{0:T(256)}, f32[256,4]{0,1:T(4,128)}, f32[256,4]{0,1:T(4,128)}, f32[4,32]{1,0:T(4,128)}, /*index=5*/f32[4,32]{1,0:T(4,128)}, f32[160]{0:T(256)}) all-reduce(f32[160]{0:T(256)S(1)} %get-tuple-element.540, f32[160]{0:T(256)S(1)} %get-tuple-element.539, ...), channel_id=1, replica_groups=mesh['seq'=16,'rep'=2] {'seq','rep'}, use_global_device_ids=true, to_apply=%region_10.11 | all-reduce | flops 2784 | bytes 22272 | tf_op jit(solution)/shard_map/psum | solution.py:220
  1553.8 79.6 %all-reduce.16.cloned.1.call-done = f32[160,160]{0,1:T(8,128)} async-done(((f32[160,160]{0,1:T(8,128)}), f32[160,160]{0,1:T(8,128)}) %all-reduce.16.cloned.1.call-update) | async-done | bytes 102416 | tf_op jit(solution)/shard_map/psum | solution.py:220
  1633.4 1.7 copy.191
  (1247 shorter events, 361.5 us)
Async XLA Ops:
  7.2 773.0 %copy-start = (f32[256,4]{0,1:T(4,128)S(1)}, f32[256,4]{0,1:T(4,128)}, u32[]{:S(2)}) copy-start(f32[256,4]{0,1:T(4,128)} %param.21) | copy-start | bytes 12292
  88.2 692.5 %copy-start.36 = (f32[90]{0:T(128)}, f32[90]{0:T(128)S(1)}, u32[]{:S(2)}) copy-start(f32[90]{0:T(128)S(1)} %add_convert_fusion) | copy-start | bytes 1084
  89.3 5.5 copy-start.19
  91.3 848.0 %all-to-all-start.2 = ((f32[1,160,90]{2,0,1:T(1,128)}), f32[1,160,90]{2,0,1:T(1,128)S(1)}, u32[]{:S(2)}, u32[]{:S(2)}) async-start(f32[1,160,90]{2,0,1:T(1,128)} %bitcast.45), calls=%async_computation.2 | async-start | bytes 163840 | tf_op jit(solution)/shard_map/all_to_all | solution.py:171
  94.9 686.6 %copy-start.44 = (f32[256]{0:T(256)}, f32[256]{0:T(256)S(1)}, u32[]{:S(2)}) copy-start(f32[256]{0:T(256)S(1)} %add_multiply_fusion) | copy-start | bytes 3076
  95.2 841.7 %copy-start.10 = (pred[810,90]{0,1:T(8,128)(4,1)}, pred[810,90]{0,1:T(8,128)(4,1)S(1)}, u32[]{:S(2)}) copy-start(pred[810,90]{0,1:T(8,128)(4,1)S(1)} %fusion.44) | copy-start | bytes 218704
  780.2 157.7 %copy-start.40 = (f32[256]{0:T(256)}, f32[256]{0:T(256)S(1)}, u32[]{:S(2)}) copy-start(f32[256]{0:T(256)S(1)} %slice_reduce_fusion) | copy-start | bytes 3076
  781.4 134.0 %copy-start.7 = (s32[72900]{0:T(1024)}, s32[72900]{0:T(1024)S(1)}, u32[]{:S(2)}) copy-start(s32[72900]{0:T(1024)S(1)} %reshape.353) | copy-start | bytes 874804
  935.2 6.0 copy-start.27
  935.2 6.0 copy-start.29
  937.2 6.3 copy-start.8
  938.0 5.1 copy-start.50
  939.3 3.9 copy-start.46
  939.3 4.1 copy-start.12
  941.2 4.2 copy-start.21
  945.7 19.7 %copy-start.13 = (f32[1,10,16,90]{3,2,1,0:T(8,128)S(1)}, f32[1,10,16,90]{3,2,1,0:T(8,128)}, u32[]{:S(2)}) copy-start(f32[1,10,16,90]{3,2,1,0:T(8,128)} %copy-done.12) | copy-start | bytes 172804
  955.4 19.2 %copy-start.4 = (f32[1,160,90]{2,1,0:T(8,128)S(1)}, f32[1,160,90]{2,1,0:T(8,128)}, u32[]{:S(2)}) copy-start(f32[1,160,90]{2,1,0:T(8,128)} %param.17) | copy-start | bytes 172804
  955.4 19.2 %copy-start.5 = (f32[160,90]{1,0:T(8,128)S(1)}, f32[160,90]{1,0:T(8,128)}, u32[]{:S(2)}) copy-start(f32[160,90]{1,0:T(8,128)} %get-tuple-element.510) | copy-start | bytes 172804
  955.4 19.2 %copy-start.37 = (f32[90]{0:T(128)S(1)}, f32[90]{0:T(128)}, u32[]{:S(2)}) copy-start(f32[90]{0:T(128)} %copy-done.36) | copy-start | bytes 1084
  957.8 17.6 %copy-start.25 = (f32[160]{0:T(256)S(1)}, f32[160]{0:T(256)}, u32[]{:S(2)}) copy-start(f32[160]{0:T(256)} %param.19) | copy-start | bytes 1924
  957.8 17.6 %copy-start.32 = (f32[160]{0:T(256)S(1)}, f32[160]{0:T(256)}, u32[]{:S(2)}) copy-start(f32[160]{0:T(256)} %param.20) | copy-start | bytes 1924
  957.8 14.5 all-to-all-start.3
  975.4 13.1 copy-start.14
  976.1 11.1 all-to-all-start
  991.4 4.2 copy-start.28
  991.4 4.2 copy-start.30
  991.4 4.2 copy-start.47
  1007.2 424.7 %all-to-all-start.1 = ((f32[16,1,900]{2,1,0:T(1,128)}), f32[16,1,900]{2,1,0:T(1,128)S(1)}, u32[]{:S(2)}, u32[]{:S(2)}) async-start(f32[16,1,900]{2,1,0:T(1,128)} %reshape.408), calls=%async_computation.1 | async-start | bytes 131072 | tf_op jit(solution)/shard_map/all_to_all | solution.py:153
  1010.9 622.5 %all-reduce.16.cloned.1.call-start = ((), (), s32[]{:S(2)}) async-start(), calls=%async_computation.4 | async-start | bytes 327680 | tf_op jit(solution)/shard_map/psum | solution.py:220
  1013.1 416.5 %copy-start.3 = (f32[256,720]{1,0:T(8,128)S(1)}, f32[256,720]{1,0:T(8,128)}, u32[]{:S(2)}) copy-start(f32[256,720]{1,0:T(8,128)} %copy-done.2) | copy-start | bytes 2211844
  1013.1 416.5 %copy-start.45 = (f32[256]{0:T(256)S(1)}, f32[256]{0:T(256)}, u32[]{:S(2)}) copy-start(f32[256]{0:T(256)} %copy-done.44) | copy-start | bytes 3076
  1013.2 417.3 %copy-start.24 = (f32[10,1440,1]{1,2,0:T(1,128)S(1)}, f32[10,1440,1]{1,2,0:T(1,128)}, u32[]{:S(2)}) copy-start(f32[10,1440,1]{1,2,0:T(1,128)} %reshape.398) | copy-start | bytes 172804
  1031.0 400.8 %copy-start.41 = (f32[256]{0:T(256)S(1)}, f32[256]{0:T(256)}, u32[]{:S(2)}) copy-start(f32[256]{0:T(256)} %copy-done.40) | copy-start | bytes 3076
  1430.5 3.8 copy-start.6
  1430.5 3.8 copy-start.26
  1430.5 3.8 copy-start.33
  1430.6 3.9 copy-start.18
  1430.6 3.9 copy-start.31
  1432.8 3.9 copy-start.15
  1432.8 3.9 copy-start.16
  1432.8 3.9 copy-start.23
  1432.8 3.9 copy-start.49
  1434.2 82.4 %copy-start.39 = (f32[160]{0:T(256)S(1)}, f32[160]{0:T(256)}, u32[]{:S(2)}) copy-start(f32[160]{0:T(256)} %get-tuple-element.503) | copy-start | bytes 1924
  1434.2 82.4 %copy-start.42 = (f32[160]{0:T(256)S(1)}, f32[160]{0:T(256)}, u32[]{:S(2)}) copy-start(f32[160]{0:T(256)} %reduce_sum.89) | copy-start | bytes 1924
  1434.2 82.4 %copy-start.34 = (f32[4,32]{1,0:T(4,128)S(1)}, f32[4,32]{1,0:T(4,128)}, u32[]{:S(2)}) copy-start(f32[4,32]{1,0:T(4,128)} %get-tuple-element.454) | copy-start | bytes 1540
  1434.2 82.4 %copy-start.35 = (f32[4,32]{1,0:T(4,128)S(1)}, f32[4,32]{1,0:T(4,128)}, u32[]{:S(2)}) copy-start(f32[4,32]{1,0:T(4,128)} %get-tuple-element.455) | copy-start | bytes 1540
  1434.2 82.4 %copy-start.43 = (f32[160]{0:T(256)S(1)}, f32[160]{0:T(256)}, u32[]{:S(2)}) copy-start(f32[160]{0:T(256)} %reduce_sum.92) | copy-start | bytes 1924
  1434.2 200.9 %copy-start.1 = (f32[256,4]{0,1:T(4,128)S(1)}, f32[256,4]{0,1:T(4,128)}, u32[]{:S(2)}) copy-start(f32[256,4]{0,1:T(4,128)} %param.21) | copy-start | bytes 12292
  (11 other events, 31.4 us)
Sparse Core Ops, SparseCore 0:
  1515.7 117.7 all-reduce.15
where the time goes:
time: 1670 us; the launch traced here: 1640 us
  other arithmetic  587 us (35%)
  local copies, waits for them, and re-layouts  371 us (22%)
  loops' own time  343 us (21%)
  blocking collectives  192 us (11%)
  waiting for transfers between devices  91.8 us (5%)
  matrix products  22.9 us (1%)
  starting transfers between devices  17.7 us (1%)
    scatter-add x1, other arithmetic, band_table(): picked = kernel[:, jnp.clip(lag, 0, WINDOW - 1)]  399 us
    another operation x1, loops' own time, legendre_rows(): lax.scan(advance, initial, jnp.arange(degrees).astype(jnp.float32))  343 us
    div x256, other arithmetic, advance(): ((2.0 * degree + 1.0) * points * this_poly - degree * lower_poly) / (degr...  168 us
    gather x3, local copies, waits for them, and re-layouts, band_table(): picked = kernel[:, jnp.clip(lag, 0, WINDOW - 1)]  155 us
    dynamic_slice x256, local copies, waits for them, and re-layouts, legendre_rows(): lax.scan(advance, initial, jnp.arange(degrees).astype(jnp.float32))  150 us
    psum x1, waiting for transfers between devices, body(): lax.psum((gain_grad, offset_grad, mode_in_grad, mode_out_grad, mode_re_gr...  79.6 us
    all_gather x2, blocking collectives, entering(): everything = jax.tree.map(lambda part: lax.all_gather(part, axis), shard)  77.9 us
    unnamed x1, blocking collectives  77 us
  transfers between devices with their start and end apart: 5, of which 3 were waited for; matrix products, arithmetic and copies ran while one was open for 56% of the time, Pallas kernels for 0%

commit v1 on v0

v1 whole, which is shorter than its diff:
```python
import functools
import math

import jax
import jax.numpy as jnp
import ml_dtypes
import numpy as np
from jax import lax
from jax.experimental import pallas as pl
from jax.experimental.pallas import tpu as pltpu
from jax.sharding import PartitionSpec as P

ORDER = 256
MODES = 32
RANK = 4
WINDOW = 720
EPSILON = 1e-05

LANES = 128
SLOT = 16
SEND = 24
f32 = jnp.float32
bf16 = jnp.bfloat16


def up(value, multiple):
    return -(-value // multiple) * multiple


def legendre_table():
    one, two = np.float32(1.0), np.float32(2.0)
    lags = np.arange(WINDOW).astype(np.float32)
    points = one - (two * (lags + np.float32(0.5))) * np.float32(1.0 / WINDOW)
    lower, this = np.zeros_like(points), np.ones_like(points)
    rows = []
    for degree in np.arange(ORDER).astype(np.float32):
        rows.append(this)
        upper = ((two * degree + one) * points * this - degree * lower) / (degree + one)
        lower, this = this, upper
    return np.stack(rows)


def in_blocks(values, steps):
    blocks = WINDOW // steps
    framed = np.zeros(values.shape[:-1] + (blocks, LANES))
    framed[..., :steps] = values.reshape(values.shape[:-1] + (blocks, steps))
    return framed.reshape(values.shape[:-1] + (blocks * LANES,))


def halves(values):
    high = values.astype(np.float32).astype(ml_dtypes.bfloat16)
    low = (values - high.astype(np.float64)).astype(ml_dtypes.bfloat16)
    return high, low


def constants(steps):
    legendre = legendre_table()
    degree = np.arange(ORDER).astype(np.float32)
    weights = legendre * ((np.float32(2.0) * degree + np.float32(1.0)) / np.float32(WINDOW))[:, None]
    flipped = in_blocks(weights[:, ::-1], steps)
    high, low = halves(flipped)
    table = {}
    table["weights"] = np.concatenate([high, low], 1)
    table["weights_t"] = np.concatenate([high.T, low.T], 1)
    table["endpoint"] = legendre[:, 0][None, :].astype(np.float32)
    mode = np.arange(MODES)[:, None]
    step = np.arange(WINDOW)[None, :]
    angle = 2.0 * math.pi / WINDOW * (mode * step % WINDOW)
    cosine, sine = np.cos(angle), np.sin(angle)
    back = 2.0 * math.pi / WINDOW * (mode * (WINDOW - 1 - step) % WINDOW)
    table["turn"] = np.concatenate(
        [in_blocks(v, steps) for v in (cosine, sine, np.cos(back), np.sin(back))]
    ).astype(np.float32)
    scale = np.where(np.arange(MODES) == 0, 1.0, 2.0) / WINDOW
    table["scale"] = np.concatenate([scale, scale])[None, :].astype(np.float32)
    table["scale_t"] = np.concatenate([scale, scale])[:, None].astype(np.float32)
    high, low = halves(in_blocks(np.concatenate([cosine, -sine]), steps))
    table["to_modes"] = np.concatenate([high.T, low.T], 1)
    wave = in_blocks(np.concatenate([scale[:, None] * cosine, -scale[:, None] * sine]), steps)
    high, low = halves(np.concatenate([wave, wave]))
    table["from_modes"] = np.concatenate([high, low, high])
    lane = np.arange(LANES)
    upper = (lane[:, None] <= lane[None, :]).astype(np.float32)
    ones = np.ones((LANES, LANES), np.float32)
    for name, part in (("earlier", upper), ("later", upper.T)):
        both = np.concatenate([part, ones], 1)
        table[name] = np.concatenate([both, both]).astype(ml_dtypes.bfloat16)
    return table


def split(value):
    high = value.astype(bf16)
    return high, (value - high.astype(f32)).astype(bf16)


def dot(a, b):
    return lax.dot_general(a, b, (((1,), (0,)), ((), ())), preferred_element_type=f32)


def dot_nt(a, b):
    return lax.dot_general(a, b, (((1,), (1,)), ((), ())), preferred_element_type=f32)


def stacked_dot(value, table):
    rows, width = value.shape[0], table.shape[1] // 2
    high, low = split(value)
    out = dot(jnp.concatenate([high, low], 0), table)
    return out[:rows, :width] + out[:rows, width:] + out[rows:, :width]


def thrice(value):
    high, low = split(value)
    return jnp.concatenate([high, high, low], 1)


def scan_lanes(value, table):
    high, low = split(value)
    out = dot(jnp.concatenate([high, low], 1), table)
    return out[:, :LANES], out[:, LANES:]


def row_of(i, kind):
    return 8 * kind + i if i < 8 else 16 + (i - 8) + 2 * kind


def to_wide(blocks, windows):
    per = len(blocks) // windows
    return jnp.concatenate(
        [jnp.concatenate(blocks[w * per : (w + 1) * per], 1) for w in range(windows)], 0
    )


def to_blocks(wide, windows):
    per = wide.shape[1] // LANES
    return [
        wide[w * SLOT : (w + 1) * SLOT, b * LANES : (b + 1) * LANES]
        for w in range(windows)
        for b in range(per)
    ]


def blocks_of(value):
    return [value[k * SLOT : (k + 1) * SLOT] for k in range(value.shape[0] // SLOT)]


def same_rows(groups_ref, start, rows):
    channels = groups_ref.shape[1]
    ids = groups_ref[...].astype(f32)
    row = lax.broadcasted_iota(jnp.int32, (rows, channels), 0) + start
    lane = lax.broadcasted_iota(jnp.int32, (rows, channels), 1)
    column = jnp.sum(jnp.where(row == lane, ids, 0.0), axis=1, keepdims=True)
    return column == ids


def own_lanes(place, channels, width, count, blocks):
    row = lax.broadcasted_iota(jnp.int32, (SLOT, width), 0)
    lane = lax.broadcasted_iota(jnp.int32, (SLOT, width), 1)
    return (lane == row * blocks + place) & (row < count)


def send_kernel(own, series_ref, cot_ref, mixing_ref, groups_ref, send_ref, pad_ref, grad_ref):
    channels, steps = mixing_ref.shape[0], series_ref.shape[2]
    blocks = channels // own
    chunk = channels if channels <= 512 else 256
    zero = jnp.zeros((blocks, LANES), f32)
    for r in range(16 + 4 * (own - 8) // 2, SEND):
        send_ref[pl.ds(r, blocks, stride=SEND), :] = zero
    pad_ref[...] = jnp.zeros_like(pad_ref)
    pad_ref[:, :steps] = series_ref[0]
    for i in range(own):
        send_ref[pl.ds(row_of(i, 0), blocks, stride=SEND), :] = pad_ref[
            blocks * i : blocks * (i + 1), :
        ]
    pad_ref[:, :steps] = cot_ref[0]
    total = None
    for start in range(0, channels, chunk):
        same = same_rows(groups_ref, start, chunk)
        masked = jnp.where(same, mixing_ref[start : start + chunk, :], 0.0)
        high, low = split(masked.T)
        both = jnp.concatenate(split(pad_ref[start : start + chunk, :]), 1)
        out = dot(jnp.concatenate([high, low], 0), both)
        part = out[:channels, :LANES] + out[:channels, LANES:] + out[channels:, :LANES]
        total = part if total is None else total + part
    grad_ref[...] = total
    for i in range(own):
        send_ref[pl.ds(row_of(i, 1), blocks, stride=SEND), :] = grad_ref[
            blocks * i : blocks * (i + 1), :
        ]


def table_kernel(
    own,
    place_ref,
    series_ref,
    cot_ref,
    mixing_ref,
    groups_ref,
    gain_ref,
    bias_ref,
    out_bias_ref,
    mode_in_ref,
    mode_out_ref,
    mode_re_ref,
    mode_im_ref,
    weights_ref,
    endpoint_ref,
    turn_ref,
    scale_ref,
    scale_t_ref,
    later_ref,
    ahead_ref,
    back_ref,
    kernel_ref,
    small_ref,
    own_ref,
    base_ref,
    masked_ref,
    same_ref,
    cot3_ref,
    cot_sum_ref,
    pad_ref,
    turned_ref,
):
    channels, steps = mixing_ref.shape[0], series_ref.shape[2]
    width = ahead_ref.shape[0]
    per = width // LANES
    blocks = channels // own
    turned_ref[...] = jnp.zeros_like(turned_ref)
    turned_ref[:, 0:RANK] = mode_in_ref[...]
    turned_ref[:, RANK : 2 * RANK] = mode_out_ref[...]
    factors = turned_ref[...].T
    high, low = split(factors[0:8])
    out = dot(jnp.concatenate([high, low], 0), weights_ref[...])
    kernel = out[0:8, :width] + out[0:8, width:] + out[8:16, :width]
    kernel_ref[...] = kernel
    mix = jnp.sum(factors[0:8] * endpoint_ref[...], axis=1, keepdims=True)[RANK : 2 * RANK]
    scale = scale_ref[...]
    gain_re, gain_im = mode_re_ref[...], mode_im_ref[...]
    mixed = jnp.concatenate([gain_re, gain_im], 1) * mix
    signed = jnp.concatenate([gain_re, -gain_im], 1) * scale
    sign = jnp.where(lax.broadcasted_iota(jnp.int32, (RANK, 2 * MODES), 1) < MODES, 1.0, -1.0)
    small_ref[...] = jnp.zeros_like(small_ref)
    small_ref[0:RANK, 0 : 2 * MODES] = signed * mix
    small_ref[8 : 8 + RANK, 0 : 2 * MODES] = sign * scale * mix
    small_ref[16 : 16 + RANK, 0 : 2 * MODES] = signed
    turned_ref[...] = jnp.zeros_like(turned_ref)
    turned_ref[0:RANK, 0 : 2 * MODES] = mixed
    columns = turned_ref[0:LANES, :].T[0 : 2 * MODES]
    response = None
    for r in range(RANK):
        term = columns[:, r : r + 1] * kernel[r : r + 1, :]
        response = term if response is None else response + term
    real, imag = response[:MODES], response[MODES:]
    cosine, sine = turn_ref[0:MODES], turn_ref[MODES : 2 * MODES]
    cos_b, sin_b = turn_ref[2 * MODES : 3 * MODES], turn_ref[3 * MODES : 4 * MODES]
    turned = jnp.concatenate([real * cos_b + imag * sin_b, imag * cos_b - real * sin_b], 0)
    rows = jnp.concatenate([turned[:, b * LANES : (b + 1) * LANES] for b in range(per)], 0)
    local, total = scan_lanes(rows, later_ref[...])
    count = 2 * MODES
    run = jnp.zeros((count, LANES), f32)
    suffix = [None] * per
    for b in reversed(range(per)):
        suffix[b] = local[b * count : (b + 1) * count] + run
        run = run + total[b * count : (b + 1) * count]
    scale_t = scale_t_ref[...]
    for b in range(per):
        at = slice(b * LANES, (b + 1) * LANES)
        c, s = cosine[:, at], sine[:, at]
        parts = []
        for value in (suffix[b], run - suffix[b]):
            re, im = value[:MODES], value[MODES:]
            parts += [re * c + im * s, im * c - re * s]
        both = jnp.concatenate(parts, 0)
        high, low = split(both.T)
        ahead_ref[at, 0:LANES] = high
        ahead_ref[at, LANES : 2 * LANES] = low
        high, low = split(both * jnp.concatenate([scale_t, scale_t], 0))
        back_ref[0:LANES, at] = high
        back_ref[LANES : 2 * LANES, at] = low
        back_ref[2 * LANES : 3 * LANES, at] = high
    mine = own_lanes(place_ref[0], channels, channels, own, blocks)
    real_row = lax.broadcasted_iota(jnp.int32, (SLOT, 1), 0) < own
    gain = jnp.sum(jnp.where(mine, gain_ref[...], 0.0), axis=1, keepdims=True)
    gain = jnp.where(real_row, gain, 1.0)
    bias = jnp.sum(jnp.where(mine, bias_ref[...], 0.0), axis=1, keepdims=True)
    own_ref[0:SLOT, :] = jnp.broadcast_to(gain, (SLOT, LANES))
    own_ref[SLOT : 2 * SLOT, :] = jnp.broadcast_to(bias, (SLOT, LANES))
    own_ref[2 * SLOT : 3 * SLOT, :] = jnp.broadcast_to(1.0 / gain, (SLOT, LANES))
    chunk = channels if channels <= 512 else 256
    for start in range(0, channels, chunk):
        at = slice(start, start + chunk)
        same = same_rows(groups_ref, start, chunk)
        high, low = split(jnp.where(same, mixing_ref[at, :], 0.0))
        masked_ref[0, at, :] = high
        masked_ref[1, at, :] = low
        same_ref[at, 0:channels] = jnp.where(same, 1.0, 0.0)
        row = lax.broadcasted_iota(jnp.int32, (chunk, channels), 0) + start
        lane = lax.broadcasted_iota(jnp.int32, (chunk, channels), 1)
        shift = jnp.sum(jnp.where(row == lane, out_bias_ref[...], 0.0), axis=1, keepdims=True)
        base_ref[at, :] = series_ref[0, at, :] + shift
    pad_ref[...] = jnp.zeros_like(pad_ref)
    pad_ref[0:channels, :steps] = cot_ref[0]
    three = thrice(pad_ref[...])
    cot3_ref[...] = three
    cot_sum_ref[...] = dot_nt(jnp.ones((8, 2 * LANES), bf16), three[:, LANES : 3 * LANES])


def normalized(x, blocks, steps, earlier):
    rows = x.shape[0]
    local, total = scan_lanes(jnp.concatenate([x, x * x], 0), earlier)
    first, second = blocks_of(local[:rows]), blocks_of(local[rows:])
    first_all, second_all = blocks_of(total[:rows]), blocks_of(total[rows:])
    run_one = jnp.zeros((SLOT, LANES), f32)
    run_two = jnp.zeros((SLOT, LANES), f32)
    lane = lax.broadcasted_iota(jnp.int32, (SLOT, LANES), 1)
    means, variances, inverses = [], [], []
    for k in range(blocks):
        inverse = 1.0 / (lane + (k * steps + 1 + WINDOW)).astype(f32)
        mean = (first[k] + run_one) * inverse
        means.append(mean)
        variances.append((second[k] + run_two + WINDOW) * inverse - mean * mean + EPSILON)
        inverses.append(inverse)
        run_one = run_one + first_all[k]
        run_two = run_two + second_all[k]
    return means, variances, inverses


def forward_kernel(
    blocks,
    steps,
    recv_ref,
    own_ref,
    ahead_ref,
    from_modes_ref,
    earlier_ref,
    send_ref,
    mean_ref,
    inverse_ref,
    shifted_ref,
):
    windows = blocks * steps // WINDOW
    got = recv_ref[...].reshape(blocks, SEND, LANES)
    x = jnp.concatenate([got[:, 0:8], got[:, 16:24]], 1).reshape(blocks * SLOT, LANES)
    means, variances, unused = normalized(x, blocks, steps, earlier_ref[...])
    gain, bias, over = own_ref[0:SLOT], own_ref[SLOT : 2 * SLOT], own_ref[2 * SLOT : 3 * SLOT]
    normal, spreads = [], []
    for k, series in enumerate(blocks_of(x)):
        at = slice(k * SLOT, (k + 1) * SLOT)
        inverse = lax.rsqrt(variances[k])
        normal.append(gain * ((series - means[k]) * inverse) + bias)
        spreads.append(variances[k] * inverse)
        mean_ref[at, :] = means[k]
        inverse_ref[at, :] = inverse
    spectra = stacked_dot(to_wide(normal, windows), ahead_ref[...])
    zero = jnp.zeros((SLOT, LANES), f32)
    before = jnp.concatenate([zero, spectra[:-SLOT]], 0) if windows > 1 else zero
    lane = lax.broadcasted_iota(jnp.int32, spectra.shape, 1)
    spectra = jnp.where(lane < 2 * MODES, spectra, before)
    recon = dot(thrice(spectra), from_modes_ref[...])
    for k, value in enumerate(to_blocks(recon, windows)):
        at = slice(k * SLOT, (k + 1) * SLOT)
        shifted = (value - bias) * over
        shifted_ref[at, :] = shifted
        send_ref[at, :] = shifted * spreads[k] + means[k]


def backward_kernel(
    own,
    blocks,
    steps,
    place_ref,
    recv_ref,
    own_ref,
    mean_ref,
    inverse_ref,
    shifted_ref,
    back_ref,
    kernel_ref,
    small_ref,
    turn_ref,
    to_modes_ref,
    weights_t_ref,
    earlier_ref,
    later_ref,
    cot_sum_ref,
    part_ref,
    misc_ref,
):
    windows = blocks * steps // WINDOW
    wide = cot_sum_ref.shape[1]
    got = recv_ref[...].reshape(blocks, SEND, LANES)
    x = blocks_of(
        jnp.concatenate([got[:, 0:8], got[:, 16:24]], 1).reshape(blocks * SLOT, LANES)
    )
    tail = pltpu.roll(got[:, 16:24], 6, 1)
    grad = blocks_of(jnp.concatenate([got[:, 8:16], tail], 1).reshape(blocks * SLOT, LANES))
    mean, inverse = blocks_of(mean_ref[...]), blocks_of(inverse_ref[...])
    shifted = blocks_of(shifted_ref[...])
    gain, bias, over = own_ref[0:SLOT], own_ref[SLOT : 2 * SLOT], own_ref[2 * SLOT : 3 * SLOT]
    row = lax.broadcasted_iota(jnp.int32, (SLOT, LANES), 0)
    lane = lax.broadcasted_iota(jnp.int32, (SLOT, LANES), 1)
    held = (row < own) & (lane < steps)
    centered, normal, recon_grad = [], [], []
    for k in range(blocks):
        centered.append((x[k] - mean[k]) * inverse[k])
        normal.append(gain * centered[k] + bias)
        recon_grad.append(jnp.where(held, grad[k] / inverse[k] * over, 0.0))
    waves = stacked_dot(to_wide(recon_grad, windows), to_modes_ref[...])
    zero = jnp.zeros((SLOT, 2 * MODES), f32)
    after = jnp.concatenate([waves[SLOT:], zero], 0) if windows > 1 else zero
    waves = jnp.concatenate([waves, after], 1)
    normal_grad = to_blocks(dot(thrice(waves), back_ref[...]), windows)
    gain_sum = jnp.zeros((SLOT, LANES), f32)
    bias_sum = jnp.zeros((SLOT, LANES), f32)
    scaled, ones, twos = [], [], []
    for k in range(blocks):
        over_q = 1.0 / (lane + (k * steps + 1 + WINDOW)).astype(f32)
        scaled.append(normal_grad[k] * gain * inverse[k])
        gain_sum = gain_sum + jnp.where(
            held, normal_grad[k] * centered[k] - recon_grad[k] * shifted[k], 0.0
        )
        bias_sum = bias_sum + jnp.where(held, normal_grad[k] - recon_grad[k], 0.0)
        spread_grad = grad[k] * shifted[k] - scaled[k] * centered[k]
        mean_grad = grad[k] - scaled[k]
        variance_grad = spread_grad * (0.5 * inverse[k])
        first = (mean_grad - 2.0 * mean[k] * variance_grad) * over_q
        ones.append(jnp.where(held, first, 0.0))
        twos.append(jnp.where(held, variance_grad * over_q, 0.0))
    rows = blocks * SLOT
    local, total = scan_lanes(jnp.concatenate(ones + twos, 0), later_ref[...])
    run_one = jnp.zeros((SLOT, LANES), f32)
    run_two = jnp.zeros((SLOT, LANES), f32)
    for k in reversed(range(blocks)):
        at = slice(k * SLOT, (k + 1) * SLOT)
        there = slice(rows + k * SLOT, rows + (k + 1) * SLOT)
        part_ref[at, :] = (
            scaled[k] + local[at] + run_one + 2.0 * x[k] * (local[there] + run_two)
        )
        run_one = run_one + total[at]
        run_two = run_two + total[there]
    signal = to_wide([jnp.where(held, v, 0.0) for v in normal], windows)
    high, low = split(signal)
    pairs = dot(thrice(waves.T), jnp.concatenate([high, low, high], 0))
    cosine, sine = turn_ref[0:MODES], turn_ref[MODES : 2 * MODES]
    cos_b, sin_b = turn_ref[2 * MODES : 3 * MODES], turn_ref[3 * MODES : 4 * MODES]
    count = 2 * MODES

    def turned(value):
        re, im = value[:MODES], value[MODES:]
        return jnp.concatenate([re * cosine - im * sine, -(re * sine + im * cosine)], 0)

    per = pairs.shape[1] // LANES
    after = turned(pairs[count:])
    left = turned(pairs[:count]) - after
    after_all = jnp.sum(sum(after[:, b * LANES : (b + 1) * LANES] for b in range(per)), 1, keepdims=True)
    rows = jnp.concatenate([left[:, b * LANES : (b + 1) * LANES] for b in range(per)], 0)
    local, total = scan_lanes(rows, earlier_ref[...])
    run = jnp.broadcast_to(after_all, (count, LANES))
    sums = []
    for b in range(per):
        sums.append(local[b * count : (b + 1) * count] + run)
        run = run + total[b * count : (b + 1) * count]
    sums = jnp.concatenate(sums, 1)
    re, im = sums[:MODES], sums[MODES:]
    crossed = jnp.concatenate([re * cos_b + im * sin_b, im * cos_b - re * sin_b], 0)
    high, low = split(crossed)
    kernel_grad = dot(
        thrice_narrow(small_ref[0:8, 0:count]), jnp.concatenate([high, low, high], 0)
    )
    mode_in_grad = stacked_dot(kernel_grad, weights_t_ref[...])
    k_high, k_low = split(kernel_ref[...])
    overlap = dot_nt(
        jnp.concatenate([k_high, k_high, k_low], 1), jnp.concatenate([high, low, high], 1)
    )
    modes = overlap * small_ref[8:16, 0:count]
    mix_grad = jnp.sum(overlap * small_ref[16:24, 0:count], axis=1, keepdims=True)
    misc_ref[...] = jnp.zeros_like(misc_ref)
    misc_ref[0:RANK, :] = mode_in_grad[0:RANK, :LANES]
    misc_ref[RANK : 2 * RANK, :] = mode_in_grad[0:RANK, LANES:]
    misc_ref[8 : 8 + RANK, 0:count] = modes[0:RANK]
    misc_ref[8 : 8 + RANK, count : 2 * count] = jnp.broadcast_to(mix_grad, (8, count))[0:RANK]
    mine = own_lanes(place_ref[0], 0, wide, own, blocks)
    at = 12
    gain_row = jnp.sum(
        jnp.where(mine, jnp.sum(gain_sum, 1, keepdims=True), 0.0), axis=0, keepdims=True
    )
    bias_row = jnp.sum(
        jnp.where(mine, jnp.sum(bias_sum, 1, keepdims=True), 0.0), axis=0, keepdims=True
    )
    for value in (gain_row, bias_row, cot_sum_ref[0:1, :]):
        for j in range(wide // LANES):
            misc_ref[at : at + 1, :] = value[:, j * LANES : (j + 1) * LANES]
            at += 1


def thrice_narrow(value):
    high, low = split(value)
    return jnp.concatenate([high, high, low], 1)


def pieces(channels, devices):
    tiles, rest = channels // LANES, channels % LANES
    each = channels // devices
    rest_rows = channels * rest // LANES
    misc_rows = 12 + 3 * (up(channels, LANES) // LANES)
    extra = up(rest_rows + misc_rows, devices) // devices
    return tiles, rest, each, rest_rows, misc_rows, extra


def mix_kernel(
    own,
    devices,
    recv_ref,
    base_ref,
    masked_ref,
    same_ref,
    cot3_ref,
    misc_ref,
    part_ref,
    out_ref,
    send_ref,
    rest_ref,
    misc_all_ref,
):
    channels, steps = base_ref.shape
    blocks = channels // own
    tiles, rest, each, rest_rows, misc_rows, extra = pieces(channels, devices)
    share = up(tiles * each + extra, 8)
    slot = send_ref.shape[0] // devices
    if rest_ref.shape[0] > channels:
        rest_ref[channels:, :] = jnp.zeros((rest_ref.shape[0] - channels, LANES), f32)
    for i in range(own):
        rest_ref[blocks * i : blocks * (i + 1), :] = recv_ref[pl.ds(i, blocks, stride=SLOT), :]
    high, low = split(rest_ref[...])
    both = jnp.concatenate([high[:channels], low[:channels]], 1)
    three = jnp.concatenate([high, low, high], 1)
    chunk = channels if channels <= 512 else devices
    for start in range(0, channels, chunk):
        at = slice(start, start + chunk)
        out = dot(jnp.concatenate([masked_ref[0, at, :], masked_ref[1, at, :]], 0), both)
        mixed = out[:chunk, :LANES] + out[:chunk, LANES:] + out[chunk:, :LANES]
        out_ref[0, at, :] = base_ref[at, :] + mixed[:, :steps]
        grad = dot_nt(cot3_ref[at, :], three)
        for j in range(tiles):
            lanes = slice(j * LANES, (j + 1) * LANES)
            tile = grad[:, lanes] * same_ref[at, lanes]
            for i in range(chunk // devices):
                send_ref[pl.ds(j * each + start // devices + i, devices, stride=slot), :] = tile[
                    devices * i : devices * (i + 1)
                ]
        if rest:
            lanes = slice(tiles * LANES, tiles * LANES + LANES)
            last = grad[:, lanes]
            last = last * same_ref[at, lanes]
            folded = last[0:rest_rows]
            for g in range(1, LANES // rest):
                folded = folded + pltpu.roll(
                    last[g * rest_rows : (g + 1) * rest_rows], g * rest, 1
                )
            misc_all_ref[0:rest_rows, :] = folded
    misc_all_ref[rest_rows : rest_rows + misc_rows, :] = misc_ref[0:misc_rows, :]
    if misc_all_ref.shape[0] > rest_rows + misc_rows:
        misc_all_ref[rest_rows + misc_rows :, :] = jnp.zeros(
            (misc_all_ref.shape[0] - rest_rows - misc_rows, LANES), f32
        )
    for k in range(extra):
        send_ref[pl.ds(tiles * each + k, devices, stride=slot), :] = misc_all_ref[
            devices * k : devices * (k + 1), :
        ]
    half = own // 2
    for i in range(own):
        to_core, k = i // half, i % half
        send_ref[pl.ds(to_core * slot + share + k, blocks, stride=2 * slot), :] = part_ref[
            pl.ds(i, blocks, stride=SLOT), :
        ]


def sum_kernel(own, devices, share, core_ref, recv_ref, send_ref, mine_ref, theirs_ref):
    slot = recv_ref.shape[0] // devices
    total = recv_ref[0:share, :]
    for s in range(1, devices):
        total = total + recv_ref[s * slot : s * slot + share, :]
    for s in range(devices):
        send_ref[s * share : (s + 1) * share, :] = total
    blocks = devices // 2
    first = core_ref[0] == 0
    for k in range(own // 2):
        even = recv_ref[pl.ds(share + k, blocks, stride=2 * slot), :]
        odd = recv_ref[pl.ds(slot + share + k, blocks, stride=2 * slot), :]
        at = slice(k * blocks, (k + 1) * blocks)
        mine_ref[at, :] = jnp.where(first, even, odd)
        theirs_ref[at, :] = jnp.where(first, odd, even)


def series_kernel(own, core_ref, cot_ref, mine_ref, theirs_ref, out_ref):
    steps = cot_ref.shape[2]
    first = core_ref[0] == 0
    half = mine_ref.shape[0]
    low = jnp.where(first, mine_ref[...], theirs_ref[...])
    high = jnp.where(first, theirs_ref[...], mine_ref[...])
    out_ref[0, 0:half, :] = cot_ref[0, 0:half, :] + low[:, :steps]
    out_ref[0, half : 2 * half, :] = cot_ref[0, half : 2 * half, :] + high[:, :steps]


def spread_kernel(
    devices,
    recv_ref,
    endpoint_ref,
    gain_ref,
    bias_ref,
    mode_in_ref,
    mode_out_ref,
    mode_re_ref,
    mode_im_ref,
    mixing_ref,
    out_bias_ref,
    misc_ref,
    turned_ref,
):
    channels = mixing_ref.shape[0]
    tiles, rest, each, rest_rows, misc_rows, extra = pieces(channels, devices)
    share = recv_ref.shape[0] // devices
    for j in range(tiles):
        for i in range(each):
            mixing_ref[devices * i : devices * (i + 1), j * LANES : (j + 1) * LANES] = recv_ref[
                pl.ds(j * each + i, devices, stride=share), :
            ]
    for k in range(extra):
        misc_ref[devices * k : devices * (k + 1), :] = recv_ref[
            pl.ds(tiles * each + k, devices, stride=share), :
        ]
    if rest:
        folded = misc_ref[0:rest_rows, :]
        for g in range(LANES // rest):
            piece = folded if g == 0 else pltpu.roll(folded, LANES - g * rest, 1)
            mixing_ref[g * rest_rows : (g + 1) * rest_rows, tiles * LANES :] = piece[:, :rest]
    at = rest_rows
    modes = misc_ref[at + 8 : at + 8 + RANK, :]
    mode_re_ref[...] = modes[:, 0:MODES]
    mode_im_ref[...] = modes[:, MODES : 2 * MODES]
    mix_grad = modes[:, 2 * MODES : 2 * MODES + 1]
    turned_ref[...] = jnp.zeros_like(turned_ref)
    turned_ref[0:RANK, 0:LANES] = misc_ref[at : at + RANK, :]
    turned_ref[0:RANK, LANES : 2 * LANES] = misc_ref[at + RANK : at + 2 * RANK, :]
    turned_ref[RANK : 2 * RANK, :] = mix_grad * endpoint_ref[...]
    columns = turned_ref[...].T
    mode_in_ref[...] = columns[:, 0:RANK]
    mode_out_ref[...] = columns[:, RANK : 2 * RANK]
    at += 12
    for ref in (gain_ref, bias_ref, out_bias_ref):
        for start in range(0, channels, LANES):
            size = min(LANES, channels - start)
            ref[:, start : start + size] = misc_ref[at : at + 1, 0:size]
            at += 1


def call(kernel, outs, scratch=(), scalars=0, count=0, cost=None, limit=None):
    vmem = pl.BlockSpec(memory_space=pltpu.VMEM)
    smem = pl.BlockSpec(memory_space=pltpu.SMEM)
    return pl.pallas_call(
        kernel,
        out_shape=tuple(jax.ShapeDtypeStruct(shape, kind) for shape, kind in outs),
        in_specs=[smem] * scalars + [vmem] * count,
        out_specs=tuple(vmem for unused in outs),
        scratch_shapes=[pltpu.VMEM(shape, kind) for shape, kind in scratch],
        compiler_params=pltpu.CompilerParams(vmem_limit_bytes=limit),
        cost_estimate=cost,
    )


def exchange(value, axis, count):
    rows = value.shape[0] // count
    out = lax.all_to_all(
        value.reshape(count, rows, value.shape[1]), axis, split_axis=0, concat_axis=0
    )
    return out.reshape(value.shape)


def body(
    series,
    group_ids,
    rev_gain,
    rev_bias,
    mode_in,
    mode_out,
    mode_re,
    mode_im,
    mixing,
    out_bias,
    cotangent,
):
    samples, channels, steps = series.shape
    blocks = lax.axis_size("seq")
    devices = blocks * lax.axis_size("rep")
    own = channels // blocks
    per = WINDOW // steps
    width = per * LANES
    padded = up(channels, LANES)
    place = lax.axis_index("seq").astype(jnp.int32).reshape(1)
    core = lax.axis_index("rep").astype(jnp.int32).reshape(1)
    const = {name: jnp.asarray(value) for name, value in constants(steps).items()}
    groups = group_ids.reshape(1, channels)
    limit = (16 if channels <= 512 else 56) * 2**20
    run = functools.partial(call, limit=limit)
    busy = pl.CostEstimate(flops=4_000_000_000, bytes_accessed=8_000_000, transcendentals=0)
    brief = pl.CostEstimate(flops=100_000_000, bytes_accessed=1_000_000, transcendentals=0)

    (send,) = run(
        functools.partial(send_kernel, own),
        [((blocks * SEND, LANES), f32)],
        [((channels, LANES), f32)] * 2,
        count=4,
        cost=brief,
    )(series, cotangent, mixing, groups)
    tables = run(
        functools.partial(table_kernel, own),
        [
            ((width, 2 * LANES), bf16),
            ((3 * LANES, width), bf16),
            ((8, width), f32),
            ((24, LANES), f32),
            ((3 * SLOT, LANES), f32),
            ((channels, steps), f32),
            ((2, channels, channels), bf16),
            ((channels, padded), f32),
            ((padded, 3 * LANES), bf16),
            ((8, padded), f32),
        ],
        [((padded, LANES), f32), ((ORDER, LANES), f32)],
        scalars=1,
        count=17,
        cost=busy,
    )(
        place,
        series,
        cotangent,
        mixing,
        groups,
        rev_gain.reshape(1, channels),
        rev_bias.reshape(1, channels),
        out_bias.reshape(1, channels),
        mode_in,
        mode_out,
        mode_re,
        mode_im,
        const["weights"],
        const["endpoint"],
        const["turn"],
        const["scale"],
        const["scale_t"],
        const["later"],
    )
    ahead, back, kernel, small, mine, base, masked, same, cot3, cot_sum = tables
    owned = exchange(send, "seq", blocks)
    rows = blocks * SLOT
    restored, mean, inverse, shifted = run(
        functools.partial(forward_kernel, blocks, steps),
        [((rows, LANES), f32)] * 4,
        count=5,
        cost=brief,
    )(owned, mine, ahead, const["from_modes"], const["earlier"])
    there = exchange(restored, "seq", blocks)
    tiles, rest, each, rest_rows, misc_rows, extra = pieces(channels, devices)
    share = up(tiles * each + extra, 8)
    slot = share + up(own // 2, 8)
    part, misc = run(
        functools.partial(backward_kernel, own, blocks, steps),
        [((rows, LANES), f32), ((up(misc_rows, 8), LANES), f32)],
        scalars=1,
        count=14,
        cost=busy,
    )(
        place,
        owned,
        mine,
        mean,
        inverse,
        shifted,
        back,
        kernel,
        small,
        const["turn"],
        const["to_modes"],
        const["weights_t"],
        const["earlier"],
        const["later"],
        cot_sum,
    )
    layer_out, send = run(
        functools.partial(mix_kernel, own, devices),
        [((1, channels, steps), f32), ((devices * slot, LANES), f32)],
        [((padded, LANES), f32), ((up(extra * devices, 8), LANES), f32)],
        count=7,
        cost=brief,
    )(there, base, masked, same, cot3, misc, part)
    shares = exchange(send, ("seq", "rep"), devices)
    half = own // 2 * blocks
    send, kept, given = run(
        functools.partial(sum_kernel, own, devices, share),
        [((devices * share, LANES), f32), ((half, LANES), f32), ((half, LANES), f32)],
        scalars=1,
        count=1,
        cost=brief,
    )(core, shares)
    sums = exchange(send, ("seq", "rep"), devices)
    given = lax.ppermute(given, "rep", [(0, 1), (1, 0)])
    (series_grad,) = run(
        functools.partial(series_kernel, own),
        [((1, channels, steps), f32)],
        scalars=1,
        count=3,
        cost=brief,
    )(core, cotangent, kept, given)
    outs = run(
        functools.partial(spread_kernel, devices),
        [
            ((1, channels), f32),
            ((1, channels), f32),
            ((ORDER, RANK), f32),
            ((ORDER, RANK), f32),
            ((RANK, MODES), f32),
            ((RANK, MODES), f32),
            ((channels, channels), f32),
            ((1, channels), f32),
        ],
        [((up(extra * devices, 8), LANES), f32), ((LANES, ORDER), f32)],
        count=2,
        cost=brief,
    )(sums, const["endpoint"])
    return (
        layer_out,
        series_grad,
        outs[0].reshape(channels),
        outs[1].reshape(channels),
        outs[2],
        outs[3],
        outs[4],
        outs[5],
        outs[6],
        outs[7].reshape(channels),
    )


def solution(mesh):
    time_split = P("rep", None, "seq")
    in_specs = (time_split,) + (P(),) * 9 + (time_split,)
    out_specs = (time_split, time_split) + (P(),) * 8
    return jax.shard_map(body, mesh=mesh, in_specs=in_specs, out_specs=out_specs, check_vma=False)
```

time: 1670 us -> 66.2 us (0.04); the launches traced: 1640 us -> 65.4 us
  other arithmetic: 587 us -> 0 us
  local copies, waits for them, and re-layouts: 371 us -> 13.9 us
  loops' own time: 343 us -> 0 us
  blocking collectives: 192 us -> 0 us
  waiting for transfers between devices: 91.8 us -> 22.3 us
  matrix products: 22.9 us -> 0 us
    scatter-add x1 -> x0, other arithmetic: 399 us -> none  [band_table(): picked = kernel[:, jnp.clip(lag, 0, WINDOW - 1)]]
    another operation x3 -> x0, loops' own time: 343 us -> none  [the longest x1 343 us: legendre_rows(): lax.scan(advance, initial, jnp.arange(degrees).astype(jnp.float32))]
    div x258 -> x0, other arithmetic: 168 us -> none  [the longest x256 168 us: advance(): ((2.0 * degree + 1.0) * points * this_poly - degree * lower_poly) / (degr...]
    gather x3 -> x0, local copies, waits for them, and re-layouts: 155 us -> none  [band_table(): picked = kernel[:, jnp.clip(lag, 0, WINDOW - 1)]]
    dynamic_slice x256 -> x0, local copies, waits for them, and re-layouts: 150 us -> none  [legendre_rows(): lax.scan(advance, initial, jnp.arange(degrees).astype(jnp.float32))]
    psum x1 -> x0, waiting for transfers between devices: 79.6 us -> none  [body(): lax.psum((gain_grad, offset_grad, mode_in_grad, mode_out_grad, mode_re_gr...]
    all_gather x2 -> x0, blocking collectives: 77.9 us -> none  [entering(): everything = jax.tree.map(lambda part: lax.all_gather(part, axis), shard)]
    unnamed x1 -> x0, blocking collectives: 77 us -> none
  transfers between devices with their start and end apart: 5 -> 5, of which waited for: 3 -> 5; matrix products, arithmetic and copies ran while one was open for 56% -> 0% of each run, Pallas kernels for 0% -> 5%
where the time goes in v1:
time: 66.2 us; the launch traced here: 65.4 us
  waiting for transfers between devices  22.3 us (34%)
  starting transfers between devices  19.8 us (30%)
  local copies, waits for them, and re-layouts  13.9 us (21%)
  Pallas kernels  8.38 us (13%)
  between operations  0.9 us (1%)
    all_to_all x4, waiting for transfers between devices, exchange(): lax.all_to_all(value.reshape(count, rows, value.shape[1]), axis, split_ax...  21.2 us
    all_to_all x4, starting transfers between devices, exchange(): lax.all_to_all(value.reshape(count, rows, value.shape[1]), axis, split_ax...  19.7 us
    unnamed x66, local copies, waits for them, and re-layouts  13.9 us
    pallas_call x1, Pallas kernels, body(): run(functools.partial(backward_kernel, own, blocks, steps), [((rows, LANE...  1.65 us
    pallas_call x1, Pallas kernels, body(): run(functools.partial(forward_kernel, blocks, steps), [((rows, LANES), f3...  1.36 us
  transfers between devices with their start and end apart: 5, of which 5 were waited for; matrix products, arithmetic and copies ran while one was open for 0% of the time, Pallas kernels for 5%

profile of v1, /device:TPU:0, one launch (start us, length us, event | category | flops | bytes accessed | tf_op | source)
XLA Modules:
  0.0 65.4 jit_solution(17111466034642607719)
XLA Ops:
  0.7 0.7 %copy-done.8 = s32[160]{0:T(256)S(1)} copy-done((s32[160]{0:T(256)S(1)}, s32[160]{0:T(256)}, u32[]{:S(2)}) %copy-start.8) | copy-done | bytes 664
  1.3 0.9 %copy-done.1 = f32[160,160]{1,0:T(8,128)S(1)} copy-done((f32[160,160]{1,0:T(8,128)S(1)}, f32[160,160]{1,0:T(8,128)}, u32[]{:S(2)}) %copy-start.1) | copy-done | bytes 102424
  2.2 0.9 %copy-done.4 = f32[1,160,90]{2,1,0:T(8,128)S(1)} copy-done((f32[1,160,90]{2,1,0:T(8,128)S(1)}, f32[1,160,90]{2,1,0:T(8,128)}, u32[]{:S(2)}) %copy-start.4) | copy-done | bytes 57624
  3.1 0.9 %copy-done.6 = f32[1,160,90]{2,1,0:T(8,128)S(1)} copy-done((f32[1,160,90]{2,1,0:T(8,128)S(1)}, f32[1,160,90]{2,1,0:T(8,128)}, u32[]{:S(2)}) %copy-start.6) | copy-done | bytes 57624
  4.0 1.0 %shard_map.276 = f32[384,128]{1,0:T(8,128)} custom-call(f32[1,160,90]{2,1,0:T(8,128)S(1)} %copy-done.4, f32[1,160,90]{2,1,0:T(8,128)S(1)} %copy-done.6, f32[160,160]{1,0:T(8,128)S(1)} %copy-done.1, s32[1,160]{1,0:T(1,128)S(1)} %bitcast.22), custom_call_target="tpu_custom_call" | custom-call | flops 100000000 | bytes 1000000 | tf_op jit(solution)/shard_map/pallas_call | solution.py:708
  5.0 0.0 copy-start.22
  5.1 8.5 %all-to-all-start = ((f32[16,24,128]{2,1,0:T(8,128)}), f32[16,24,128]{2,1,0:T(8,128)S(1)}, u32[]{:S(2)}, u32[]{:S(2)}) async-start(f32[16,24,128]{2,1,0:T(8,128)} %bitcast.1), calls=%async_computation | async-start | bytes 393216 | tf_op jit(solution)/shard_map/all_to_all | solution.py:673
  13.5 0.0 copy-start.2
  13.5 0.1 copy.31.mode_in_ref
  13.7 0.0 copy-start.5
  13.7 0.0 copy-start.10
  13.7 0.0 copy-start.12
  13.7 0.0 copy-start.13
  13.7 0.0 copy-start.20
  13.8 0.1 copy.32.mode_out_ref
  13.9 0.0 copy-start.9
  13.9 0.0 copy-start.11
  14.0 0.5 copy-done.2
  14.4 0.2 copy-done.5
  14.6 0.0 copy-start.15
  14.7 1.2 %copy-done.15 = bf16[256,2048]{1,0:T(8,128)(2,1)S(1)} copy-done((bf16[256,2048]{1,0:T(8,128)(2,1)S(1)}, bf16[256,2048]{1,0:T(8,128)(2,1)}, u32[]{:S(2)}) %copy-start.15) | copy-done | bytes 1048600
  15.9 0.9 %copy-done.18 = bf16[256,256]{1,0:T(8,128)(2,1)S(1)} copy-done((bf16[256,256]{1,0:T(8,128)(2,1)S(1)}, bf16[256,256]{1,0:T(8,128)(2,1)}, u32[]{:S(2)}) %copy-start.18) | copy-done | bytes 131096
  16.8 1.1 %shard_map.277 = (bf16[1024,256]{1,0:T(8,128)(2,1)S(1)}, bf16[384,1024]{1,0:T(8,128)(2,1)S(1)}, f32[8,1024]{1,0:T(8,128)S(1)}, f32[24,128]{1,0:T(8,128)S(1)}, f3...) custom-call(s32[1]{0:T(128)} %bitcast.3.place_ref, ...), custom_call_target="tpu_custom_call" | custom-call | flops 4000000000 | bytes 8000000 | tf_op jit(solution)/shard_map/pallas_call | solution.py:715
  17.9 0.9 %copy-done.23 = bf16[384,1024]{1,0:T(8,128)(2,1)} copy-done((bf16[384,1024]{1,0:T(8,128)(2,1)}, bf16[384,1024]{1,0:T(8,128)(2,1)S(1)}, u32[]{:S(2)}) %copy-start.23) | copy-done | bytes 786456
  18.8 0.6 copy-done.25
  19.4 0.6 copy-done.27
  19.9 2.2 %all-to-all-done = f32[16,24,128]{2,1,0:T(8,128)S(1)} async-done(((f32[16,24,128]{2,1,0:T(8,128)}), f32[16,24,128]{2,1,0:T(8,128)S(1)}, u32[]{:S(2)}, u32[]{:S(2)}) %all-to-all-start) | async-done | bytes 196640 | tf_op jit(solution)/shard_map/all_to_all | solution.py:673
  22.2 1.4 %shard_map.278 = (f32[256,128]{1,0:T(8,128)}, f32[256,128]{1,0:T(8,128)S(1)}, f32[256,128]{1,0:T(8,128)S(1)}, f32[256,128]{1,0:T(8,128)S(1)}) custom-call(f32[384,128]{1,0:T(8,128)S(1)} %bitcast.17, f32[48,128]{1,0:T(8,128)S(1)} %get-tuple-element.39.own_ref, bf16[1024,256]{1,0:T(8,128)(2,1)S(1)} %get-tuple-element.40.ahead_ref, ...), custom_call_target="tpu_custom_call" | custom-call | flops 100000000 | bytes 1000000 | tf_op jit(solution)/shard_map/pallas_call | solution.py:756
  23.5 4.8 %all-to-all-start.1 = ((f32[16,16,128]{2,1,0:T(8,128)}), f32[16,16,128]{2,1,0:T(8,128)S(1)}, u32[]{:S(2)}, u32[]{:S(2)}) async-start(f32[16,16,128]{2,1,0:T(8,128)} %bitcast.7), calls=%async_computation.1 | async-start | bytes 262144 | tf_op jit(solution)/shard_map/all_to_all | solution.py:673
  28.4 0.0 copy-start.26
  28.4 0.7 %copy-done.26 = f32[24,128]{1,0:T(8,128)S(1)} copy-done((f32[24,128]{1,0:T(8,128)S(1)}, f32[24,128]{1,0:T(8,128)}, u32[]{:S(2)}) %copy-start.26) | copy-done | bytes 12312
  29.1 1.2 %copy-done.14 = bf16[1024,512]{1,0:T(8,128)(2,1)S(1)} copy-done((bf16[1024,512]{1,0:T(8,128)(2,1)S(1)}, bf16[1024,512]{1,0:T(8,128)(2,1)}, u32[]{:S(2)}) %copy-start.14) | copy-done | bytes 1048600
  30.3 0.9 %copy-done.17 = bf16[1024,128]{1,0:T(8,128)(2,1)S(1)} copy-done((bf16[1024,128]{1,0:T(8,128)(2,1)S(1)}, bf16[1024,128]{1,0:T(8,128)(2,1)}, u32[]{:S(2)}) %copy-start.17) | copy-done | bytes 262168
  31.3 1.1 %copy-done.24 = bf16[384,1024]{1,0:T(8,128)(2,1)S(1)} copy-done((bf16[384,1024]{1,0:T(8,128)(2,1)S(1)}, bf16[384,1024]{1,0:T(8,128)(2,1)}, u32[]{:S(2)}) %copy-start.24) | copy-done | bytes 786456
  32.4 1.7 %shard_map.279 = (f32[256,128]{1,0:T(8,128)S(1)}, f32[24,128]{1,0:T(8,128)S(1)}) custom-call(s32[1]{0:T(128)} %bitcast.3.place_ref, f32[384,128]{1,0:T(8,128)S(1)} %bitcast.18, f32[48,128]{1,0:T(8,128)S(1)} %get-tuple-element.39.own_ref, f32[256,128]{1,0:T(8,128)S(1)} %get-tuple-element.46.mean_ref, f32[256,128]{1,0:T(8,128)S(1)} %get-tuple-element.47.inverse_ref, ...), custom_call_target="tpu_custom_call" | custom-call | flops 4000000000 | bytes 8000000 | tf_op jit(solution)/shard_map/pallas_call | solution.py:766
  34.0 2.1 %all-to-all-done.1 = f32[16,16,128]{2,1,0:T(8,128)S(1)} async-done(((f32[16,16,128]{2,1,0:T(8,128)}), f32[16,16,128]{2,1,0:T(8,128)S(1)}, u32[]{:S(2)}, u32[]{:S(2)}) %all-to-all-start.1) | async-done | bytes 131104 | tf_op jit(solution)/shard_map/all_to_all | solution.py:673
  36.2 1.1 %shard_map.280 = (f32[1,160,90]{2,1,0:T(8,128)}, f32[512,128]{1,0:T(8,128)}) custom-call(f32[256,128]{1,0:T(8,128)S(1)} %bitcast.19, f32[160,90]{1,0:T(8,128)S(1)} %get-tuple-element.42.base_ref, bf16[2,160,160]{2,1,0:T(8,128)(2,1)S(1)} %get-tuple-element.43.masked_ref, f32[160,256]{1,0:T(8,128)S(1)} %get-tuple-element.44.same_ref, ...), custom_call_target="tpu_custom_call" | custom-call | flops 100000000 | bytes 1000000 | tf_op jit(solution)/shard_map/pallas_call | solution.py:789
  37.2 3.8 %all-to-all-start.2 = ((f32[32,16,128]{2,1,0:T(8,128)}), f32[32,16,128]{2,1,0:T(8,128)S(1)}, u32[]{:S(2)}, u32[]{:S(2)}) async-start(f32[32,16,128]{2,1,0:T(8,128)} %bitcast.10), calls=%async_computation.2 | async-start | bytes 524288 | tf_op jit(solution)/shard_map/all_to_all | solution.py:673
  41.0 10.6 %all-to-all-done.2 = f32[32,16,128]{2,1,0:T(8,128)S(1)} async-done(((f32[32,16,128]{2,1,0:T(8,128)}), f32[32,16,128]{2,1,0:T(8,128)S(1)}, u32[]{:S(2)}, u32[]{:S(2)}) %all-to-all-start.2) | async-done | bytes 262176 | tf_op jit(solution)/shard_map/all_to_all | solution.py:673
  51.6 0.7 %shard_map.281 = (f32[256,128]{1,0:T(8,128)}, f32[80,128]{1,0:T(8,128)S(1)}, f32[80,128]{1,0:T(8,128)S(1)}) custom-call(s32[1]{0:T(128)} %bitcast.9.core_ref, f32[512,128]{1,0:T(8,128)S(1)} %bitcast.20), custom_call_target="tpu_custom_call" | custom-call | flops 100000000 | bytes 1000000 | tf_op jit(solution)/shard_map/pallas_call | solution.py:798
  52.4 2.6 %all-to-all-start.3 = ((f32[32,8,128]{2,1,0:T(8,128)}), f32[32,8,128]{2,1,0:T(8,128)S(1)}, u32[]{:S(2)}, u32[]{:S(2)}) async-start(f32[32,8,128]{2,1,0:T(8,128)} %bitcast.12), calls=%async_computation.3 | async-start | bytes 262144 | tf_op jit(solution)/shard_map/all_to_all | solution.py:673
  54.9 0.2 collective-permute-start
  55.1 1.1 %collective-permute-done.theirs_ref = f32[80,128]{1,0:T(8,128)S(1)} collective-permute-done((f32[80,128]{1,0:T(8,128)S(1)}, f32[80,128]{1,0:T(8,128)S(1)}, u32[]{:S(2)}, u32[]{:S(2)}) %collective-permute-start) | collective-permute-done | bytes 40992 | tf_op jit(solution)/shard_map/ppermute | solution.py:806
  56.2 0.6 shard_map.282
  56.9 6.3 %all-to-all-done.3 = f32[32,8,128]{2,1,0:T(8,128)S(1)} async-done(((f32[32,8,128]{2,1,0:T(8,128)}), f32[32,8,128]{2,1,0:T(8,128)S(1)}, u32[]{:S(2)}, u32[]{:S(2)}) %all-to-all-start.3) | async-done | bytes 131104 | tf_op jit(solution)/shard_map/all_to_all | solution.py:673
  63.2 0.9 %shard_map.283 = (f32[1,160]{1,0:T(1,128)}, f32[1,160]{1,0:T(1,128)}, f32[256,4]{1,0:T(8,128)S(1)}, f32[256,4]{1,0:T(8,128)S(1)}, f32[4,32]{1,0:T(4,128)}, /*ind...) custom-call(f32[256,128]{1,0:T(8,128)S(1)} %bitcast.21, f32[1,256]{1,0:T(1,128)S(1)} %copy-done.21), custom_call_target="tpu_custom_call" | custom-call | flops 100000000 | bytes 1000000 | tf_op jit(solution)/shard_map/pallas_call | solution.py:814
  64.0 0.7 %copy.33 = f32[256,4]{0,1:T(4,128)} copy(f32[256,4]{1,0:T(8,128)S(1)} %get-tuple-element.72) | data formatting | bytes 8192
  64.7 0.7 %copy.34 = f32[256,4]{0,1:T(4,128)} copy(f32[256,4]{1,0:T(8,128)S(1)} %get-tuple-element.73) | data formatting | bytes 8192
  (36 shorter events, 0.1 us)
Async XLA Ops:
  0.6 0.7 %copy-start.8 = (s32[160]{0:T(256)S(1)}, s32[160]{0:T(256)}, u32[]{:S(2)}) copy-start(s32[160]{0:T(256)} %param.22) | copy-start | bytes 1924
  1.3 0.9 %copy-start.1 = (f32[160,160]{1,0:T(8,128)S(1)}, f32[160,160]{1,0:T(8,128)}, u32[]{:S(2)}) copy-start(f32[160,160]{1,0:T(8,128)} %mixing_ref.3) | copy-start | bytes 307204
  2.2 0.9 %copy-start.4 = (f32[1,160,90]{2,1,0:T(8,128)S(1)}, f32[1,160,90]{2,1,0:T(8,128)}, u32[]{:S(2)}) copy-start(f32[1,160,90]{2,1,0:T(8,128)} %series_ref.3) | copy-start | bytes 172804
  3.1 0.9 %copy-start.6 = (f32[1,160,90]{2,1,0:T(8,128)S(1)}, f32[1,160,90]{2,1,0:T(8,128)}, u32[]{:S(2)}) copy-start(f32[1,160,90]{2,1,0:T(8,128)} %cot_ref.5) | copy-start | bytes 172804
  4.0 9.9 %copy-start.16 = (f32[128,1024]{1,0:T(8,128)S(1)}, f32[128,1024]{1,0:T(8,128)}, u32[]{:S(2)}) copy-start(f32[128,1024]{1,0:T(8,128)} %constant.31.clone.turn_ref) | copy-start | bytes 1572868
  5.0 8.5 %copy-start.29 = (f32[256,4]{0,1:T(4,128)S(1)}, f32[256,4]{0,1:T(4,128)}, u32[]{:S(2)}) copy-start(f32[256,4]{0,1:T(4,128)} %param.25) | copy-start | bytes 12292
  5.0 8.7 %copy-start.30 = (f32[256,4]{0,1:T(4,128)S(1)}, f32[256,4]{0,1:T(4,128)}, u32[]{:S(2)}) copy-start(f32[256,4]{0,1:T(4,128)} %param.26) | copy-start | bytes 12292
  5.0 8.9 %copy-start.7 = (f32[1,160,90]{2,1,0:T(8,128)S(1)}, f32[1,160,90]{2,1,0:T(8,128)}, u32[]{:S(2)}) copy-start(f32[1,160,90]{2,1,0:T(8,128)} %cot_ref.5) | copy-start | bytes 172804
  5.0 8.9 %copy-start.21 = (f32[1,256]{1,0:T(1,128)S(1)}, f32[1,256]{1,0:T(1,128)}, u32[]{:S(2)}) copy-start(f32[1,256]{1,0:T(1,128)} %constant.30.clone.endpoint_ref) | copy-start | bytes 3076
  5.0 8.9 %copy-start.22 = (f32[1,64]{1,0:T(1,128)S(1)}, f32[1,64]{1,0:T(1,128)}, u32[]{:S(2)}) copy-start(f32[1,64]{1,0:T(1,128)} %constant.32.clone.scale_ref) | copy-start | bytes 772
  5.1 17.1 %all-to-all-start = ((f32[16,24,128]{2,1,0:T(8,128)}), f32[16,24,128]{2,1,0:T(8,128)S(1)}, u32[]{:S(2)}, u32[]{:S(2)}) async-start(f32[16,24,128]{2,1,0:T(8,128)} %bitcast.1), calls=%async_computation | async-start | bytes 393216 | tf_op jit(solution)/shard_map/all_to_all | solution.py:673
  13.5 0.9 %copy-start.2 = (f32[160,160]{1,0:T(8,128)S(1)}, f32[160,160]{1,0:T(8,128)}, u32[]{:S(2)}) copy-start(f32[160,160]{1,0:T(8,128)} %mixing_ref.3) | copy-start | bytes 307204
  13.7 0.9 %copy-start.5 = (f32[1,160,90]{2,1,0:T(8,128)S(1)}, f32[1,160,90]{2,1,0:T(8,128)}, u32[]{:S(2)}) copy-start(f32[1,160,90]{2,1,0:T(8,128)} %series_ref.3) | copy-start | bytes 172804
  13.7 0.9 %copy-start.10 = (f32[4,32]{1,0:T(4,128)S(1)}, f32[4,32]{1,0:T(4,128)}, u32[]{:S(2)}) copy-start(f32[4,32]{1,0:T(4,128)} %mode_im_ref.1) | copy-start | bytes 1540
  13.7 0.9 %copy-start.12 = (f32[160]{0:T(256)S(1)}, f32[160]{0:T(256)}, u32[]{:S(2)}) copy-start(f32[160]{0:T(256)} %param.24) | copy-start | bytes 1924
  13.7 0.9 %copy-start.13 = (f32[160]{0:T(256)S(1)}, f32[160]{0:T(256)}, u32[]{:S(2)}) copy-start(f32[160]{0:T(256)} %param.30) | copy-start | bytes 1924
  13.7 0.9 %copy-start.20 = (f32[64,1]{1,0:T(8,128)S(1)}, f32[64,1]{1,0:T(8,128)}, u32[]{:S(2)}) copy-start(f32[64,1]{1,0:T(8,128)} %constant.33.clone.scale_t_ref) | copy-start | bytes 772
  13.9 0.7 %copy-start.9 = (f32[4,32]{1,0:T(4,128)S(1)}, f32[4,32]{1,0:T(4,128)}, u32[]{:S(2)}) copy-start(f32[4,32]{1,0:T(4,128)} %mode_re_ref.1) | copy-start | bytes 1540
  13.9 0.7 %copy-start.11 = (f32[160]{0:T(256)S(1)}, f32[160]{0:T(256)}, u32[]{:S(2)}) copy-start(f32[160]{0:T(256)} %param.23) | copy-start | bytes 1924
  14.6 1.2 %copy-start.15 = (bf16[256,2048]{1,0:T(8,128)(2,1)S(1)}, bf16[256,2048]{1,0:T(8,128)(2,1)}, u32[]{:S(2)}) copy-start(bf16[256,2048]{1,0:T(8,128)(2,1)} %constant.28.clone.weights_ref) | copy-start | bytes 3145732
  15.9 0.9 %copy-start.18 = (bf16[256,256]{1,0:T(8,128)(2,1)S(1)}, bf16[256,256]{1,0:T(8,128)(2,1)}, u32[]{:S(2)}) copy-start(bf16[256,256]{1,0:T(8,128)(2,1)} %constant.37.clone.later_ref) | copy-start | bytes 393220
  16.8 5.4 %copy-start = (bf16[384,1024]{1,0:T(8,128)(2,1)S(1)}, bf16[384,1024]{1,0:T(8,128)(2,1)}, u32[]{:S(2)}) copy-start(bf16[384,1024]{1,0:T(8,128)(2,1)} %constant.35.clone.from_modes_ref) | copy-start | bytes 2359300
  16.8 5.4 %copy-start.3 = (bf16[256,256]{1,0:T(8,128)(2,1)S(1)}, bf16[256,256]{1,0:T(8,128)(2,1)}, u32[]{:S(2)}) copy-start(bf16[256,256]{1,0:T(8,128)(2,1)} %constant.36.clone.earlier_ref) | copy-start | bytes 393220
  17.8 0.9 %copy-start.23 = (bf16[384,1024]{1,0:T(8,128)(2,1)}, bf16[384,1024]{1,0:T(8,128)(2,1)S(1)}, u32[]{:S(2)}) copy-start(bf16[384,1024]{1,0:T(8,128)(2,1)S(1)} %get-tuple-element.49.back_ref) | copy-start | bytes 2359300
  18.7 0.6 copy-start.25
  19.3 0.6 copy-start.27
  23.5 4.9 %copy-start.19 = (bf16[256,256]{1,0:T(8,128)(2,1)S(1)}, bf16[256,256]{1,0:T(8,128)(2,1)}, u32[]{:S(2)}) copy-start(bf16[256,256]{1,0:T(8,128)(2,1)} %constant.37.clone.later_ref) | copy-start | bytes 393220
  23.5 4.9 %copy-start.28 = (f32[8,256]{1,0:T(8,128)S(1)}, f32[8,256]{1,0:T(8,128)}, u32[]{:S(2)}) copy-start(f32[8,256]{1,0:T(8,128)} %copy-done.27) | copy-start | bytes 24580
  23.5 12.6 %all-to-all-start.1 = ((f32[16,16,128]{2,1,0:T(8,128)}), f32[16,16,128]{2,1,0:T(8,128)S(1)}, u32[]{:S(2)}, u32[]{:S(2)}) async-start(f32[16,16,128]{2,1,0:T(8,128)} %bitcast.7), calls=%async_computation.1 | async-start | bytes 262144 | tf_op jit(solution)/shard_map/all_to_all | solution.py:673
  28.4 0.7 %copy-start.26 = (f32[24,128]{1,0:T(8,128)S(1)}, f32[24,128]{1,0:T(8,128)}, u32[]{:S(2)}) copy-start(f32[24,128]{1,0:T(8,128)} %copy-done.25) | copy-start | bytes 36868
  29.1 1.2 %copy-start.14 = (bf16[1024,512]{1,0:T(8,128)(2,1)S(1)}, bf16[1024,512]{1,0:T(8,128)(2,1)}, u32[]{:S(2)}) copy-start(bf16[1024,512]{1,0:T(8,128)(2,1)} %constant.29.clone.weights_t_ref) | copy-start | bytes 3145732
  30.3 0.9 %copy-start.17 = (bf16[1024,128]{1,0:T(8,128)(2,1)S(1)}, bf16[1024,128]{1,0:T(8,128)(2,1)}, u32[]{:S(2)}) copy-start(bf16[1024,128]{1,0:T(8,128)(2,1)} %constant.34.clone.to_modes_ref) | copy-start | bytes 786436
  31.3 1.1 %copy-start.24 = (bf16[384,1024]{1,0:T(8,128)(2,1)S(1)}, bf16[384,1024]{1,0:T(8,128)(2,1)}, u32[]{:S(2)}) copy-start(bf16[384,1024]{1,0:T(8,128)(2,1)} %copy-done.23) | copy-start | bytes 2359300
  37.2 14.4 %all-to-all-start.2 = ((f32[32,16,128]{2,1,0:T(8,128)}), f32[32,16,128]{2,1,0:T(8,128)S(1)}, u32[]{:S(2)}, u32[]{:S(2)}) async-start(f32[32,16,128]{2,1,0:T(8,128)} %bitcast.10), calls=%async_computation.2 | async-start | bytes 524288 | tf_op jit(solution)/shard_map/all_to_all | solution.py:673
  52.4 10.8 %all-to-all-start.3 = ((f32[32,8,128]{2,1,0:T(8,128)}), f32[32,8,128]{2,1,0:T(8,128)S(1)}, u32[]{:S(2)}, u32[]{:S(2)}) async-start(f32[32,8,128]{2,1,0:T(8,128)} %bitcast.12), calls=%async_computation.3 | async-start | bytes 262144 | tf_op jit(solution)/shard_map/all_to_all | solution.py:673
  54.9 1.3 %collective-permute-start = (f32[80,128]{1,0:T(8,128)S(1)}, f32[80,128]{1,0:T(8,128)S(1)}, u32[]{:S(2)}, u32[]{:S(2)}) collective-permute-start(f32[80,128]{1,0:T(8,128)S(1)} %get-tuple-element.58), channel_id=1, source_target_pairs={{0,1},{1,0},{2,3},{3,2},{4,5},{5,4},{6,7},{7,6},{8,9},{9,8},{10,11... | collective-permute-start | bytes 122888 | tf_op jit(solution)/shard_map/ppermute | solution.py:806

commit v2 on v1

v2 whole, which is shorter than its diff:
```python
import functools
import math

import jax
import jax.numpy as jnp
import ml_dtypes
import numpy as np
from jax import lax
from jax.experimental import pallas as pl
from jax.experimental.pallas import tpu as pltpu
from jax.sharding import PartitionSpec as P

ORDER = 256
MODES = 32
RANK = 4
WINDOW = 720
EPSILON = 1e-05

LANES = 128
SLOT = 16
SEND = 24
f32 = jnp.float32
bf16 = jnp.bfloat16


def up(value, multiple):
    return -(-value // multiple) * multiple


def legendre_table():
    one, two = np.float32(1.0), np.float32(2.0)
    lags = np.arange(WINDOW).astype(np.float32)
    points = one - (two * (lags + np.float32(0.5))) * np.float32(1.0 / WINDOW)
    lower, this = np.zeros_like(points), np.ones_like(points)
    rows = []
    for degree in np.arange(ORDER).astype(np.float32):
        rows.append(this)
        upper = ((two * degree + one) * points * this - degree * lower) / (degree + one)
        lower, this = this, upper
    return np.stack(rows)


def in_blocks(values, steps):
    blocks = WINDOW // steps
    framed = np.zeros(values.shape[:-1] + (blocks, LANES))
    framed[..., :steps] = values.reshape(values.shape[:-1] + (blocks, steps))
    return framed.reshape(values.shape[:-1] + (blocks * LANES,))


def halves(values):
    high = values.astype(np.float32).astype(ml_dtypes.bfloat16)
    low = (values - high.astype(np.float64)).astype(ml_dtypes.bfloat16)
    return high, low


def constants(steps):
    legendre = legendre_table()
    degree = np.arange(ORDER).astype(np.float32)
    weights = legendre * ((np.float32(2.0) * degree + np.float32(1.0)) / np.float32(WINDOW))[:, None]
    flipped = in_blocks(weights[:, ::-1], steps)
    high, low = halves(flipped)
    table = {}
    table["weights"] = np.concatenate([high, low], 1)
    table["weights_t"] = np.concatenate([high.T, low.T], 1)
    table["endpoint"] = legendre[:, 0][None, :].astype(np.float32)
    mode = np.arange(MODES)[:, None]
    step = np.arange(WINDOW)[None, :]
    angle = 2.0 * math.pi / WINDOW * (mode * step % WINDOW)
    cosine, sine = np.cos(angle), np.sin(angle)
    back = 2.0 * math.pi / WINDOW * (mode * (WINDOW - 1 - step) % WINDOW)
    table["turn"] = np.concatenate(
        [in_blocks(v, steps) for v in (cosine, sine, np.cos(back), np.sin(back))]
    ).astype(np.float32)
    scale = np.where(np.arange(MODES) == 0, 1.0, 2.0) / WINDOW
    table["scale"] = np.tile(scale, 4)[None, :].astype(np.float32)
    high, low = halves(in_blocks(np.concatenate([cosine, -sine]), steps))
    table["to_modes"] = np.concatenate([high.T, low.T], 1)
    wave = in_blocks(np.concatenate([scale[:, None] * cosine, -scale[:, None] * sine]), steps)
    table["from_modes"] = np.concatenate(halves(wave), 1)
    lane = np.arange(LANES)
    upper = (lane[:, None] <= lane[None, :]).astype(np.float32)
    ones = np.ones((LANES, LANES), np.float32)
    for name, part in (("earlier", upper), ("later", upper.T)):
        both = np.concatenate([part, ones], 1)
        table[name] = np.concatenate([both, both]).astype(ml_dtypes.bfloat16)
    return table


def split(value):
    high = value.astype(bf16)
    return high, (value - high.astype(f32)).astype(bf16)


def dot(a, b):
    return lax.dot_general(a, b, (((1,), (0,)), ((), ())), preferred_element_type=f32)


def dot_nt(a, b):
    return lax.dot_general(a, b, (((1,), (1,)), ((), ())), preferred_element_type=f32)


def stacked_dot(value, table):
    rows, width = value.shape[0], table.shape[1] // 2
    high, low = split(value)
    out = dot(jnp.concatenate([high, low], 0), table)
    return out[:rows, :width] + out[:rows, width:] + out[rows:, :width]


def scan_lanes(value, table):
    high, low = split(value)
    out = dot(jnp.concatenate([high, low], 1), table)
    return out[:, :LANES], out[:, LANES:]


def row_of(i, kind):
    return 8 * kind + i if i < 8 else 16 + (i - 8) + 2 * kind


def order_mask(blocks):
    return blocks * 11 // 16


def to_wide(blocks, windows):
    per = len(blocks) // windows
    return jnp.concatenate(
        [jnp.concatenate(blocks[w * per : (w + 1) * per], 1) for w in range(windows)], 0
    )


def to_blocks(wide, windows):
    per = wide.shape[1] // LANES
    return [
        wide[w * SLOT : (w + 1) * SLOT, b * LANES : (b + 1) * LANES]
        for w in range(windows)
        for b in range(per)
    ]


def fetch(pairs, sems):
    copies = [pltpu.make_async_copy(a, b, sems.at[k]) for k, (a, b) in enumerate(pairs)]
    for copy in copies:
        copy.start()

    def ready(*which):
        for k in which:
            copies[k].wait()

    return ready


def blocks_of(value):
    return [value[k * SLOT : (k + 1) * SLOT] for k in range(value.shape[0] // SLOT)]


def same_rows(groups_ref, start, rows):
    channels = groups_ref.shape[1]
    ids = groups_ref[...].astype(f32)
    row = lax.broadcasted_iota(jnp.int32, (rows, channels), 0) + start
    lane = lax.broadcasted_iota(jnp.int32, (rows, channels), 1)
    column = jnp.sum(jnp.where(row == lane, ids, 0.0), axis=1, keepdims=True)
    return column == ids


def own_lanes(place, width, count, blocks):
    row = lax.broadcasted_iota(jnp.int32, (SLOT, width), 0)
    lane = lax.broadcasted_iota(jnp.int32, (SLOT, width), 1)
    return (lane == row * blocks + place) & (row < count)


def send_kernel(
    own,
    series_hbm,
    cot_hbm,
    mixing_hbm,
    groups_hbm,
    send_ref,
    grad_ref,
    series_ref,
    cot_ref,
    mixing_ref,
    groups_ref,
    pad_ref,
    sems,
):
    channels, steps = cot_ref.shape[1:]
    blocks = channels // own
    ready = fetch(
        [
            (groups_hbm, groups_ref),
            (mixing_hbm, mixing_ref),
            (cot_hbm, cot_ref),
            (series_hbm, series_ref),
        ],
        sems,
    )
    zero = jnp.zeros((blocks, LANES), f32)
    for r in range(row_of(own - 1, 1) + 1, SEND):
        send_ref[pl.ds(r, blocks, stride=SEND), :] = zero
    pad_ref[...] = jnp.zeros_like(pad_ref)
    ready(0, 1, 2)
    pad_ref[:, :steps] = cot_ref[0]
    chunk = channels if channels <= 512 else 256
    total = None
    for start in range(0, channels, chunk):
        same = same_rows(groups_ref, start, chunk)
        masked = jnp.where(same, mixing_ref[start : start + chunk, :], 0.0)
        high, low = split(masked.T)
        both = jnp.concatenate(split(pad_ref[start : start + chunk, :]), 1)
        out = dot(jnp.concatenate([high, low], 0), both)
        part = out[:channels, :LANES] + out[:channels, LANES:] + out[channels:, :LANES]
        total = part if total is None else total + part
    grad_ref[...] = total
    ready(3)
    pad_ref[:, :steps] = series_ref[0]
    for i in range(own):
        at = slice(blocks * i, blocks * (i + 1))
        send_ref[pl.ds(row_of(i, 0), blocks, stride=SEND), :] = pad_ref[at, :]
        send_ref[pl.ds(row_of(i, 1), blocks, stride=SEND), :] = grad_ref[at, :]


def table_kernel(
    own,
    block_ref,
    cot_hbm,
    mixing_hbm,
    groups_hbm,
    gain_hbm,
    bias_hbm,
    out_bias_hbm,
    mode_in_hbm,
    mode_out_hbm,
    mode_re_hbm,
    mode_im_hbm,
    weights_hbm,
    endpoint_hbm,
    turn_hbm,
    scale_hbm,
    later_hbm,
    ahead_ref,
    lines_ref,
    own_ref,
    columns_ref,
    masked_ref,
    same_ref,
    cot3_ref,
    cot_sum_ref,
    cot_ref,
    mixing_ref,
    groups_ref,
    gain_ref,
    bias_ref,
    out_bias_ref,
    mode_in_ref,
    mode_out_ref,
    mode_re_ref,
    mode_im_ref,
    weights_ref,
    endpoint_ref,
    turn_ref,
    scale_ref,
    later_ref,
    pad_ref,
    turned_ref,
    sems,
):
    ready = fetch(
        [
            (mode_in_hbm, mode_in_ref),
            (mode_out_hbm, mode_out_ref),
            (endpoint_hbm, endpoint_ref),
            (weights_hbm, weights_ref),
            (mode_re_hbm, mode_re_ref),
            (mode_im_hbm, mode_im_ref),
            (scale_hbm, scale_ref),
            (turn_hbm, turn_ref),
            (later_hbm, later_ref),
            (groups_hbm, groups_ref),
            (mixing_hbm, mixing_ref),
            (cot_hbm, cot_ref),
            (gain_hbm, gain_ref),
            (bias_hbm, bias_ref),
            (out_bias_hbm, out_bias_ref),
        ],
        sems,
    )
    channels, steps = cot_ref.shape[1:]
    width = ahead_ref.shape[0]
    per = width // LANES
    blocks = channels // own
    count = 2 * MODES
    lines_ref[...] = jnp.zeros_like(lines_ref)
    turned_ref[...] = jnp.zeros_like(turned_ref)
    pad_ref[...] = jnp.zeros_like(pad_ref)
    ready(0, 1, 2, 3)
    high, low = split(mode_in_ref[...])
    out = dot(jnp.concatenate([high, low], 0), weights_ref[...])
    kernel = out[:RANK, :width] + out[:RANK, width:] + out[RANK:, :width]
    lines_ref[0:RANK, :] = kernel
    mix = jnp.sum(mode_out_ref[...] * endpoint_ref[...], axis=1, keepdims=True)
    ready(4, 5, 6)
    scale = scale_ref[:, 0:count]
    gain_re, gain_im = mode_re_ref[...], mode_im_ref[...]
    signed = jnp.concatenate([gain_re, -gain_im], 1) * scale
    sign = jnp.where(lax.broadcasted_iota(jnp.int32, (RANK, count), 1) < MODES, 1.0, -1.0)
    lines_ref[8 : 8 + RANK, 0:count] = signed * mix
    lines_ref[16 : 16 + RANK, 0:count] = sign * scale * mix
    lines_ref[24 : 24 + RANK, 0:count] = signed
    lines_ref[28:29, 0:LANES] = scale_ref[...]
    turned_ref[0:RANK, 0:count] = jnp.concatenate([gain_re, gain_im], 1) * mix
    columns = turned_ref[...].T[0:count]
    response = None
    for r in range(RANK):
        term = columns[:, r : r + 1] * kernel[r : r + 1, :]
        response = term if response is None else response + term
    ready(7, 8)
    real, imag = response[:MODES], response[MODES:]
    cosine, sine = turn_ref[0:MODES], turn_ref[MODES : 2 * MODES]
    cos_b, sin_b = turn_ref[2 * MODES : 3 * MODES], turn_ref[3 * MODES : 4 * MODES]
    turned = jnp.concatenate([real * cos_b + imag * sin_b, imag * cos_b - real * sin_b], 0)
    rows = jnp.concatenate([turned[:, b * LANES : (b + 1) * LANES] for b in range(per)], 0)
    local, total = scan_lanes(rows, later_ref[...])
    run = jnp.zeros((count, LANES), f32)
    suffix = [None] * per
    for b in reversed(range(per)):
        suffix[b] = local[b * count : (b + 1) * count] + run
        run = run + total[b * count : (b + 1) * count]
    for b in range(per):
        at = slice(b * LANES, (b + 1) * LANES)
        c, s = cosine[:, at], sine[:, at]
        parts = []
        for value in (suffix[b], run - suffix[b]):
            re, im = value[:MODES], value[MODES:]
            parts += [re * c + im * s, im * c - re * s]
        high, low = split(jnp.concatenate(parts, 0).T)
        ahead_ref[at, 0:LANES] = high
        ahead_ref[at, LANES : 2 * LANES] = low
    ready(9, 10, 11, 12, 13, 14)
    chunk = channels if channels <= 512 else 256
    for start in range(0, channels, chunk):
        at = slice(start, start + chunk)
        same = same_rows(groups_ref, start, chunk)
        high, low = split(jnp.where(same, mixing_ref[at, :], 0.0))
        masked_ref[0, at, :] = high
        masked_ref[1, at, :] = low
        same_ref[at, 0:channels] = jnp.where(same, 1.0, 0.0)
        row = lax.broadcasted_iota(jnp.int32, (chunk, channels), 0) + start
        lane = lax.broadcasted_iota(jnp.int32, (chunk, channels), 1)
        for k, ref in enumerate((gain_ref, bias_ref, out_bias_ref)):
            columns_ref[at, k : k + 1] = jnp.sum(
                jnp.where(row == lane, ref[...], 0.0), axis=1, keepdims=True
            )
    mine = own_lanes(block_ref[0] ^ order_mask(blocks), channels, own, blocks)
    gain = jnp.sum(jnp.where(mine, gain_ref[...], 0.0), axis=1, keepdims=True)
    gain = jnp.where(lax.broadcasted_iota(jnp.int32, (SLOT, 1), 0) < own, gain, 1.0)
    bias = jnp.sum(jnp.where(mine, bias_ref[...], 0.0), axis=1, keepdims=True)
    own_ref[0:SLOT, :] = jnp.broadcast_to(gain, (SLOT, LANES))
    own_ref[SLOT : 2 * SLOT, :] = jnp.broadcast_to(bias, (SLOT, LANES))
    own_ref[2 * SLOT : 3 * SLOT, :] = jnp.broadcast_to(1.0 / gain, (SLOT, LANES))
    pad_ref[0:channels, :steps] = cot_ref[0]
    high, low = split(pad_ref[...])
    cot3_ref[...] = jnp.concatenate([high, high, low], 1)
    cot_sum_ref[...] = dot_nt(
        jnp.ones((8, 2 * LANES), bf16), jnp.concatenate([high, low], 1)
    )


def normalized(x, blocks, steps, earlier):
    rows = x.shape[0]
    local, total = scan_lanes(jnp.concatenate([x, x * x], 0), earlier)
    first, second = blocks_of(local[:rows]), blocks_of(local[rows:])
    first_all, second_all = blocks_of(total[:rows]), blocks_of(total[rows:])
    run_one = jnp.zeros((SLOT, LANES), f32)
    run_two = jnp.zeros((SLOT, LANES), f32)
    lane = lax.broadcasted_iota(jnp.int32, (SLOT, LANES), 1)
    found = []
    for k in range(blocks):
        inverse = 1.0 / (lane + (k * steps + 1 + WINDOW)).astype(f32)
        mean = (first[k] + run_one) * inverse
        variance = (second[k] + run_two + WINDOW) * inverse - mean * mean + EPSILON
        found.append((mean, variance, run_one, run_two))
        run_one = run_one + first_all[k]
        run_two = run_two + second_all[k]
    return found


def owned(recv_ref, blocks):
    got = recv_ref[...].reshape(blocks, SEND, LANES)
    tail = pltpu.roll(got[:, 16:24], 6, 1)
    x = jnp.concatenate([got[:, 0:8], got[:, 16:24]], 1)
    grad = jnp.concatenate([got[:, 8:16], tail], 1)
    mask = order_mask(blocks)
    return [x[b ^ mask] for b in range(blocks)], [grad[b ^ mask] for b in range(blocks)]


def forward_kernel(
    own,
    blocks,
    steps,
    recv_ref,
    own_ref,
    ahead_ref,
    from_modes_ref,
    to_modes_ref,
    earlier_ref,
    send_ref,
    mean_ref,
    inverse_ref,
    shifted_ref,
    waves_ref,
):
    windows = blocks * steps // WINDOW
    width = ahead_ref.shape[0]
    x, grad = owned(recv_ref, blocks)
    found = normalized(jnp.concatenate(x, 0), blocks, steps, earlier_ref[...])
    gain, bias, over = own_ref[0:SLOT], own_ref[SLOT : 2 * SLOT], own_ref[2 * SLOT : 3 * SLOT]
    row = lax.broadcasted_iota(jnp.int32, (SLOT, LANES), 0)
    lane = lax.broadcasted_iota(jnp.int32, (SLOT, LANES), 1)
    held = (row < own) & (lane < steps)
    normal, spreads, recon_grad = [], [], []
    for k in range(blocks):
        at = slice(k * SLOT, (k + 1) * SLOT)
        mean, variance = found[k][:2]
        inverse = lax.rsqrt(variance)
        spread = variance * inverse
        normal.append(gain * ((x[k] - mean) * inverse) + bias)
        spreads.append(spread)
        recon_grad.append(jnp.where(held, grad[k] * spread * over, 0.0))
        mean_ref[at, :] = mean
        inverse_ref[at, :] = inverse
    spectra = stacked_dot(to_wide(normal, windows), ahead_ref[...])
    waves = stacked_dot(to_wide(recon_grad, windows), to_modes_ref[...])
    count = 2 * MODES
    current, before = spectra[:, :count], spectra[:, count:]
    zero = jnp.zeros((SLOT, count), f32)
    after = zero
    if windows > 1:
        current = current + jnp.concatenate([zero, before[:-SLOT]], 0)
        after = jnp.concatenate([waves[SLOT:], zero], 0)
    recon = stacked_dot(current, from_modes_ref[...])
    waves = jnp.concatenate([waves, after], 1)
    waves_ref[...] = waves
    recon = to_blocks(recon, windows)
    row = row[0:8]
    per = blocks // windows
    for b in range(blocks):
        at = slice(b * SLOT, (b + 1) * SLOT)
        mean, variance, run_one, run_two = found[b]
        shifted = (recon[b] - bias) * over
        shifted_ref[at, :] = shifted
        back = shifted * spreads[b] + mean
        back = jnp.where(lane == steps, run_one, jnp.where(lane == steps + 1, run_two, back))
        wave = waves[b // per * SLOT : (b // per + 1) * SLOT]
        slot = (b ^ order_mask(blocks)) * SEND
        send_ref[slot : slot + 8, :] = back[0:8]
        send_ref[slot + 8 : slot + 16, :] = wave[0:8]
        send_ref[slot + 16 : slot + 24, :] = jnp.where(
            row < 2, back[8:16], pltpu.roll(wave[8:16], 2, 0)
        )


def backward_kernel(
    own,
    blocks,
    steps,
    block_ref,
    recv_ref,
    own_ref,
    mean_ref,
    inverse_ref,
    shifted_ref,
    waves_ref,
    ahead_ref,
    lines_ref,
    cot_sum_ref,
    turn_hbm,
    weights_t_hbm,
    earlier_hbm,
    misc_ref,
    starts_ref,
    turn_ref,
    weights_t_ref,
    earlier_ref,
    sems,
):
    ready = fetch(
        [(turn_hbm, turn_ref), (earlier_hbm, earlier_ref), (weights_t_hbm, weights_t_ref)], sems
    )
    windows = blocks * steps // WINDOW
    wide = cot_sum_ref.shape[1]
    count = 2 * MODES
    x, grad = owned(recv_ref, blocks)
    mean, inverse = blocks_of(mean_ref[...]), blocks_of(inverse_ref[...])
    shifted = blocks_of(shifted_ref[...])
    gain, bias, over = own_ref[0:SLOT], own_ref[SLOT : 2 * SLOT], own_ref[2 * SLOT : 3 * SLOT]
    row = lax.broadcasted_iota(jnp.int32, (SLOT, LANES), 0)
    lane = lax.broadcasted_iota(jnp.int32, (SLOT, LANES), 1)
    held = (row < own) & (lane < steps)
    waves = waves_ref[...]
    normal_grad = to_blocks(convolved_back(waves * lines_ref[28:29, 0:LANES], ahead_ref[...]), windows)
    gain_sum = jnp.zeros((SLOT, LANES), f32)
    bias_sum = jnp.zeros((SLOT, LANES), f32)
    normal, ones, twos = [], [], []
    for k in range(blocks):
        over_q = 1.0 / (lane + (k * steps + 1 + WINDOW)).astype(f32)
        centered = (x[k] - mean[k]) * inverse[k]
        normal.append(jnp.where(held, gain * centered + bias, 0.0))
        recon_grad = grad[k] / inverse[k] * over
        gain_sum = gain_sum + normal_grad[k] * centered - recon_grad * shifted[k]
        bias_sum = bias_sum + normal_grad[k] - recon_grad
        first, second, unused = statistics(
            grad[k], shifted[k], normal_grad[k] * gain * inverse[k], centered, mean[k], inverse[k], over_q
        )
        ones.append(jnp.where(held, first, 0.0))
        twos.append(jnp.where(held, second, 0.0))
    gain_sum, bias_sum = jnp.where(held, gain_sum, 0.0), jnp.where(held, bias_sum, 0.0)
    run_one = jnp.zeros((SLOT, LANES), f32)
    run_two = jnp.zeros((SLOT, LANES), f32)
    spots = (lane == row) & (row < own)
    for k in reversed(range(blocks)):
        both = jnp.where(spots, jnp.sum(run_one, 1, keepdims=True), 0.0)
        both = both + pltpu.roll(
            jnp.where(spots, jnp.sum(run_two, 1, keepdims=True), 0.0), SLOT, 1
        )
        starts_ref[k : k + 1, :] = jnp.sum(both, 0, keepdims=True)
        run_one = run_one + ones[k]
        run_two = run_two + twos[k]
    signal = to_wide(normal, windows)
    high, low = split(signal)
    w_high, w_low = split(waves.T)
    pairs = dot(
        jnp.concatenate([w_high, w_high, w_low], 1), jnp.concatenate([high, low, high], 0)
    )
    ready(0)
    cosine, sine = turn_ref[0:MODES], turn_ref[MODES : 2 * MODES]
    cos_b, sin_b = turn_ref[2 * MODES : 3 * MODES], turn_ref[3 * MODES : 4 * MODES]

    def turned(value):
        re, im = value[:MODES], value[MODES:]
        return jnp.concatenate([re * cosine - im * sine, -(re * sine + im * cosine)], 0)

    per = pairs.shape[1] // LANES
    after = turned(pairs[count:])
    left = turned(pairs[:count]) - after
    after = sum(after[:, b * LANES : (b + 1) * LANES] for b in range(per))
    ready(1)
    local, total = scan_lanes(
        jnp.concatenate([left[:, b * LANES : (b + 1) * LANES] for b in range(per)], 0),
        earlier_ref[...],
    )
    run = jnp.broadcast_to(jnp.sum(after, 1, keepdims=True), (count, LANES))
    sums = []
    for b in range(per):
        sums.append(local[b * count : (b + 1) * count] + run)
        run = run + total[b * count : (b + 1) * count]
    sums = jnp.concatenate(sums, 1)
    re, im = sums[:MODES], sums[MODES:]
    crossed = jnp.concatenate([re * cos_b + im * sin_b, im * cos_b - re * sin_b], 0)
    high, low = split(crossed)
    s_high, s_low = split(lines_ref[8:16, 0:count])
    kernel_grad = dot(
        jnp.concatenate([s_high, s_high, s_low], 1), jnp.concatenate([high, low, high], 0)
    )
    k_high, k_low = split(lines_ref[0:8, :])
    overlap = dot_nt(
        jnp.concatenate([k_high, k_high, k_low], 1), jnp.concatenate([high, low, high], 1)
    )
    modes = overlap * lines_ref[16:24, 0:count]
    mix_grad = jnp.sum(overlap * lines_ref[24:32, 0:count], axis=1, keepdims=True)
    ready(2)
    mode_in_grad = stacked_dot(kernel_grad, weights_t_ref[...])
    misc_ref[...] = jnp.zeros_like(misc_ref)
    misc_ref[0:RANK, :] = mode_in_grad[0:RANK, :LANES]
    misc_ref[RANK : 2 * RANK, :] = mode_in_grad[0:RANK, LANES:]
    misc_ref[8 : 8 + RANK, 0:count] = modes[0:RANK]
    misc_ref[8 : 8 + RANK, count : 2 * count] = jnp.broadcast_to(mix_grad, (8, count))[0:RANK]
    mine = own_lanes(block_ref[0] ^ order_mask(blocks), wide, own, blocks)
    at = 12
    gain_row = jnp.sum(
        jnp.where(mine, jnp.sum(gain_sum, 1, keepdims=True), 0.0), axis=0, keepdims=True
    )
    bias_row = jnp.sum(
        jnp.where(mine, jnp.sum(bias_sum, 1, keepdims=True), 0.0), axis=0, keepdims=True
    )
    for value in (gain_row, bias_row, cot_sum_ref[0:1, :]):
        for j in range(wide // LANES):
            misc_ref[at : at + 1, :] = value[:, j * LANES : (j + 1) * LANES]
            at += 1


def convolved_back(waves, ahead):
    rows = waves.shape[0]
    high, low = split(waves)
    out = dot_nt(jnp.concatenate([high, low], 0), ahead[:, :LANES])
    return out[:rows] + out[rows:] + dot_nt(high, ahead[:, LANES:])


def statistics(grad, shifted, scaled, centered, mean, inverse, over_q):
    variance_grad = (grad * shifted - scaled * centered) * (0.5 * inverse)
    first = (grad - scaled - 2.0 * mean * variance_grad) * over_q
    return first, variance_grad * over_q, scaled


def pieces(channels, devices):
    tiles, rest = channels // LANES, channels % LANES
    each = channels // devices
    rest_rows = channels * rest // LANES
    misc_rows = 12 + 3 * (up(channels, LANES) // LANES)
    extra = up(rest_rows + misc_rows, devices) // devices
    return tiles, rest, each, rest_rows, misc_rows, extra


def gathered(recv_ref, kind, own, blocks, dense_ref):
    for i in range(own):
        dense_ref[blocks * i : blocks * (i + 1), :] = recv_ref[
            pl.ds(row_of(i, kind), blocks, stride=SEND), :
        ]


def mix_kernel(
    own,
    devices,
    recv_ref,
    same_ref,
    cot3_ref,
    misc_ref,
    starts_ref,
    send_ref,
    dense_ref,
    misc_all_ref,
):
    channels = same_ref.shape[0]
    blocks = channels // own
    tiles, rest, each, rest_rows, misc_rows, extra = pieces(channels, devices)
    slot = send_ref.shape[0] // devices
    if dense_ref.shape[0] > channels:
        dense_ref[channels:, :] = jnp.zeros((dense_ref.shape[0] - channels, LANES), f32)
    gathered(recv_ref, 0, own, blocks, dense_ref)
    high, low = split(dense_ref[...])
    three = jnp.concatenate([high, low, high], 1)
    chunk = channels if channels <= 512 else devices
    for start in range(0, channels, chunk):
        at = slice(start, start + chunk)
        grad = dot_nt(cot3_ref[at, :], three)
        for j in range(tiles):
            lanes = slice(j * LANES, (j + 1) * LANES)
            tile = grad[:, lanes] * same_ref[at, lanes]
            for i in range(chunk // devices):
                send_ref[pl.ds(j * each + start // devices + i, devices, stride=slot), :] = tile[
                    devices * i : devices * (i + 1)
                ]
        if rest:
            lanes = slice(tiles * LANES, tiles * LANES + LANES)
            last = grad[:, lanes] * same_ref[at, lanes]
            folded = last[0:rest_rows]
            for g in range(1, LANES // rest):
                folded = folded + pltpu.roll(
                    last[g * rest_rows : (g + 1) * rest_rows], g * rest, 1
                )
            misc_all_ref[0:rest_rows, :] = folded
    end = rest_rows + misc_rows
    misc_all_ref[rest_rows:end, :] = misc_ref[0:misc_rows, :]
    if misc_all_ref.shape[0] > end:
        misc_all_ref[end:, :] = jnp.zeros((misc_all_ref.shape[0] - end, LANES), f32)
    for k in range(extra):
        send_ref[pl.ds(tiles * each + k, devices, stride=slot), :] = misc_all_ref[
            devices * k : devices * (k + 1), :
        ]
    for k in range(tiles * each + extra, slot - 1):
        send_ref[pl.ds(k, devices, stride=slot), :] = jnp.zeros((devices, LANES), f32)
    for r in range(2):
        send_ref[pl.ds(r * slot + slot - 1, blocks, stride=2 * slot), :] = starts_ref[...]


def steps_kernel(
    own,
    block_ref,
    recv_ref,
    grad_ref,
    ahead_ref,
    lines_ref,
    columns_ref,
    masked_ref,
    series_hbm,
    cot_hbm,
    earlier_hbm,
    later_hbm,
    out_ref,
    part_ref,
    series_ref,
    cot_ref,
    earlier_ref,
    later_ref,
    dense_ref,
    waves_ref,
    pad_ref,
    sems,
):
    ready = fetch(
        [
            (series_hbm, series_ref),
            (cot_hbm, cot_ref),
            (earlier_hbm, earlier_ref),
            (later_hbm, later_ref),
        ],
        sems,
    )
    channels, steps = series_ref.shape[1:]
    blocks = channels // own
    per = ahead_ref.shape[0] // LANES
    block = block_ref[0]
    gathered(recv_ref, 0, own, blocks, dense_ref)
    gathered(recv_ref, 1, own, blocks, waves_ref)
    pad_ref[...] = jnp.zeros_like(pad_ref)
    gain, bias, shift = (columns_ref[:, k : k + 1] for k in range(3))
    restored = dense_ref[...]
    both = jnp.concatenate(split(restored), 1)
    at = pl.ds(pl.multiple_of(block % per * LANES, LANES), LANES)
    normal_grad = convolved_back(waves_ref[...] * lines_ref[28:29, 0:LANES], ahead_ref[at, :])
    ready(0)
    pad_ref[:, :steps] = series_ref[0]
    chunk = channels if channels <= 512 else 256
    for start in range(0, channels, chunk):
        at = slice(start, start + chunk)
        out = dot(jnp.concatenate([masked_ref[0, at, :], masked_ref[1, at, :]], 0), both)
        mixed = out[:chunk, :LANES] + out[:chunk, LANES:] + out[chunk:, :LANES]
        out_ref[0, at, :] = (pad_ref[at, :] + mixed + shift[at])[:, :steps]
    x = pad_ref[...]
    ready(2)
    local, unused = scan_lanes(jnp.concatenate([x, x * x], 0), earlier_ref[...])
    lane = lax.broadcasted_iota(jnp.int32, (channels, LANES), 1)
    over_q = 1.0 / (lane + (block * steps + 1 + WINDOW)).astype(f32)
    mean = (local[:channels] + restored[:, steps : steps + 1]) * over_q
    variance = (local[channels:] + restored[:, steps + 1 : steps + 2] + WINDOW) * over_q
    inverse = lax.rsqrt(variance - mean * mean + EPSILON)
    centered = (x - mean) * inverse
    first, second, scaled = statistics(
        grad_ref[...],
        (restored - mean) * inverse,
        normal_grad * gain * inverse,
        centered,
        mean,
        inverse,
        over_q,
    )
    held = lane < steps
    ready(3)
    local, unused = scan_lanes(
        jnp.concatenate([jnp.where(held, first, 0.0), jnp.where(held, second, 0.0)], 0),
        later_ref[...],
    )
    part = scaled + local[:channels] + 2.0 * x * local[channels:]
    ready(1)
    part_ref[...] = cot_ref[0] + part[:, :steps]


def sum_kernel(devices, recv_ref, send_ref):
    slot = recv_ref.shape[0] // devices
    total = recv_ref[0:slot, :]
    for s in range(1, devices):
        total = total + recv_ref[s * slot : (s + 1) * slot, :]
    for s in range(devices):
        send_ref[s * slot : (s + 1) * slot, :] = total


def series_kernel(own, devices, core_ref, recv_ref, part_ref, series_hbm, out_ref, series_ref, sems):
    ready = fetch([(series_hbm, series_ref)], sems)
    channels, steps = part_ref.shape
    blocks = channels // own
    slot = recv_ref.shape[0] // devices
    mask = order_mask(blocks)
    first = core_ref[0] == 0
    rows = []
    for s in range(blocks):
        at = (s ^ mask) * 2 * slot + slot - 1
        rows.append(
            jnp.where(first, recv_ref[at : at + 1, :], recv_ref[at + slot : at + slot + 1, :])
        )
    sums = jnp.concatenate(rows, 0)
    ready(0)
    for i in range(own):
        at = slice(blocks * i, blocks * (i + 1))
        out_ref[0, at, :] = part_ref[at, :] + (
            sums[:, i : i + 1] + 2.0 * series_ref[0, at, :] * sums[:, SLOT + i : SLOT + i + 1]
        )


def spread_kernel(
    devices,
    recv_ref,
    endpoint_ref,
    gain_ref,
    bias_ref,
    mode_in_ref,
    mode_out_ref,
    mode_re_ref,
    mode_im_ref,
    mixing_ref,
    out_bias_ref,
    misc_ref,
):
    channels = mixing_ref.shape[0]
    tiles, rest, each, rest_rows, misc_rows, extra = pieces(channels, devices)
    slot = recv_ref.shape[0] // devices
    for j in range(tiles):
        for i in range(each):
            mixing_ref[devices * i : devices * (i + 1), j * LANES : (j + 1) * LANES] = recv_ref[
                pl.ds(j * each + i, devices, stride=slot), :
            ]
    for k in range(extra):
        misc_ref[devices * k : devices * (k + 1), :] = recv_ref[
            pl.ds(tiles * each + k, devices, stride=slot), :
        ]
    if rest:
        folded = misc_ref[0:rest_rows, :]
        for g in range(LANES // rest):
            piece = folded if g == 0 else pltpu.roll(folded, LANES - g * rest, 1)
            mixing_ref[g * rest_rows : (g + 1) * rest_rows, tiles * LANES :] = piece[:, :rest]
    at = rest_rows
    mode_in_ref[:, 0:LANES] = misc_ref[at : at + RANK, :]
    mode_in_ref[:, LANES : 2 * LANES] = misc_ref[at + RANK : at + 2 * RANK, :]
    modes = misc_ref[at + 8 : at + 8 + RANK, :]
    mode_re_ref[...] = modes[:, 0:MODES]
    mode_im_ref[...] = modes[:, MODES : 2 * MODES]
    mode_out_ref[...] = modes[:, 2 * MODES : 2 * MODES + 1] * endpoint_ref[...]
    at += 12
    for ref in (gain_ref, bias_ref, out_bias_ref):
        for start in range(0, channels, LANES):
            size = min(LANES, channels - start)
            ref[:, start : start + size] = misc_ref[at : at + 1, 0:size]
            at += 1


def call(kernel, outs, smem=(), vmem=(), hbm=(), scratch=(), cost=None, limit=None):
    in_vmem = pl.BlockSpec(memory_space=pltpu.VMEM)
    in_smem = pl.BlockSpec(memory_space=pltpu.SMEM)
    in_hbm = pl.BlockSpec(memory_space=pltpu.HBM)
    held = [pltpu.VMEM(a.shape, a.dtype) for a in hbm] + list(scratch)
    if hbm:
        held.append(pltpu.SemaphoreType.DMA((len(hbm),)))
    hbm = [pltpu.with_memory_space_constraint(a, pltpu.HBM) for a in hbm]
    return pl.pallas_call(
        kernel,
        out_shape=tuple(jax.ShapeDtypeStruct(shape, kind) for shape, kind in outs),
        in_specs=[in_smem] * len(smem) + [in_vmem] * len(vmem) + [in_hbm] * len(hbm),
        out_specs=tuple(in_vmem for unused in outs),
        scratch_shapes=held,
        compiler_params=pltpu.CompilerParams(vmem_limit_bytes=limit),
        cost_estimate=cost,
    )(*smem, *vmem, *hbm)


def exchange(value, axis, count, order=None):
    rows = value.shape[0] // count
    out = lax.all_to_all(
        value.reshape(count, rows, value.shape[1]),
        axis,
        split_axis=0,
        concat_axis=0,
        axis_index_groups=order,
    )
    return out.reshape(value.shape)


def body(
    series,
    group_ids,
    rev_gain,
    rev_bias,
    mode_in,
    mode_out,
    mode_re,
    mode_im,
    mixing,
    out_bias,
    cotangent,
):
    samples, channels, steps = series.shape
    blocks = lax.axis_size("seq")
    devices = blocks * lax.axis_size("rep")
    own = channels // blocks
    width = WINDOW // steps * LANES
    padded = up(channels, LANES)
    block = lax.axis_index("seq").astype(jnp.int32).reshape(1)
    core = lax.axis_index("rep").astype(jnp.int32).reshape(1)
    const = {name: jnp.asarray(value) for name, value in constants(steps).items()}
    groups = group_ids.reshape(1, channels)
    order = [[k ^ order_mask(blocks) for k in range(blocks)]]
    limit = (16 if channels <= 512 else 56) * 2**20
    run = functools.partial(call, limit=limit)
    busy = pl.CostEstimate(flops=4_000_000_000, bytes_accessed=8_000_000, transcendentals=0)
    brief = pl.CostEstimate(flops=100_000_000, bytes_accessed=1_000_000, transcendentals=0)

    send, restored_grad = run(
        functools.partial(send_kernel, own),
        [((blocks * SEND, LANES), f32), ((channels, LANES), f32)],
        hbm=(series, cotangent, mixing, groups),
        scratch=[pltpu.VMEM((channels, LANES), f32)],
        cost=brief,
    )
    ahead, lines, mine, columns, masked, same, cot3, cot_sum = run(
        functools.partial(table_kernel, own),
        [
            ((width, 2 * LANES), bf16),
            ((32, width), f32),
            ((3 * SLOT, LANES), f32),
            ((channels, LANES), f32),
            ((2, channels, channels), bf16),
            ((channels, padded), f32),
            ((padded, 3 * LANES), bf16),
            ((8, padded), f32),
        ],
        smem=(block,),
        hbm=(
            cotangent,
            mixing,
            groups,
            rev_gain.reshape(1, channels),
            rev_bias.reshape(1, channels),
            out_bias.reshape(1, channels),
            mode_in.T,
            mode_out.T,
            mode_re,
            mode_im,
            const["weights"],
            const["endpoint"],
            const["turn"],
            const["scale"],
            const["later"],
        ),
        scratch=[pltpu.VMEM((padded, LANES), f32), pltpu.VMEM((LANES, LANES), f32)],
        cost=busy,
    )
    owned_rows = exchange(send, "seq", blocks, order)
    rows = blocks * SLOT
    windows = blocks * steps // WINDOW
    send, mean, inverse, shifted, waves = run(
        functools.partial(forward_kernel, own, blocks, steps),
        [((blocks * SEND, LANES), f32)]
        + [((rows, LANES), f32)] * 3
        + [((windows * SLOT, LANES), f32)],
        vmem=(
            owned_rows,
            mine,
            ahead,
            const["from_modes"],
            const["to_modes"],
            const["earlier"],
        ),
        cost=brief,
    )
    there = exchange(send, "seq", blocks, order)
    tiles, rest, each, rest_rows, misc_rows, extra = pieces(channels, devices)
    slot = up(tiles * each + extra + 1, 8)
    misc, starts = run(
        functools.partial(backward_kernel, own, blocks, steps),
        [((up(misc_rows, 8), LANES), f32), ((blocks, LANES), f32)],
        smem=(block,),
        vmem=(owned_rows, mine, mean, inverse, shifted, waves, ahead, lines, cot_sum),
        hbm=(const["turn"], const["weights_t"], const["earlier"]),
        cost=busy,
    )
    (send,) = run(
        functools.partial(mix_kernel, own, devices),
        [((devices * slot, LANES), f32)],
        vmem=(there, same, cot3, misc, starts),
        scratch=[
            pltpu.VMEM((padded, LANES), f32),
            pltpu.VMEM((up(extra * devices, 8), LANES), f32),
        ],
        cost=brief,
    )
    shares = exchange(send, ("seq", "rep"), devices)
    layer_out, part = run(
        functools.partial(steps_kernel, own),
        [((1, channels, steps), f32), ((channels, steps), f32)],
        smem=(block,),
        vmem=(there, restored_grad, ahead, lines, columns, masked),
        hbm=(series, cotangent, const["earlier"], const["later"]),
        scratch=[pltpu.VMEM((channels, LANES), f32)] * 3,
        cost=busy,
    )
    (send,) = run(
        functools.partial(sum_kernel, devices),
        [((devices * slot, LANES), f32)],
        vmem=(shares,),
        cost=brief,
    )
    sums = exchange(send, ("seq", "rep"), devices)
    (series_grad,) = run(
        functools.partial(series_kernel, own, devices),
        [((1, channels, steps), f32)],
        smem=(core,),
        vmem=(shares, part),
        hbm=(series,),
        cost=busy,
    )
    outs = run(
        functools.partial(spread_kernel, devices),
        [
            ((1, channels), f32),
            ((1, channels), f32),
            ((RANK, ORDER), f32),
            ((RANK, ORDER), f32),
            ((RANK, MODES), f32),
            ((RANK, MODES), f32),
            ((channels, channels), f32),
            ((1, channels), f32),
        ],
        vmem=(sums, const["endpoint"]),
        scratch=[pltpu.VMEM((up(extra * devices, 8), LANES), f32)],
        cost=brief,
    )
    return (
        layer_out,
        series_grad,
        outs[0].reshape(channels),
        outs[1].reshape(channels),
        outs[2].T,
        outs[3].T,
        outs[4],
        outs[5],
        outs[6],
        outs[7].reshape(channels),
    )


def solution(mesh):
    time_split = P("rep", None, "seq")
    in_specs = (time_split,) + (P(),) * 9 + (time_split,)
    out_specs = (time_split, time_split) + (P(),) * 8
    return jax.shard_map(body, mesh=mesh, in_specs=in_specs, out_specs=out_specs, check_vma=False)
```

time: 66.2 us -> 56 us (0.85)
  local copies, waits for them, and re-layouts: 13.9 us -> 0.02 us
  Pallas kernels: 8.38 us -> 15.1 us
  waiting for transfers between devices: 22.3 us -> 16.4 us
  starting transfers between devices: 19.8 us -> 23.2 us
    unnamed x66 -> x8, local copies, waits for them, and re-layouts: 13.9 us -> 0.02 us
    pallas_call x8 -> x9, Pallas kernels: 8.38 us -> 15.1 us  [call(): pl.pallas_call(kernel, out_shape=tuple((jax.ShapeDtypeStruct(shape, kind)...]
    all_to_all x4, waiting for transfers between devices: 21.2 us -> 16.4 us  [exchange(): lax.all_to_all(value.reshape(count, rows, value.shape[1]), axis, split_ax...]
    all_to_all x4, starting transfers between devices: 19.7 us -> 23.2 us  [exchange(): lax.all_to_all(value.reshape(count, rows, value.shape[1]), axis, split_ax...]
    ppermute x1 -> x0, waiting for transfers between devices: 1.11 us -> none  [body(): given = lax.ppermute(given, 'rep', [(0, 1), (1, 0)])]
  transfers between devices with their start and end apart: 5 -> 4, of which waited for: 5 -> 4; matrix products, arithmetic and copies ran while one was open for 0% -> 0% of each run, Pallas kernels for 5% -> 16%
where the time goes in v2:
time: 56 us; the launch traced here: 55.5 us
  starting transfers between devices  23.2 us (41%)
  waiting for transfers between devices  16.4 us (29%)
  Pallas kernels  15.1 us (27%)
  between operations  0.74 us (1%)
    all_to_all x4, starting transfers between devices, exchange(): lax.all_to_all(value.reshape(count, rows, value.shape[1]), axis, split_ax...  23.2 us
    all_to_all x4, waiting for transfers between devices, exchange(): lax.all_to_all(value.reshape(count, rows, value.shape[1]), axis, split_ax...  16.4 us
    pallas_call x9, Pallas kernels, call(): pl.pallas_call(kernel, out_shape=tuple((jax.ShapeDtypeStruct(shape, kind)...  15.1 us
  transfers between devices with their start and end apart: 4, of which 4 were waited for; matrix products, arithmetic and copies ran while one was open for 0% of the time, Pallas kernels for 16%

profile of v2, /device:TPU:0, one launch (start us, length us, event | category | flops | bytes accessed | tf_op | source)
XLA Modules:
  0.0 55.5 jit_solution(7063006776657451237)
XLA Ops:
  0.6 2.1 %shard_map.267 = (f32[384,128]{1,0:T(8,128)}, f32[160,128]{1,0:T(8,128)S(1)}) custom-call(f32[1,160,90]{2,1,0:T(8,128)} %series_hbm.5, f32[1,160,90]{2,1,0:T(8,128)} %cot_hbm.5, f32[160,160]{1,0:T(8,128)} %mixing_hbm.3, s32[1,160]{1,0:T(1,128)} %bitcast.30), custom_call_target="tpu_custom_call" | custom-call | flops 100000000 | bytes 1000000 | tf_op jit(solution)/shard_map/pallas_call | solution.py:841
  2.7 9.3 %all-to-all-start = ((f32[16,24,128]{2,1,0:T(8,128)}), f32[16,24,128]{2,1,0:T(8,128)S(1)}, u32[]{:S(2)}, u32[]{:S(2)}) async-start(f32[16,24,128]{2,1,0:T(8,128)} %bitcast.2), calls=%async_computation | async-start | bytes 393216 | tf_op jit(solution)/shard_map/all_to_all | solution.py:854
  12.0 0.0 copy-start
  12.0 0.0 copy-start.1
  12.1 0.0 copy-start.2
  12.1 2.8 %shard_map.268 = (bf16[1024,256]{1,0:T(8,128)(2,1)S(1)}, f32[32,1024]{1,0:T(8,128)S(1)}, f32[48,128]{1,0:T(8,128)S(1)}, f32[160,128]{1,0:T(8,128)S(1)}, bf16[2,1...) custom-call(s32[1]{0:T(128)} %bitcast.block_ref, ...), custom_call_target="tpu_custom_call" | custom-call | flops 4000000000 | bytes 8000000 | tf_op jit(solution)/shard_map/pallas_call | solution.py:841
  14.8 2.1 %all-to-all-done = f32[16,24,128]{2,1,0:T(8,128)S(1)} async-done(((f32[16,24,128]{2,1,0:T(8,128)}), f32[16,24,128]{2,1,0:T(8,128)S(1)}, u32[]{:S(2)}, u32[]{:S(2)}) %all-to-all-start) | async-done | bytes 196640 | tf_op jit(solution)/shard_map/all_to_all | solution.py:854
  17.0 0.0 copy-done
  17.0 0.0 copy-done.1
  17.0 0.0 copy-done.2
  17.0 1.4 %shard_map.269 = (f32[384,128]{1,0:T(8,128)}, f32[256,128]{1,0:T(8,128)S(1)}, f32[256,128]{1,0:T(8,128)S(1)}, f32[256,128]{1,0:T(8,128)S(1)}, f32[32,128]{1,0:T(8,128)S(1)}) custom-call(f32[384,128]{1,0:T(8,128)S(1)} %bitcast.23, f32[48,128]{1,0:T(8,128)S(1)} %get-tuple-element.38.own_ref, bf16[1024,256]{1,0:T(8,128)(2,1)S(1)} %get-tuple-element.39.ahead_ref, ...), custom_call_target="tpu_custom_call" | custom-call | flops 100000000 | bytes 1000000 | tf_op jit(solution)/shard_map/pallas_call | solution.py:841
  18.4 6.6 %all-to-all-start.1 = ((f32[16,24,128]{2,1,0:T(8,128)}), f32[16,24,128]{2,1,0:T(8,128)S(1)}, u32[]{:S(2)}, u32[]{:S(2)}) async-start(f32[16,24,128]{2,1,0:T(8,128)} %bitcast.9), calls=%async_computation.1 | async-start | bytes 393216 | tf_op jit(solution)/shard_map/all_to_all | solution.py:854
  25.0 2.3 %shard_map.271 = (f32[24,128]{1,0:T(8,128)S(1)}, f32[16,128]{1,0:T(8,128)S(1)}) custom-call(s32[1]{0:T(128)} %bitcast.block_ref, f32[384,128]{1,0:T(8,128)S(1)} %bitcast.24, f32[48,128]{1,0:T(8,128)S(1)} %get-tuple-element.38.own_ref, f32[256,128]{1,0:T(8,128)S(1)} %get-tuple-element.48.mean_ref, f32[256,128]{1,0:T(8,128)S(1)} %get-tuple-element.49.inverse_ref, ...), custom_call_target="tpu_custom_call" | custom-call | flops 4000000000 | bytes 8000000 | tf_op jit(solution)/shard_map/pallas_call | solution.py:841
  27.3 1.9 %all-to-all-done.1 = f32[16,24,128]{2,1,0:T(8,128)S(1)} async-done(((f32[16,24,128]{2,1,0:T(8,128)}), f32[16,24,128]{2,1,0:T(8,128)S(1)}, u32[]{:S(2)}, u32[]{:S(2)}) %all-to-all-start.1) | async-done | bytes 196640 | tf_op jit(solution)/shard_map/all_to_all | solution.py:854
  29.2 1.0 %shard_map.272 = f32[256,128]{1,0:T(8,128)} custom-call(f32[384,128]{1,0:T(8,128)S(1)} %bitcast.21, f32[160,256]{1,0:T(8,128)S(1)} %get-tuple-element.46.same_ref, bf16[256,384]{1,0:T(8,128)(2,1)S(1)} %get-tuple-element.47.cot3_ref, f32[24,128]{1,0:T(8,128)S(1)} %get-tuple-element.53.misc_ref, f32[16,128]{1,0:T(8,128)S(1)} %get-tuple-element.54.starts_ref), custom_call_target="tpu_custom_call" | custom-call | flops 100000000 | bytes 1000000 | tf_op jit(solution)/shard_map/pallas_call | solution.py:841
  30.2 4.8 %all-to-all-start.2 = ((f32[32,8,128]{2,1,0:T(8,128)}), f32[32,8,128]{2,1,0:T(8,128)S(1)}, u32[]{:S(2)}, u32[]{:S(2)}) async-start(f32[32,8,128]{2,1,0:T(8,128)} %bitcast.12), calls=%async_computation.2 | async-start | bytes 262144 | tf_op jit(solution)/shard_map/all_to_all | solution.py:854
  35.0 2.4 %shard_map.270 = (f32[1,160,90]{2,1,0:T(8,128)}, f32[160,90]{1,0:T(8,128)S(1)}) custom-call(s32[1]{0:T(128)} %bitcast.block_ref, f32[384,128]{1,0:T(8,128)S(1)} %bitcast.22, f32[160,128]{1,0:T(8,128)S(1)} %get-tuple-element.41.grad_ref, bf16[1024,256]{1,0:T(8,128)(2,1)S(1)} %get-tuple-element.39.ahead_ref, f32[32,1024]{1,0:T(8,128)S(1)} %get-tuple-element.42.lines_ref, ...), custom_call_target="tpu_custom_call" | custom-call | flops 4000000000 | bytes 8000000 | tf_op jit(solution)/shard_map/pallas_call | solution.py:841
  37.4 5.9 %all-to-all-done.2 = f32[32,8,128]{2,1,0:T(8,128)S(1)} async-done(((f32[32,8,128]{2,1,0:T(8,128)}), f32[32,8,128]{2,1,0:T(8,128)S(1)}, u32[]{:S(2)}, u32[]{:S(2)}) %all-to-all-start.2) | async-done | bytes 131104 | tf_op jit(solution)/shard_map/all_to_all | solution.py:854
  43.2 0.7 %shard_map.274 = f32[256,128]{1,0:T(8,128)} custom-call(f32[256,128]{1,0:T(8,128)S(1)} %bitcast.25), custom_call_target="tpu_custom_call" | custom-call | flops 100000000 | bytes 1000000 | tf_op jit(solution)/shard_map/pallas_call | solution.py:841
  43.9 2.6 %all-to-all-start.3 = ((f32[32,8,128]{2,1,0:T(8,128)}), f32[32,8,128]{2,1,0:T(8,128)S(1)}, u32[]{:S(2)}, u32[]{:S(2)}) async-start(f32[32,8,128]{2,1,0:T(8,128)} %bitcast.14), calls=%async_computation.3 | async-start | bytes 262144 | tf_op jit(solution)/shard_map/all_to_all | solution.py:854
  46.5 1.7 %shard_map.273 = f32[1,160,90]{2,1,0:T(8,128)} custom-call(s32[1]{0:T(128)} %bitcast.11.core_ref, f32[256,128]{1,0:T(8,128)S(1)} %bitcast.26, f32[160,90]{1,0:T(8,128)S(1)} %get-tuple-element.55.part_ref, f32[1,160,90]{2,1,0:T(8,128)} %series_hbm.5), custom_call_target="tpu_custom_call" | custom-call | flops 4000000000 | bytes 8000000 | tf_op jit(solution)/shard_map/pallas_call | solution.py:841
  48.2 0.0 copy-start.3
  48.2 6.5 %all-to-all-done.3 = f32[32,8,128]{2,1,0:T(8,128)S(1)} async-done(((f32[32,8,128]{2,1,0:T(8,128)}), f32[32,8,128]{2,1,0:T(8,128)S(1)}, u32[]{:S(2)}, u32[]{:S(2)}) %all-to-all-start.3) | async-done | bytes 131104 | tf_op jit(solution)/shard_map/all_to_all | solution.py:854
  54.7 0.0 copy-done.3
  54.7 0.8 %shard_map.275 = (f32[1,160]{1,0:T(1,128)}, f32[1,160]{1,0:T(1,128)}, f32[4,256]{1,0:T(4,128)}, f32[4,256]{1,0:T(4,128)}, f32[4,32]{1,0:T(4,128)}, /*index=5*/f3...) custom-call(f32[256,128]{1,0:T(8,128)S(1)} %bitcast.27, f32[1,256]{1,0:T(1,128)S(1)} %copy-done.3), custom_call_target="tpu_custom_call" | custom-call | flops 100000000 | bytes 1000000 | tf_op jit(solution)/shard_map/pallas_call | solution.py:841
Async XLA Ops:
  2.7 14.2 %all-to-all-start = ((f32[16,24,128]{2,1,0:T(8,128)}), f32[16,24,128]{2,1,0:T(8,128)S(1)}, u32[]{:S(2)}, u32[]{:S(2)}) async-start(f32[16,24,128]{2,1,0:T(8,128)} %bitcast.2), calls=%async_computation | async-start | bytes 393216 | tf_op jit(solution)/shard_map/all_to_all | solution.py:854
  12.0 4.9 %copy-start = (bf16[64,2048]{1,0:T(8,128)(2,1)S(1)}, bf16[64,2048]{1,0:T(8,128)(2,1)}, u32[]{:S(2)}) copy-start(bf16[64,2048]{1,0:T(8,128)(2,1)} %constant.32.clone.from_modes_ref) | copy-start | bytes 786436
  12.0 4.9 %copy-start.1 = (bf16[1024,128]{1,0:T(8,128)(2,1)S(1)}, bf16[1024,128]{1,0:T(8,128)(2,1)}, u32[]{:S(2)}) copy-start(bf16[1024,128]{1,0:T(8,128)(2,1)} %constant.31.clone.to_modes_ref) | copy-start | bytes 786436
  12.1 4.9 %copy-start.2 = (bf16[256,256]{1,0:T(8,128)(2,1)S(1)}, bf16[256,256]{1,0:T(8,128)(2,1)}, u32[]{:S(2)}) copy-start(bf16[256,256]{1,0:T(8,128)(2,1)} %constant.33.clone.earlier_ref.earlier_hbm) | copy-start | bytes 393220
  18.4 10.8 %all-to-all-start.1 = ((f32[16,24,128]{2,1,0:T(8,128)}), f32[16,24,128]{2,1,0:T(8,128)S(1)}, u32[]{:S(2)}, u32[]{:S(2)}) async-start(f32[16,24,128]{2,1,0:T(8,128)} %bitcast.9), calls=%async_computation.1 | async-start | bytes 393216 | tf_op jit(solution)/shard_map/all_to_all | solution.py:854
  30.2 13.0 %all-to-all-start.2 = ((f32[32,8,128]{2,1,0:T(8,128)}), f32[32,8,128]{2,1,0:T(8,128)S(1)}, u32[]{:S(2)}, u32[]{:S(2)}) async-start(f32[32,8,128]{2,1,0:T(8,128)} %bitcast.12), calls=%async_computation.2 | async-start | bytes 262144 | tf_op jit(solution)/shard_map/all_to_all | solution.py:854
  43.9 10.8 %all-to-all-start.3 = ((f32[32,8,128]{2,1,0:T(8,128)}), f32[32,8,128]{2,1,0:T(8,128)S(1)}, u32[]{:S(2)}, u32[]{:S(2)}) async-start(f32[32,8,128]{2,1,0:T(8,128)} %bitcast.14), calls=%async_computation.3 | async-start | bytes 262144 | tf_op jit(solution)/shard_map/all_to_all | solution.py:854
  48.2 6.6 %copy-start.3 = (f32[1,256]{1,0:T(1,128)S(1)}, f32[1,256]{1,0:T(1,128)}, u32[]{:S(2)}) copy-start(f32[1,256]{1,0:T(1,128)} %constant.28.clone.endpoint_hbm.endpoint_ref) | copy-start | bytes 3076

commit v3 on v2

--- a/solution.py
+++ b/solution.py
@@ -17,8 +17,10 @@
 EPSILON = 1e-05
 
 LANES = 128
+CORES = 2
 SLOT = 16
-SEND = 24
+SEND = 16
+EXTRA = 36
 f32 = jnp.float32
 bf16 = jnp.bfloat16
 
@@ -112,8 +114,24 @@
     return out[:, :LANES], out[:, LANES:]
 
 
-def row_of(i, kind):
-    return 8 * kind + i if i < 8 else 16 + (i - 8) + 2 * kind
+def unpacked(ref, i, kind, blocks, steps):
+    if i < 8:
+        return ref[pl.ds(8 * kind + i, blocks, stride=SEND), :]
+    lane = lax.broadcasted_iota(jnp.int32, (blocks, LANES), 1)
+    value = None
+    for p in reversed(range(3)):
+        row = ref[pl.ds(8 * kind + 4 * (i - 8) + p, blocks, stride=SEND), :]
+        row = pltpu.roll(row, LANES - steps + EXTRA * p, 1)
+        value = row if value is None else jnp.where(lane < EXTRA * (p + 1), row, value)
+    return value
+
+
+def pack_extra(ref, value, i, kind, blocks, steps):
+    lane = lax.broadcasted_iota(jnp.int32, (blocks, LANES), 1)
+    behind = (lane >= steps) & (lane < steps + EXTRA)
+    for p in range(3):
+        at = pl.ds(8 * kind + 4 * (i - 8) + p, blocks, stride=SEND)
+        ref[at, :] = jnp.where(behind, pltpu.roll(value, steps - EXTRA * p, 1), ref[at, :])
 
 
 def order_mask(blocks):
@@ -193,9 +211,6 @@
         ],
         sems,
     )
-    zero = jnp.zeros((blocks, LANES), f32)
-    for r in range(row_of(own - 1, 1) + 1, SEND):
-        send_ref[pl.ds(r, blocks, stride=SEND), :] = zero
     pad_ref[...] = jnp.zeros_like(pad_ref)
     ready(0, 1, 2)
     pad_ref[:, :steps] = cot_ref[0]
@@ -212,15 +227,18 @@
     grad_ref[...] = total
     ready(3)
     pad_ref[:, :steps] = series_ref[0]
-    for i in range(own):
-        at = slice(blocks * i, blocks * (i + 1))
-        send_ref[pl.ds(row_of(i, 0), blocks, stride=SEND), :] = pad_ref[at, :]
-        send_ref[pl.ds(row_of(i, 1), blocks, stride=SEND), :] = grad_ref[at, :]
+    for kind, ref in enumerate((pad_ref, grad_ref)):
+        for i in range(own):
+            value = ref[blocks * i : blocks * (i + 1), :]
+            if i < 8:
+                send_ref[pl.ds(8 * kind + i, blocks, stride=SEND), :] = value
+            else:
+                pack_extra(send_ref, value, i, kind, blocks, steps)
 
 
 def table_kernel(
     own,
-    block_ref,
+    place_ref,
     cot_hbm,
     mixing_hbm,
     groups_hbm,
@@ -305,7 +323,6 @@
     lines_ref[8 : 8 + RANK, 0:count] = signed * mix
     lines_ref[16 : 16 + RANK, 0:count] = sign * scale * mix
     lines_ref[24 : 24 + RANK, 0:count] = signed
-    lines_ref[28:29, 0:LANES] = scale_ref[...]
     turned_ref[0:RANK, 0:count] = jnp.concatenate([gain_re, gain_im], 1) * mix
     columns = turned_ref[...].T[0:count]
     response = None
@@ -349,13 +366,14 @@
             columns_ref[at, k : k + 1] = jnp.sum(
                 jnp.where(row == lane, ref[...], 0.0), axis=1, keepdims=True
             )
-    mine = own_lanes(block_ref[0] ^ order_mask(blocks), channels, own, blocks)
+    mine = own_lanes(place_ref[0] // CORES ^ order_mask(blocks), channels, own, blocks)
     gain = jnp.sum(jnp.where(mine, gain_ref[...], 0.0), axis=1, keepdims=True)
     gain = jnp.where(lax.broadcasted_iota(jnp.int32, (SLOT, 1), 0) < own, gain, 1.0)
     bias = jnp.sum(jnp.where(mine, bias_ref[...], 0.0), axis=1, keepdims=True)
     own_ref[0:SLOT, :] = jnp.broadcast_to(gain, (SLOT, LANES))
     own_ref[SLOT : 2 * SLOT, :] = jnp.broadcast_to(bias, (SLOT, LANES))
     own_ref[2 * SLOT : 3 * SLOT, :] = jnp.broadcast_to(1.0 / gain, (SLOT, LANES))
+    own_ref[3 * SLOT :, :] = jnp.broadcast_to(scale_ref[...], (8, LANES))
     pad_ref[0:channels, :steps] = cot_ref[0]
     high, low = split(pad_ref[...])
     cot3_ref[...] = jnp.concatenate([high, high, low], 1)
@@ -383,11 +401,19 @@
     return found
 
 
-def owned(recv_ref, blocks):
+def owned(recv_ref, tail_ref, own, blocks, steps):
+    lane = lax.broadcasted_iota(jnp.int32, (blocks, LANES), 1)
+    tail_ref[...] = jnp.zeros_like(tail_ref)
+    for kind in range(2):
+        for i in range(8, own):
+            tail_ref[pl.ds(8 * kind + i - 8, blocks, stride=SLOT), :] = jnp.where(
+                lane < steps, unpacked(recv_ref, i, kind, blocks, steps), 0.0
+            )
     got = recv_ref[...].reshape(blocks, SEND, LANES)
-    tail = pltpu.roll(got[:, 16:24], 6, 1)
-    x = jnp.concatenate([got[:, 0:8], got[:, 16:24]], 1)
-    grad = jnp.concatenate([got[:, 8:16], tail], 1)
+    got = jnp.where(lax.broadcasted_iota(jnp.int32, got.shape, 2) < steps, got, 0.0)
+    tail = tail_ref[...].reshape(blocks, SLOT, LANES)
+    x = jnp.concatenate([got[:, 0:8], tail[:, 0:8]], 1)
+    grad = jnp.concatenate([got[:, 8:16], tail[:, 8:16]], 1)
     mask = order_mask(blocks)
     return [x[b ^ mask] for b in range(blocks)], [grad[b ^ mask] for b in range(blocks)]
 
@@ -405,12 +431,15 @@
     send_ref,
     mean_ref,
     inverse_ref,
+    centered_ref,
     shifted_ref,
+    grad_ref,
+    normal_grad_ref,
     waves_ref,
+    tail_ref,
 ):
     windows = blocks * steps // WINDOW
-    width = ahead_ref.shape[0]
-    x, grad = owned(recv_ref, blocks)
+    x, grad = owned(recv_ref, tail_ref, own, blocks, steps)
     found = normalized(jnp.concatenate(x, 0), blocks, steps, earlier_ref[...])
     gain, bias, over = own_ref[0:SLOT], own_ref[SLOT : 2 * SLOT], own_ref[2 * SLOT : 3 * SLOT]
     row = lax.broadcasted_iota(jnp.int32, (SLOT, LANES), 0)
@@ -422,11 +451,14 @@
         mean, variance = found[k][:2]
         inverse = lax.rsqrt(variance)
         spread = variance * inverse
-        normal.append(gain * ((x[k] - mean) * inverse) + bias)
+        centered = (x[k] - mean) * inverse
+        normal.append(gain * centered + bias)
         spreads.append(spread)
         recon_grad.append(jnp.where(held, grad[k] * spread * over, 0.0))
         mean_ref[at, :] = mean
         inverse_ref[at, :] = inverse
+        centered_ref[at, :] = centered
+        grad_ref[at, :] = grad[k]
     spectra = stacked_dot(to_wide(normal, windows), ahead_ref[...])
     waves = stacked_dot(to_wide(recon_grad, windows), to_modes_ref[...])
     count = 2 * MODES
@@ -440,36 +472,43 @@
     waves = jnp.concatenate([waves, after], 1)
     waves_ref[...] = waves
     recon = to_blocks(recon, windows)
-    row = row[0:8]
-    per = blocks // windows
+    normal_grad = to_blocks(convolved_back(waves * own_ref[3 * SLOT : 3 * SLOT + 1], ahead_ref[...]), windows)
     for b in range(blocks):
         at = slice(b * SLOT, (b + 1) * SLOT)
         mean, variance, run_one, run_two = found[b]
         shifted = (recon[b] - bias) * over
         shifted_ref[at, :] = shifted
+        normal_grad_ref[at, :] = normal_grad[b]
         back = shifted * spreads[b] + mean
-        back = jnp.where(lane == steps, run_one, jnp.where(lane == steps + 1, run_two, back))
-        wave = waves[b // per * SLOT : (b // per + 1) * SLOT]
+        one, two = lane[0:8] == LANES - 2, lane[0:8] == LANES - 1
         slot = (b ^ order_mask(blocks)) * SEND
-        send_ref[slot : slot + 8, :] = back[0:8]
-        send_ref[slot + 8 : slot + 16, :] = wave[0:8]
-        send_ref[slot + 16 : slot + 24, :] = jnp.where(
-            row < 2, back[8:16], pltpu.roll(wave[8:16], 2, 0)
+        send_ref[slot : slot + 8, :] = jnp.where(
+            one, run_one[0:8], jnp.where(two, run_two[0:8], back[0:8])
         )
+        send_ref[slot + 8 : slot + 16, :] = jnp.where(
+            one, run_one[8:16], jnp.where(two, run_two[8:16], normal_grad[b][0:8])
+        )
+        tail_ref[slot : slot + 8, :] = back[8:16]
+        tail_ref[slot + 8 : slot + 16, :] = normal_grad[b][8:16]
+    for kind in range(2):
+        for i in range(8, own):
+            value = tail_ref[pl.ds(8 * kind + i - 8, blocks, stride=SLOT), :]
+            pack_extra(send_ref, value, i, kind, blocks, steps)
 
 
 def backward_kernel(
     own,
     blocks,
     steps,
-    block_ref,
-    recv_ref,
+    place_ref,
     own_ref,
     mean_ref,
     inverse_ref,
+    centered_ref,
     shifted_ref,
+    grad_ref,
+    normal_grad_ref,
     waves_ref,
-    ahead_ref,
     lines_ref,
     cot_sum_ref,
     turn_hbm,
@@ -488,27 +527,39 @@
     windows = blocks * steps // WINDOW
     wide = cot_sum_ref.shape[1]
     count = 2 * MODES
-    x, grad = owned(recv_ref, blocks)
-    mean, inverse = blocks_of(mean_ref[...]), blocks_of(inverse_ref[...])
-    shifted = blocks_of(shifted_ref[...])
+    mean, inverse, centered, shifted, grad, normal_grad = (
+        blocks_of(ref[...])
+        for ref in (
+            mean_ref,
+            inverse_ref,
+            centered_ref,
+            shifted_ref,
+            grad_ref,
+            normal_grad_ref,
+        )
+    )
     gain, bias, over = own_ref[0:SLOT], own_ref[SLOT : 2 * SLOT], own_ref[2 * SLOT : 3 * SLOT]
     row = lax.broadcasted_iota(jnp.int32, (SLOT, LANES), 0)
     lane = lax.broadcasted_iota(jnp.int32, (SLOT, LANES), 1)
     held = (row < own) & (lane < steps)
     waves = waves_ref[...]
-    normal_grad = to_blocks(convolved_back(waves * lines_ref[28:29, 0:LANES], ahead_ref[...]), windows)
     gain_sum = jnp.zeros((SLOT, LANES), f32)
     bias_sum = jnp.zeros((SLOT, LANES), f32)
     normal, ones, twos = [], [], []
     for k in range(blocks):
         over_q = 1.0 / (lane + (k * steps + 1 + WINDOW)).astype(f32)
-        centered = (x[k] - mean[k]) * inverse[k]
-        normal.append(jnp.where(held, gain * centered + bias, 0.0))
+        normal.append(jnp.where(held, gain * centered[k] + bias, 0.0))
         recon_grad = grad[k] / inverse[k] * over
-        gain_sum = gain_sum + normal_grad[k] * centered - recon_grad * shifted[k]
+        gain_sum = gain_sum + normal_grad[k] * centered[k] - recon_grad * shifted[k]
         bias_sum = bias_sum + normal_grad[k] - recon_grad
-        first, second, unused = statistics(
-            grad[k], shifted[k], normal_grad[k] * gain * inverse[k], centered, mean[k], inverse[k], over_q
+        first, second = statistics(
+            grad[k],
+            shifted[k],
+            normal_grad[k] * gain * inverse[k],
+            centered[k],
+            mean[k],
+            inverse[k],
+            over_q,
         )
         ones.append(jnp.where(held, first, 0.0))
         twos.append(jnp.where(held, second, 0.0))
@@ -573,7 +624,7 @@
     misc_ref[RANK : 2 * RANK, :] = mode_in_grad[0:RANK, LANES:]
     misc_ref[8 : 8 + RANK, 0:count] = modes[0:RANK]
     misc_ref[8 : 8 + RANK, count : 2 * count] = jnp.broadcast_to(mix_grad, (8, count))[0:RANK]
-    mine = own_lanes(block_ref[0] ^ order_mask(blocks), wide, own, blocks)
+    mine = own_lanes(place_ref[0] // CORES ^ order_mask(blocks), wide, own, blocks)
     at = 12
     gain_row = jnp.sum(
         jnp.where(mine, jnp.sum(gain_sum, 1, keepdims=True), 0.0), axis=0, keepdims=True
@@ -597,7 +648,7 @@
 def statistics(grad, shifted, scaled, centered, mean, inverse, over_q):
     variance_grad = (grad * shifted - scaled * centered) * (0.5 * inverse)
     first = (grad - scaled - 2.0 * mean * variance_grad) * over_q
-    return first, variance_grad * over_q, scaled
+    return first, variance_grad * over_q
 
 
 def pieces(channels, devices):
@@ -609,16 +660,15 @@
     return tiles, rest, each, rest_rows, misc_rows, extra
 
 
-def gathered(recv_ref, kind, own, blocks, dense_ref):
+def gathered(recv_ref, kind, own, blocks, steps, dense_ref):
     for i in range(own):
-        dense_ref[blocks * i : blocks * (i + 1), :] = recv_ref[
-            pl.ds(row_of(i, kind), blocks, stride=SEND), :
-        ]
+        dense_ref[blocks * i : blocks * (i + 1), :] = unpacked(recv_ref, i, kind, blocks, steps)
 
 
 def mix_kernel(
     own,
     devices,
+    steps,
     recv_ref,
     same_ref,
     cot3_ref,
@@ -634,7 +684,7 @@
     slot = send_ref.shape[0] // devices
     if dense_ref.shape[0] > channels:
         dense_ref[channels:, :] = jnp.zeros((dense_ref.shape[0] - channels, LANES), f32)
-    gathered(recv_ref, 0, own, blocks, dense_ref)
+    gathered(recv_ref, 0, own, blocks, steps, dense_ref)
     high, low = split(dense_ref[...])
     three = jnp.concatenate([high, low, high], 1)
     chunk = channels if channels <= 512 else devices
@@ -673,11 +723,11 @@
 
 def steps_kernel(
     own,
-    block_ref,
+    devices,
+    place_ref,
     recv_ref,
+    shares_ref,
     grad_ref,
-    ahead_ref,
-    lines_ref,
     columns_ref,
     masked_ref,
     series_hbm,
@@ -685,13 +735,14 @@
     earlier_hbm,
     later_hbm,
     out_ref,
-    part_ref,
+    series_grad_ref,
     series_ref,
     cot_ref,
     earlier_ref,
     later_ref,
     dense_ref,
-    waves_ref,
+    back_ref,
+    sums_ref,
     pad_ref,
     sems,
 ):
@@ -706,16 +757,15 @@
     )
     channels, steps = series_ref.shape[1:]
     blocks = channels // own
-    per = ahead_ref.shape[0] // LANES
-    block = block_ref[0]
-    gathered(recv_ref, 0, own, blocks, dense_ref)
-    gathered(recv_ref, 1, own, blocks, waves_ref)
+    block = place_ref[0] // CORES
+    gathered(recv_ref, 0, own, blocks, steps, dense_ref)
+    gathered(recv_ref, 1, own, blocks, steps, back_ref)
+    for i in range(own):
+        sums_ref[blocks * i : blocks * (i + 1), :] = recv_ref[pl.ds(i, blocks, stride=SEND), :]
     pad_ref[...] = jnp.zeros_like(pad_ref)
     gain, bias, shift = (columns_ref[:, k : k + 1] for k in range(3))
     restored = dense_ref[...]
     both = jnp.concatenate(split(restored), 1)
-    at = pl.ds(pl.multiple_of(block % per * LANES, LANES), LANES)
-    normal_grad = convolved_back(waves_ref[...] * lines_ref[28:29, 0:LANES], ahead_ref[at, :])
     ready(0)
     pad_ref[:, :steps] = series_ref[0]
     chunk = channels if channels <= 512 else 256
@@ -729,18 +779,13 @@
     local, unused = scan_lanes(jnp.concatenate([x, x * x], 0), earlier_ref[...])
     lane = lax.broadcasted_iota(jnp.int32, (channels, LANES), 1)
     over_q = 1.0 / (lane + (block * steps + 1 + WINDOW)).astype(f32)
-    mean = (local[:channels] + restored[:, steps : steps + 1]) * over_q
-    variance = (local[channels:] + restored[:, steps + 1 : steps + 2] + WINDOW) * over_q
+    mean = (local[:channels] + sums_ref[:, LANES - 2 : LANES - 1]) * over_q
+    variance = (local[channels:] + sums_ref[:, LANES - 1 : LANES] + WINDOW) * over_q
     inverse = lax.rsqrt(variance - mean * mean + EPSILON)
     centered = (x - mean) * inverse
-    first, second, scaled = statistics(
-        grad_ref[...],
-        (restored - mean) * inverse,
-        normal_grad * gain * inverse,
-        centered,
-        mean,
-        inverse,
-        over_q,
+    scaled = back_ref[...] * gain * inverse
+    first, second = statistics(
+        grad_ref[...], (restored - mean) * inverse, scaled, centered, mean, inverse, over_q
     )
     held = lane < steps
     ready(3)
@@ -748,9 +793,23 @@
         jnp.concatenate([jnp.where(held, first, 0.0), jnp.where(held, second, 0.0)], 0),
         later_ref[...],
     )
+    slot = shares_ref.shape[0] // devices
+    first_core = place_ref[0] % CORES == 0
+    rows = []
+    for s in range(blocks):
+        at = (s ^ order_mask(blocks)) * 2 * slot + slot - 1
+        rows.append(
+            jnp.where(
+                first_core, shares_ref[at : at + 1, :], shares_ref[at + slot : at + slot + 1, :]
+            )
+        )
+    later = jnp.concatenate(rows, 0)
     part = scaled + local[:channels] + 2.0 * x * local[channels:]
     ready(1)
-    part_ref[...] = cot_ref[0] + part[:, :steps]
+    for i in range(own):
+        at = slice(blocks * i, blocks * (i + 1))
+        sums = later[:, i : i + 1] + 2.0 * x[at] * later[:, SLOT + i : SLOT + i + 1]
+        series_grad_ref[0, at, :] = cot_ref[0, at, :] + (part[at] + sums)[:, :steps]
 
 
 def sum_kernel(devices, recv_ref, send_ref):
@@ -760,28 +819,6 @@
         total = total + recv_ref[s * slot : (s + 1) * slot, :]
     for s in range(devices):
         send_ref[s * slot : (s + 1) * slot, :] = total
-
-
-def series_kernel(own, devices, core_ref, recv_ref, part_ref, series_hbm, out_ref, series_ref, sems):
-    ready = fetch([(series_hbm, series_ref)], sems)
-    channels, steps = part_ref.shape
-    blocks = channels // own
-    slot = recv_ref.shape[0] // devices
-    mask = order_mask(blocks)
-    first = core_ref[0] == 0
-    rows = []
-    for s in range(blocks):
-        at = (s ^ mask) * 2 * slot + slot - 1
-        rows.append(
-            jnp.where(first, recv_ref[at : at + 1, :], recv_ref[at + slot : at + slot + 1, :])
-        )
-    sums = jnp.concatenate(rows, 0)
-    ready(0)
-    for i in range(own):
-        at = slice(blocks * i, blocks * (i + 1))
-        out_ref[0, at, :] = part_ref[at, :] + (
-            sums[:, i : i + 1] + 2.0 * series_ref[0, at, :] * sums[:, SLOT + i : SLOT + i + 1]
-        )
 
 
 def spread_kernel(
@@ -880,8 +917,7 @@
     own = channels // blocks
     width = WINDOW // steps * LANES
     padded = up(channels, LANES)
-    block = lax.axis_index("seq").astype(jnp.int32).reshape(1)
-    core = lax.axis_index("rep").astype(jnp.int32).reshape(1)
+    place = lax.axis_index(("seq", "rep")).astype(jnp.int32).reshape(1)
     const = {name: jnp.asarray(value) for name, value in constants(steps).items()}
     groups = group_ids.reshape(1, channels)
     order = [[k ^ order_mask(blocks) for k in range(blocks)]]
@@ -902,14 +938,14 @@
         [
             ((width, 2 * LANES), bf16),
             ((32, width), f32),
-            ((3 * SLOT, LANES), f32),
+            ((3 * SLOT + 8, LANES), f32),
             ((channels, LANES), f32),
             ((2, channels, channels), bf16),
             ((channels, padded), f32),
             ((padded, 3 * LANES), bf16),
             ((8, padded), f32),
         ],
-        smem=(block,),
+        smem=(place,),
         hbm=(
             cotangent,
             mixing,
@@ -933,10 +969,10 @@
     owned_rows = exchange(send, "seq", blocks, order)
     rows = blocks * SLOT
     windows = blocks * steps // WINDOW
-    send, mean, inverse, shifted, waves = run(
+    send, *kept = run(
         functools.partial(forward_kernel, own, blocks, steps),
         [((blocks * SEND, LANES), f32)]
-        + [((rows, LANES), f32)] * 3
+        + [((rows, LANES), f32)] * 6
         + [((windows * SLOT, LANES), f32)],
         vmem=(
             owned_rows,
@@ -946,6 +982,7 @@
             const["to_modes"],
             const["earlier"],
         ),
+        scratch=[pltpu.VMEM((rows, LANES), f32)],
         cost=brief,
     )
     there = exchange(send, "seq", blocks, order)
@@ -954,13 +991,13 @@
     misc, starts = run(
         functools.partial(backward_kernel, own, blocks, steps),
         [((up(misc_rows, 8), LANES), f32), ((blocks, LANES), f32)],
-        smem=(block,),
-        vmem=(owned_rows, mine, mean, inverse, shifted, waves, ahead, lines, cot_sum),
+        smem=(place,),
+        vmem=(mine, *kept, lines, cot_sum),
         hbm=(const["turn"], const["weights_t"], const["earlier"]),
         cost=busy,
     )
     (send,) = run(
-        functools.partial(mix_kernel, own, devices),
+        functools.partial(mix_kernel, own, devices, steps),
         [((devices * slot, LANES), f32)],
         vmem=(there, same, cot3, misc, starts),
         scratch=[
@@ -970,15 +1007,6 @@
         cost=brief,
     )
     shares = exchange(send, ("seq", "rep"), devices)
-    layer_out, part = run(
-        functools.partial(steps_kernel, own),
-        [((1, channels, steps), f32), ((channels, steps), f32)],
-        smem=(block,),
-        vmem=(there, restored_grad, ahead, lines, columns, masked),
-        hbm=(series, cotangent, const["earlier"], const["later"]),
-        scratch=[pltpu.VMEM((channels, LANES), f32)] * 3,
-        cost=busy,
-    )
     (send,) = run(
         functools.partial(sum_kernel, devices),
         [((devices * slot, LANES), f32)],
@@ -986,12 +1014,13 @@
         cost=brief,
     )
     sums = exchange(send, ("seq", "rep"), devices)
-    (series_grad,) = run(
-        functools.partial(series_kernel, own, devices),
-        [((1, channels, steps), f32)],
-        smem=(core,),
-        vmem=(shares, part),
-        hbm=(series,),
+    layer_out, series_grad = run(
+        functools.partial(steps_kernel, own, devices),
+        [((1, channels, steps), f32), ((1, channels, steps), f32)],
+        smem=(place,),
+        vmem=(there, shares, restored_grad, columns, masked),
+        hbm=(series, cotangent, const["earlier"], const["later"]),
+        scratch=[pltpu.VMEM((channels, LANES), f32)] * 4,
         cost=busy,
     )
     outs = run(

time: 56 us -> 54.1 us (0.966)
  blocking collectives: 0 us -> 12.8 us
  waiting for transfers between devices: 16.4 us -> 7.59 us
  starting transfers between devices: 23.2 us -> 18.6 us
  Pallas kernels: 15.1 us -> 14 us
    all_to_all x0 -> x1, blocking collectives: none -> 12.8 us  [exchange(): lax.all_to_all(value.reshape(count, rows, value.shape[1]), axis, split_ax...]
    all_to_all x4 -> x3, waiting for transfers between devices: 16.4 us -> 7.59 us  [exchange(): lax.all_to_all(value.reshape(count, rows, value.shape[1]), axis, split_ax...]
    all_to_all x4 -> x3, starting transfers between devices: 23.2 us -> 18.6 us  [exchange(): lax.all_to_all(value.reshape(count, rows, value.shape[1]), axis, split_ax...]
    pallas_call x9 -> x8, Pallas kernels: 15.1 us -> 14 us  [call(): pl.pallas_call(kernel, out_shape=tuple((jax.ShapeDtypeStruct(shape, kind)...]
  transfers between devices with their start and end apart: 4 -> 3, of which waited for: 4 -> 3; matrix products, arithmetic and copies ran while one was open for 0% -> 0% of each run, Pallas kernels for 16% -> 15%
where the time goes in v3:
time: 54.1 us; the launch traced here: 53.6 us
  starting transfers between devices  18.6 us (34%)
  Pallas kernels  14 us (26%)
  blocking collectives  12.8 us (24%)
  waiting for transfers between devices  7.59 us (14%)
  between operations  0.72 us (1%)
    all_to_all x3, starting transfers between devices, exchange(): lax.all_to_all(value.reshape(count, rows, value.shape[1]), axis, split_ax...  18.6 us
    pallas_call x8, Pallas kernels, call(): pl.pallas_call(kernel, out_shape=tuple((jax.ShapeDtypeStruct(shape, kind)...  14 us
    all_to_all x1, blocking collectives, exchange(): lax.all_to_all(value.reshape(count, rows, value.shape[1]), axis, split_ax...  12.8 us
    all_to_all x3, waiting for transfers between devices, exchange(): lax.all_to_all(value.reshape(count, rows, value.shape[1]), axis, split_ax...  7.59 us
  transfers between devices with their start and end apart: 3, of which 3 were waited for; matrix products, arithmetic and copies ran while one was open for 0% of the time, Pallas kernels for 15%

profile of v3, /device:TPU:0, one launch (start us, length us, event | category | flops | bytes accessed | tf_op | source)
XLA Modules:
  0.0 53.6 jit_solution(6443443012546117325)
XLA Ops:
  0.6 2.1 %shard_map.267 = (f32[256,128]{1,0:T(8,128)}, f32[160,128]{1,0:T(8,128)S(1)}) custom-call(f32[1,160,90]{2,1,0:T(8,128)} %series_hbm.3, f32[1,160,90]{2,1,0:T(8,128)} %cot_hbm.5, f32[160,160]{1,0:T(8,128)} %mixing_hbm.3, s32[1,160]{1,0:T(1,128)} %bitcast.29), custom_call_target="tpu_custom_call" | custom-call | flops 100000000 | bytes 1000000 | tf_op jit(solution)/shard_map/pallas_call | solution.py:878
  2.8 9.3 %all-to-all-start = ((f32[16,16,128]{2,1,0:T(8,128)}), f32[16,16,128]{2,1,0:T(8,128)S(1)}, u32[]{:S(2)}, u32[]{:S(2)}) async-start(f32[16,16,128]{2,1,0:T(8,128)} %bitcast.2), calls=%async_computation | async-start | bytes 262144 | tf_op jit(solution)/shard_map/all_to_all | solution.py:891
  12.1 0.0 copy-start
  12.1 0.0 copy-start.1
  12.1 0.0 copy-start.2
  12.1 2.8 %shard_map.268 = (bf16[1024,256]{1,0:T(8,128)(2,1)S(1)}, f32[32,1024]{1,0:T(8,128)S(1)}, f32[56,128]{1,0:T(8,128)S(1)}, f32[160,128]{1,0:T(8,128)S(1)}, bf16[2,1...) custom-call(s32[1]{0:T(128)} %bitcast.place_ref, ...), custom_call_target="tpu_custom_call" | custom-call | flops 4000000000 | bytes 8000000 | tf_op jit(solution)/shard_map/pallas_call | solution.py:878
  14.9 1.0 %all-to-all-done = f32[16,16,128]{2,1,0:T(8,128)S(1)} async-done(((f32[16,16,128]{2,1,0:T(8,128)}), f32[16,16,128]{2,1,0:T(8,128)S(1)}, u32[]{:S(2)}, u32[]{:S(2)}) %all-to-all-start) | async-done | bytes 131104 | tf_op jit(solution)/shard_map/all_to_all | solution.py:891
  15.9 0.0 copy-done
  15.9 0.0 copy-done.1
  15.9 0.0 copy-done.2
  15.9 1.8 %shard_map.269 = (f32[256,128]{1,0:T(8,128)}, f32[256,128]{1,0:T(8,128)S(1)}, f32[256,128]{1,0:T(8,128)S(1)}, f32[256,128]{1,0:T(8,128)S(1)}, f32[256,128]{1,0:T...) custom-call(f32[256,128]{1,0:T(8,128)S(1)} %bitcast.23, ...), custom_call_target="tpu_custom_call" | custom-call | flops 100000000 | bytes 1000000 | tf_op jit(solution)/shard_map/pallas_call | solution.py:878
  17.7 6.7 %all-to-all-start.1 = ((f32[16,16,128]{2,1,0:T(8,128)}), f32[16,16,128]{2,1,0:T(8,128)S(1)}, u32[]{:S(2)}, u32[]{:S(2)}) async-start(f32[16,16,128]{2,1,0:T(8,128)} %bitcast.9), calls=%async_computation.1 | async-start | bytes 262144 | tf_op jit(solution)/shard_map/all_to_all | solution.py:891
  24.4 3.1 %shard_map.270 = (f32[24,128]{1,0:T(8,128)S(1)}, f32[16,128]{1,0:T(8,128)S(1)}) custom-call(s32[1]{0:T(128)} %bitcast.place_ref, f32[56,128]{1,0:T(8,128)S(1)} %get-tuple-element.41.own_ref, f32[256,128]{1,0:T(8,128)S(1)} %get-tuple-element.46.mean_ref, f32[256,128]{1,0:T(8,128)S(1)} %get-tuple-element.47.inverse_ref, ...), custom_call_target="tpu_custom_call" | custom-call | flops 4000000000 | bytes 8000000 | tf_op jit(solution)/shard_map/pallas_call | solution.py:878
  27.5 0.8 %all-to-all-done.1 = f32[16,16,128]{2,1,0:T(8,128)S(1)} async-done(((f32[16,16,128]{2,1,0:T(8,128)}), f32[16,16,128]{2,1,0:T(8,128)S(1)}, u32[]{:S(2)}, u32[]{:S(2)}) %all-to-all-start.1) | async-done | bytes 131104 | tf_op jit(solution)/shard_map/all_to_all | solution.py:891
  28.2 0.3 shard_map.271
  28.6 12.8 %all_to_all.20 = f32[32,8,128]{2,1,0:T(8,128)S(1)} all-to-all(f32[32,8,128]{2,1,0:T(8,128)S(1)} %bitcast.22), channel_id=1, replica_groups=mesh['seq'=16,'rep'=2] {'seq','rep'}, dimensions={0} | all-to-all | bytes 262144 | tf_op jit(solution)/shard_map/all_to_all | solution.py:891
  41.4 0.7 %shard_map.273 = f32[256,128]{1,0:T(8,128)} custom-call(f32[256,128]{1,0:T(8,128)S(1)} %bitcast.25), custom_call_target="tpu_custom_call" | custom-call | flops 100000000 | bytes 1000000 | tf_op jit(solution)/shard_map/pallas_call | solution.py:878
  42.1 2.6 %all-to-all-start.3 = ((f32[32,8,128]{2,1,0:T(8,128)}), f32[32,8,128]{2,1,0:T(8,128)S(1)}, u32[]{:S(2)}, u32[]{:S(2)}) async-start(f32[32,8,128]{2,1,0:T(8,128)} %bitcast.13), calls=%async_computation.3 | async-start | bytes 262144 | tf_op jit(solution)/shard_map/all_to_all | solution.py:891
  44.6 2.4 %shard_map.272 = (f32[1,160,90]{2,1,0:T(8,128)}, f32[1,160,90]{2,1,0:T(8,128)}) custom-call(s32[1]{0:T(128)} %bitcast.place_ref, f32[256,128]{1,0:T(8,128)S(1)} %bitcast.21, f32[256,128]{1,0:T(8,128)S(1)} %bitcast.26, f32[160,128]{1,0:T(8,128)S(1)} %get-tuple-element.57.grad_ref, f32[160,128]{1,0:T(8,128)S(1)} %get-tuple-element.58.columns_ref, ...), custom_call_target="tpu_custom_call" | custom-call | flops 4000000000 | bytes 8000000 | tf_op jit(solution)/shard_map/pallas_call | solution.py:878
  47.1 0.0 copy-start.3
  47.1 5.8 %all-to-all-done.3 = f32[32,8,128]{2,1,0:T(8,128)S(1)} async-done(((f32[32,8,128]{2,1,0:T(8,128)}), f32[32,8,128]{2,1,0:T(8,128)S(1)}, u32[]{:S(2)}, u32[]{:S(2)}) %all-to-all-start.3) | async-done | bytes 131104 | tf_op jit(solution)/shard_map/all_to_all | solution.py:891
  52.9 0.0 copy-done.3
  52.9 0.8 %shard_map.274 = (f32[1,160]{1,0:T(1,128)}, f32[1,160]{1,0:T(1,128)}, f32[4,256]{1,0:T(4,128)}, f32[4,256]{1,0:T(4,128)}, f32[4,32]{1,0:T(4,128)}, /*index=5*/f3...) custom-call(f32[256,128]{1,0:T(8,128)S(1)} %bitcast.24, f32[1,256]{1,0:T(1,128)S(1)} %copy-done.3), custom_call_target="tpu_custom_call" | custom-call | flops 100000000 | bytes 1000000 | tf_op jit(solution)/shard_map/pallas_call | solution.py:878
Async XLA Ops:
  2.8 13.2 %all-to-all-start = ((f32[16,16,128]{2,1,0:T(8,128)}), f32[16,16,128]{2,1,0:T(8,128)S(1)}, u32[]{:S(2)}, u32[]{:S(2)}) async-start(f32[16,16,128]{2,1,0:T(8,128)} %bitcast.2), calls=%async_computation | async-start | bytes 262144 | tf_op jit(solution)/shard_map/all_to_all | solution.py:891
  12.1 3.9 %copy-start = (bf16[64,2048]{1,0:T(8,128)(2,1)S(1)}, bf16[64,2048]{1,0:T(8,128)(2,1)}, u32[]{:S(2)}) copy-start(bf16[64,2048]{1,0:T(8,128)(2,1)} %constant.34.clone.from_modes_ref) | copy-start | bytes 786436
  12.1 3.9 %copy-start.1 = (bf16[1024,128]{1,0:T(8,128)(2,1)S(1)}, bf16[1024,128]{1,0:T(8,128)(2,1)}, u32[]{:S(2)}) copy-start(bf16[1024,128]{1,0:T(8,128)(2,1)} %constant.33.clone.to_modes_ref) | copy-start | bytes 786436
  12.1 3.8 %copy-start.2 = (bf16[256,256]{1,0:T(8,128)(2,1)S(1)}, bf16[256,256]{1,0:T(8,128)(2,1)}, u32[]{:S(2)}) copy-start(bf16[256,256]{1,0:T(8,128)(2,1)} %constant.35.clone.earlier_ref.earlier_hbm) | copy-start | bytes 393220
  17.7 10.5 %all-to-all-start.1 = ((f32[16,16,128]{2,1,0:T(8,128)}), f32[16,16,128]{2,1,0:T(8,128)S(1)}, u32[]{:S(2)}, u32[]{:S(2)}) async-start(f32[16,16,128]{2,1,0:T(8,128)} %bitcast.9), calls=%async_computation.1 | async-start | bytes 262144 | tf_op jit(solution)/shard_map/all_to_all | solution.py:891
  42.1 10.8 %all-to-all-start.3 = ((f32[32,8,128]{2,1,0:T(8,128)}), f32[32,8,128]{2,1,0:T(8,128)S(1)}, u32[]{:S(2)}, u32[]{:S(2)}) async-start(f32[32,8,128]{2,1,0:T(8,128)} %bitcast.13), calls=%async_computation.3 | async-start | bytes 262144 | tf_op jit(solution)/shard_map/all_to_all | solution.py:891
  47.1 5.8 %copy-start.3 = (f32[1,256]{1,0:T(1,128)S(1)}, f32[1,256]{1,0:T(1,128)}, u32[]{:S(2)}) copy-start(f32[1,256]{1,0:T(1,128)} %constant.30.clone.endpoint_hbm.endpoint_ref) | copy-start | bytes 3076

commit v4 on v3

--- a/solution.py
+++ b/solution.py
@@ -18,8 +18,9 @@
 
 LANES = 128
 CORES = 2
-SLOT = 16
-SEND = 16
+HALVES = 2
+SLOT = 24
+KIND = 16
 EXTRA = 36
 f32 = jnp.float32
 bf16 = jnp.bfloat16
@@ -62,7 +63,7 @@
     flipped = in_blocks(weights[:, ::-1], steps)
     high, low = halves(flipped)
     table = {}
-    table["weights"] = np.concatenate([high, low], 1)
+    table["weights"] = flipped.astype(np.float32)
     table["weights_t"] = np.concatenate([high.T, low.T], 1)
     table["endpoint"] = legendre[:, 0][None, :].astype(np.float32)
     mode = np.arange(MODES)[:, None]
@@ -114,28 +115,62 @@
     return out[:, :LANES], out[:, LANES:]
 
 
-def unpacked(ref, i, kind, blocks, steps):
-    if i < 8:
-        return ref[pl.ds(8 * kind + i, blocks, stride=SEND), :]
-    lane = lax.broadcasted_iota(jnp.int32, (blocks, LANES), 1)
+def scan_lanes_exactly(value, table):
+    high, low = split(value)
+    last = (value - high.astype(f32) - low.astype(f32)).astype(bf16)
+    out = dot(jnp.concatenate([high, low], 1), table) + dot(last, table[:LANES])
+    return out[:, :LANES], out[:, LANES:]
+
+
+def unpacked(ref, i, kind, count, steps):
+    rows = ref.shape[0] // count
+    if i < KIND:
+        return ref[pl.ds(KIND * kind + i, count, stride=rows), :]
+    lane = lax.broadcasted_iota(jnp.int32, (count, LANES), 1)
     value = None
     for p in reversed(range(3)):
-        row = ref[pl.ds(8 * kind + 4 * (i - 8) + p, blocks, stride=SEND), :]
+        row = ref[pl.ds(KIND * kind + 4 * (i - KIND) + p, count, stride=rows), :]
         row = pltpu.roll(row, LANES - steps + EXTRA * p, 1)
         value = row if value is None else jnp.where(lane < EXTRA * (p + 1), row, value)
     return value
 
 
-def pack_extra(ref, value, i, kind, blocks, steps):
-    lane = lax.broadcasted_iota(jnp.int32, (blocks, LANES), 1)
+def pack_extra(ref, value, i, kind, rows, steps):
+    count = value.shape[0]
+    lane = lax.broadcasted_iota(jnp.int32, (count, LANES), 1)
     behind = (lane >= steps) & (lane < steps + EXTRA)
     for p in range(3):
-        at = pl.ds(8 * kind + 4 * (i - 8) + p, blocks, stride=SEND)
+        at = pl.ds(KIND * kind + 4 * (i - KIND) + p, count, stride=rows)
         ref[at, :] = jnp.where(behind, pltpu.roll(value, steps - EXTRA * p, 1), ref[at, :])
 
 
-def order_mask(blocks):
-    return blocks * 11 // 16
+def owner_order(half):
+    return [k ^ 1 for k in range(half)]
+
+
+def owner_orders(blocks):
+    half = blocks // HALVES
+    return [[h * half + k for k in owner_order(half)] for h in range(HALVES)]
+
+
+def first_order(blocks):
+    return sum(owner_orders(blocks)[::-1], [])
+
+
+def share_order(devices):
+    sharing = devices // HALVES
+    if sharing == 16:
+        return [15, 1, 12, 14, 8, 4, 7, 3, 2, 11, 5, 6, 10, 0, 9, 13]
+    return [int(k) for k in np.random.default_rng(0).permutation(sharing)]
+
+
+def places(place_ref, blocks):
+    block, core = place_ref[0] // CORES, place_ref[0] % CORES
+    half = blocks // HALVES
+    place = jnp.int32(0)
+    for k, member in enumerate(owner_order(half)):
+        place = jnp.where(block % half == member, k, place)
+    return block, core, block // half, place
 
 
 def to_wide(blocks, windows):
@@ -201,7 +236,7 @@
     sems,
 ):
     channels, steps = cot_ref.shape[1:]
-    blocks = channels // own
+    sets = channels // own
     ready = fetch(
         [
             (groups_hbm, groups_ref),
@@ -211,9 +246,11 @@
         ],
         sems,
     )
+    rows = 2 * KIND
     pad_ref[...] = jnp.zeros_like(pad_ref)
-    ready(0, 1, 2)
+    ready(2)
     pad_ref[:, :steps] = cot_ref[0]
+    ready(0, 1)
     chunk = channels if channels <= 512 else 256
     total = None
     for start in range(0, channels, chunk):
@@ -224,16 +261,24 @@
         out = dot(jnp.concatenate([high, low], 0), both)
         part = out[:channels, :LANES] + out[:channels, LANES:] + out[channels:, :LANES]
         total = part if total is None else total + part
+    spot = lax.broadcasted_iota(jnp.int32, (channels, LANES), 1) == LANES - 2
+    sums = jnp.sum(pad_ref[...], axis=1, keepdims=True)
     grad_ref[...] = total
     ready(3)
     pad_ref[:, :steps] = series_ref[0]
+    pad_ref[...] = jnp.where(spot, sums, pad_ref[...])
     for kind, ref in enumerate((pad_ref, grad_ref)):
         for i in range(own):
-            value = ref[blocks * i : blocks * (i + 1), :]
-            if i < 8:
-                send_ref[pl.ds(8 * kind + i, blocks, stride=SEND), :] = value
+            value = ref[sets * i : sets * (i + 1), :]
+            if kind and i < own - KIND:
+                there = sets * (KIND + i)
+                value = jnp.where(spot[:sets], sums[there : there + sets], value)
+            if i < KIND:
+                send_ref[pl.ds(KIND * kind + i, sets, stride=rows), :] = value
             else:
-                pack_extra(send_ref, value, i, kind, blocks, steps)
+                pack_extra(send_ref, value, i, kind, rows, steps)
+    for half in range(1, HALVES):
+        send_ref[half * sets * rows : (half + 1) * sets * rows, :] = send_ref[0 : sets * rows, :]
 
 
 def table_kernel(
@@ -260,8 +305,8 @@
     columns_ref,
     masked_ref,
     same_ref,
-    cot3_ref,
-    cot_sum_ref,
+    cot_pad_ref,
+    cot_send_ref,
     cot_ref,
     mixing_ref,
     groups_ref,
@@ -277,7 +322,6 @@
     turn_ref,
     scale_ref,
     later_ref,
-    pad_ref,
     turned_ref,
     sems,
 ):
@@ -304,15 +348,19 @@
     channels, steps = cot_ref.shape[1:]
     width = ahead_ref.shape[0]
     per = width // LANES
-    blocks = channels // own
+    sets = channels // own
     count = 2 * MODES
     lines_ref[...] = jnp.zeros_like(lines_ref)
     turned_ref[...] = jnp.zeros_like(turned_ref)
-    pad_ref[...] = jnp.zeros_like(pad_ref)
+    cot_pad_ref[...] = jnp.zeros_like(cot_pad_ref)
     ready(0, 1, 2, 3)
-    high, low = split(mode_in_ref[...])
-    out = dot(jnp.concatenate([high, low], 0), weights_ref[...])
-    kernel = out[:RANK, :width] + out[:RANK, width:] + out[RANK:, :width]
+    kernel = lax.dot_general(
+        mode_in_ref[...],
+        weights_ref[...],
+        (((1,), (0,)), ((), ())),
+        precision=lax.Precision.HIGHEST,
+        preferred_element_type=f32,
+    )
     lines_ref[0:RANK, :] = kernel
     mix = jnp.sum(mode_out_ref[...] * endpoint_ref[...], axis=1, keepdims=True)
     ready(4, 5, 6)
@@ -335,7 +383,7 @@
     cos_b, sin_b = turn_ref[2 * MODES : 3 * MODES], turn_ref[3 * MODES : 4 * MODES]
     turned = jnp.concatenate([real * cos_b + imag * sin_b, imag * cos_b - real * sin_b], 0)
     rows = jnp.concatenate([turned[:, b * LANES : (b + 1) * LANES] for b in range(per)], 0)
-    local, total = scan_lanes(rows, later_ref[...])
+    local, total = scan_lanes_exactly(rows, later_ref[...])
     run = jnp.zeros((count, LANES), f32)
     suffix = [None] * per
     for b in reversed(range(per)):
@@ -366,7 +414,8 @@
             columns_ref[at, k : k + 1] = jnp.sum(
                 jnp.where(row == lane, ref[...], 0.0), axis=1, keepdims=True
             )
-    mine = own_lanes(place_ref[0] // CORES ^ order_mask(blocks), channels, own, blocks)
+    unused, unused, unused, place = places(place_ref, sets * HALVES)
+    mine = own_lanes(place, channels, own, sets)
     gain = jnp.sum(jnp.where(mine, gain_ref[...], 0.0), axis=1, keepdims=True)
     gain = jnp.where(lax.broadcasted_iota(jnp.int32, (SLOT, 1), 0) < own, gain, 1.0)
     bias = jnp.sum(jnp.where(mine, bias_ref[...], 0.0), axis=1, keepdims=True)
@@ -374,12 +423,15 @@
     own_ref[SLOT : 2 * SLOT, :] = jnp.broadcast_to(bias, (SLOT, LANES))
     own_ref[2 * SLOT : 3 * SLOT, :] = jnp.broadcast_to(1.0 / gain, (SLOT, LANES))
     own_ref[3 * SLOT :, :] = jnp.broadcast_to(scale_ref[...], (8, LANES))
-    pad_ref[0:channels, :steps] = cot_ref[0]
-    high, low = split(pad_ref[...])
-    cot3_ref[...] = jnp.concatenate([high, high, low], 1)
-    cot_sum_ref[...] = dot_nt(
-        jnp.ones((8, 2 * LANES), bf16), jnp.concatenate([high, low], 1)
-    )
+    cot_pad_ref[:, :steps] = cot_ref[0]
+    most = cot_send_ref.shape[0]
+    lane = lax.broadcasted_iota(jnp.int32, (channels - most, LANES), 1)
+    behind = (lane >= steps) & (lane < steps + EXTRA)
+    cot_send_ref[...] = cot_pad_ref[0:most, :]
+    for p in range(3):
+        at = pl.ds(p, channels - most, stride=3)
+        moved = pltpu.roll(cot_pad_ref[most:, :], steps - EXTRA * p, 1)
+        cot_send_ref[at, :] = jnp.where(behind, moved, cot_send_ref[at, :])
 
 
 def normalized(x, blocks, steps, earlier):
@@ -405,23 +457,25 @@
     lane = lax.broadcasted_iota(jnp.int32, (blocks, LANES), 1)
     tail_ref[...] = jnp.zeros_like(tail_ref)
     for kind in range(2):
-        for i in range(8, own):
-            tail_ref[pl.ds(8 * kind + i - 8, blocks, stride=SLOT), :] = jnp.where(
+        for i in range(KIND, own):
+            tail_ref[pl.ds(8 * kind + i - KIND, blocks, stride=16), :] = jnp.where(
                 lane < steps, unpacked(recv_ref, i, kind, blocks, steps), 0.0
             )
-    got = recv_ref[...].reshape(blocks, SEND, LANES)
+    got = recv_ref[...].reshape(blocks, 2 * KIND, LANES)
     got = jnp.where(lax.broadcasted_iota(jnp.int32, got.shape, 2) < steps, got, 0.0)
-    tail = tail_ref[...].reshape(blocks, SLOT, LANES)
-    x = jnp.concatenate([got[:, 0:8], tail[:, 0:8]], 1)
-    grad = jnp.concatenate([got[:, 8:16], tail[:, 8:16]], 1)
-    mask = order_mask(blocks)
-    return [x[b ^ mask] for b in range(blocks)], [grad[b ^ mask] for b in range(blocks)]
+    tail = tail_ref[...].reshape(blocks, 16, LANES)
+    x = jnp.concatenate([got[:, 0:KIND], tail[:, 0:8]], 1)
+    grad = jnp.concatenate([got[:, KIND : 2 * KIND], tail[:, 8:16]], 1)
+    order = first_order(blocks)
+    slots = [order.index(b) for b in range(blocks)]
+    return [x[k] for k in slots], [grad[k] for k in slots]
 
 
 def forward_kernel(
     own,
     blocks,
     steps,
+    place_ref,
     recv_ref,
     own_ref,
     ahead_ref,
@@ -437,6 +491,7 @@
     normal_grad_ref,
     waves_ref,
     tail_ref,
+    back_tail_ref,
 ):
     windows = blocks * steps // WINDOW
     x, grad = owned(recv_ref, tail_ref, own, blocks, steps)
@@ -473,34 +528,48 @@
     waves_ref[...] = waves
     recon = to_blocks(recon, windows)
     normal_grad = to_blocks(convolved_back(waves * own_ref[3 * SLOT : 3 * SLOT + 1], ahead_ref[...]), windows)
+    backs = []
     for b in range(blocks):
         at = slice(b * SLOT, (b + 1) * SLOT)
-        mean, variance, run_one, run_two = found[b]
         shifted = (recon[b] - bias) * over
         shifted_ref[at, :] = shifted
         normal_grad_ref[at, :] = normal_grad[b]
-        back = shifted * spreads[b] + mean
-        one, two = lane[0:8] == LANES - 2, lane[0:8] == LANES - 1
-        slot = (b ^ order_mask(blocks)) * SEND
-        send_ref[slot : slot + 8, :] = jnp.where(
-            one, run_one[0:8], jnp.where(two, run_two[0:8], back[0:8])
-        )
-        send_ref[slot + 8 : slot + 16, :] = jnp.where(
-            one, run_one[8:16], jnp.where(two, run_two[8:16], normal_grad[b][0:8])
-        )
-        tail_ref[slot : slot + 8, :] = back[8:16]
-        tail_ref[slot + 8 : slot + 16, :] = normal_grad[b][8:16]
-    for kind in range(2):
-        for i in range(8, own):
-            value = tail_ref[pl.ds(8 * kind + i - 8, blocks, stride=SLOT), :]
-            pack_extra(send_ref, value, i, kind, blocks, steps)
+        backs.append(shifted * spreads[b] + found[b][0])
+    unused, unused, half, unused = places(place_ref, blocks)
+    first = half == 0
+    sets = blocks // HALVES
+    count = 3 * KIND
+    one, two = lane == LANES - 2, lane == LANES - 1
+    for k, b in enumerate(owner_orders(blocks)[0]):
+        c = b + sets
+        arrays = [
+            jnp.where(first, backs[b], backs[c]),
+            jnp.where(first, backs[c], backs[b]),
+            jnp.where(first, normal_grad[b], normal_grad[c]),
+        ]
+        run_one = jnp.where(first, found[b][2], found[c][2])
+        run_two = jnp.where(first, found[b][3], found[c][3])
+        arrays[0] = jnp.where(one, run_one, jnp.where(two, run_two, arrays[0]))
+        send_ref[k * count : k * count + KIND, :] = arrays[0][:KIND]
+        tail = jnp.where(one[:8], run_one[KIND:], jnp.where(two[:8], run_two[KIND:], arrays[1][:8]))
+        send_ref[k * count + KIND : k * count + KIND + 8, :] = tail
+        send_ref[k * count + KIND + 8 : k * count + 2 * KIND, :] = arrays[1][8:KIND]
+        send_ref[k * count + 2 * KIND : k * count + 3 * KIND, :] = arrays[2][:KIND]
+        for kind in range(3):
+            back_tail_ref[(3 * k + kind) * 8 : (3 * k + kind + 1) * 8, :] = arrays[kind][KIND:]
+    for kind in range(3):
+        for i in range(KIND, own):
+            value = back_tail_ref[pl.ds(8 * kind + i - KIND, sets, stride=24), :]
+            pack_extra(send_ref, value, i, kind, count, steps)
 
 
 def backward_kernel(
     own,
     blocks,
     steps,
+    wide,
     place_ref,
+    recv_ref,
     own_ref,
     mean_ref,
     inverse_ref,
@@ -510,7 +579,6 @@
     normal_grad_ref,
     waves_ref,
     lines_ref,
-    cot_sum_ref,
     turn_hbm,
     weights_t_hbm,
     earlier_hbm,
@@ -525,7 +593,6 @@
         [(turn_hbm, turn_ref), (earlier_hbm, earlier_ref), (weights_t_hbm, weights_t_ref)], sems
     )
     windows = blocks * steps // WINDOW
-    wide = cot_sum_ref.shape[1]
     count = 2 * MODES
     mean, inverse, centered, shifted, grad, normal_grad = (
         blocks_of(ref[...])
@@ -564,17 +631,23 @@
         ones.append(jnp.where(held, first, 0.0))
         twos.append(jnp.where(held, second, 0.0))
     gain_sum, bias_sum = jnp.where(held, gain_sum, 0.0), jnp.where(held, bias_sum, 0.0)
+    ready(1)
+    high, low = split(jnp.concatenate(ones + twos, 0))
+    total = blocks_of(dot(jnp.concatenate([high, low], 1), earlier_ref[:, LANES:]))
     run_one = jnp.zeros((SLOT, LANES), f32)
     run_two = jnp.zeros((SLOT, LANES), f32)
-    spots = (lane == row) & (row < own)
+    unused, unused, half, place = places(place_ref, blocks)
+    first = half == 0
+    sets = blocks // HALVES
+    starts = [None] * blocks
     for k in reversed(range(blocks)):
-        both = jnp.where(spots, jnp.sum(run_one, 1, keepdims=True), 0.0)
-        both = both + pltpu.roll(
-            jnp.where(spots, jnp.sum(run_two, 1, keepdims=True), 0.0), SLOT, 1
-        )
-        starts_ref[k : k + 1, :] = jnp.sum(both, 0, keepdims=True)
-        run_one = run_one + ones[k]
-        run_two = run_two + twos[k]
+        both = jnp.where(lane == row, run_one, jnp.where(lane == row + 32, run_two, 0.0))
+        starts[k] = jnp.sum(both, 0, keepdims=True)
+        run_one = run_one + total[k]
+        run_two = run_two + total[blocks + k]
+    for at, device in enumerate(share_order(blocks * CORES)):
+        k = device // CORES
+        starts_ref[at : at + 1, :] = jnp.where(first, starts[k], starts[k + sets])
     signal = to_wide(normal, windows)
     high, low = split(signal)
     w_high, w_low = split(waves.T)
@@ -593,7 +666,6 @@
     after = turned(pairs[count:])
     left = turned(pairs[:count]) - after
     after = sum(after[:, b * LANES : (b + 1) * LANES] for b in range(per))
-    ready(1)
     local, total = scan_lanes(
         jnp.concatenate([left[:, b * LANES : (b + 1) * LANES] for b in range(per)], 0),
         earlier_ref[...],
@@ -624,7 +696,7 @@
     misc_ref[RANK : 2 * RANK, :] = mode_in_grad[0:RANK, LANES:]
     misc_ref[8 : 8 + RANK, 0:count] = modes[0:RANK]
     misc_ref[8 : 8 + RANK, count : 2 * count] = jnp.broadcast_to(mix_grad, (8, count))[0:RANK]
-    mine = own_lanes(place_ref[0] // CORES ^ order_mask(blocks), wide, own, blocks)
+    mine = own_lanes(place, wide, own, sets)
     at = 12
     gain_row = jnp.sum(
         jnp.where(mine, jnp.sum(gain_sum, 1, keepdims=True), 0.0), axis=0, keepdims=True
@@ -632,7 +704,11 @@
     bias_row = jnp.sum(
         jnp.where(mine, jnp.sum(bias_sum, 1, keepdims=True), 0.0), axis=0, keepdims=True
     )
-    for value in (gain_row, bias_row, cot_sum_ref[0:1, :]):
+    cot_sum = jnp.sum(recv_ref[...].reshape(blocks, 2 * KIND, LANES), axis=0)[:SLOT]
+    cot_row = jnp.sum(
+        jnp.where(mine, cot_sum[:, LANES - 2 : LANES - 1], 0.0), axis=0, keepdims=True
+    )
+    for value in (gain_row, bias_row, cot_row):
         for j in range(wide // LANES):
             misc_ref[at : at + 1, :] = value[:, j * LANES : (j + 1) * LANES]
             at += 1
@@ -660,9 +736,10 @@
     return tiles, rest, each, rest_rows, misc_rows, extra
 
 
-def gathered(recv_ref, kind, own, blocks, steps, dense_ref):
+def gathered(recv_ref, kind, own, steps, dense_ref):
+    sets = recv_ref.shape[0] // (3 * KIND)
     for i in range(own):
-        dense_ref[blocks * i : blocks * (i + 1), :] = unpacked(recv_ref, i, kind, blocks, steps)
+        dense_ref[sets * i : sets * (i + 1), :] = unpacked(recv_ref, i, kind, sets, steps)
 
 
 def mix_kernel(
@@ -671,26 +748,47 @@
     steps,
     recv_ref,
     same_ref,
-    cot3_ref,
+    cot_ref,
+    cot_partner_ref,
     misc_ref,
     starts_ref,
     send_ref,
     dense_ref,
+    partner_ref,
+    cot_all_ref,
     misc_all_ref,
 ):
     channels = same_ref.shape[0]
-    blocks = channels // own
     tiles, rest, each, rest_rows, misc_rows, extra = pieces(channels, devices)
     slot = send_ref.shape[0] // devices
-    if dense_ref.shape[0] > channels:
-        dense_ref[channels:, :] = jnp.zeros((dense_ref.shape[0] - channels, LANES), f32)
-    gathered(recv_ref, 0, own, blocks, steps, dense_ref)
-    high, low = split(dense_ref[...])
-    three = jnp.concatenate([high, low, high], 1)
+    most = cot_partner_ref.shape[0]
+    cot = cot_partner_ref[...]
+    cot_all_ref[0:most, :] = jnp.where(
+        lax.broadcasted_iota(jnp.int32, cot.shape, 1) < steps, cot, 0.0
+    )
+    lane = lax.broadcasted_iota(jnp.int32, (channels - most, LANES), 1)
+    cot = jnp.zeros((channels - most, LANES), f32)
+    for p in reversed(range(3)):
+        row = cot_partner_ref[pl.ds(p, channels - most, stride=3), :]
+        row = pltpu.roll(row, LANES - steps + EXTRA * p, 1)
+        cot = jnp.where(lane < min(EXTRA * (p + 1), steps), row, cot)
+    cot_all_ref[most:, :] = cot
+    three = []
+    for kind, ref in enumerate((dense_ref, partner_ref)):
+        if ref.shape[0] > channels:
+            ref[channels:, :] = jnp.zeros((ref.shape[0] - channels, LANES), f32)
+        gathered(recv_ref, kind, own, steps, ref)
+        high, low = split(ref[...])
+        three += [high, low, high]
+    three = jnp.concatenate(three, 1)
     chunk = channels if channels <= 512 else devices
     for start in range(0, channels, chunk):
         at = slice(start, start + chunk)
-        grad = dot_nt(cot3_ref[at, :], three)
+        six = []
+        for ref in (cot_ref, cot_all_ref):
+            high, low = split(ref[at, :])
+            six += [high, high, low]
+        grad = dot_nt(jnp.concatenate(six, 1), three)
         for j in range(tiles):
             lanes = slice(j * LANES, (j + 1) * LANES)
             tile = grad[:, lanes] * same_ref[at, lanes]
@@ -717,8 +815,7 @@
         ]
     for k in range(tiles * each + extra, slot - 1):
         send_ref[pl.ds(k, devices, stride=slot), :] = jnp.zeros((devices, LANES), f32)
-    for r in range(2):
-        send_ref[pl.ds(r * slot + slot - 1, blocks, stride=2 * slot), :] = starts_ref[...]
+    send_ref[pl.ds(slot - 1, devices, stride=slot), :] = starts_ref[...]
 
 
 def steps_kernel(
@@ -756,12 +853,12 @@
         sems,
     )
     channels, steps = series_ref.shape[1:]
-    blocks = channels // own
-    block = place_ref[0] // CORES
-    gathered(recv_ref, 0, own, blocks, steps, dense_ref)
-    gathered(recv_ref, 1, own, blocks, steps, back_ref)
+    sets = channels // own
+    block, core, unused, unused = places(place_ref, sets * HALVES)
+    gathered(recv_ref, 0, own, steps, dense_ref)
+    gathered(recv_ref, 2, own, steps, back_ref)
     for i in range(own):
-        sums_ref[blocks * i : blocks * (i + 1), :] = recv_ref[pl.ds(i, blocks, stride=SEND), :]
+        sums_ref[sets * i : sets * (i + 1), :] = recv_ref[pl.ds(i, sets, stride=3 * KIND), :]
     pad_ref[...] = jnp.zeros_like(pad_ref)
     gain, bias, shift = (columns_ref[:, k : k + 1] for k in range(3))
     restored = dense_ref[...]
@@ -794,21 +891,19 @@
         later_ref[...],
     )
     slot = shares_ref.shape[0] // devices
-    first_core = place_ref[0] % CORES == 0
     rows = []
-    for s in range(blocks):
-        at = (s ^ order_mask(blocks)) * 2 * slot + slot - 1
+    order = share_order(devices * HALVES)
+    for owner in owner_orders(sets * HALVES)[0]:
+        even, odd = (order.index(owner * CORES + r) * slot + slot - 1 for r in range(CORES))
         rows.append(
-            jnp.where(
-                first_core, shares_ref[at : at + 1, :], shares_ref[at + slot : at + slot + 1, :]
-            )
+            jnp.where(core == 0, shares_ref[even : even + 1, :], shares_ref[odd : odd + 1, :])
         )
     later = jnp.concatenate(rows, 0)
     part = scaled + local[:channels] + 2.0 * x * local[channels:]
     ready(1)
     for i in range(own):
-        at = slice(blocks * i, blocks * (i + 1))
-        sums = later[:, i : i + 1] + 2.0 * x[at] * later[:, SLOT + i : SLOT + i + 1]
+        at = slice(sets * i, sets * (i + 1))
+        sums = later[:, i : i + 1] + 2.0 * x[at] * later[:, 32 + i : 33 + i]
         series_grad_ref[0, at, :] = cot_ref[0, at, :] + (part[at] + sums)[:, :steps]
 
 
@@ -886,14 +981,14 @@
     )(*smem, *vmem, *hbm)
 
 
-def exchange(value, axis, count, order=None):
-    rows = value.shape[0] // count
+def exchange(value, axis, orders):
+    count = len(orders[0])
     out = lax.all_to_all(
-        value.reshape(count, rows, value.shape[1]),
+        value.reshape(count, value.shape[0] // count, value.shape[1]),
         axis,
         split_axis=0,
         concat_axis=0,
-        axis_index_groups=order,
+        axis_index_groups=orders,
     )
     return out.reshape(value.shape)
 
@@ -913,14 +1008,18 @@
 ):
     samples, channels, steps = series.shape
     blocks = lax.axis_size("seq")
+    sets = blocks // HALVES
     devices = blocks * lax.axis_size("rep")
-    own = channels // blocks
+    sharing = devices // HALVES
+    own = channels // sets
     width = WINDOW // steps * LANES
     padded = up(channels, LANES)
     place = lax.axis_index(("seq", "rep")).astype(jnp.int32).reshape(1)
+    halves_of = owner_orders(blocks)
+    all_of = [first_order(blocks)]
+    shares_of = [[h * sharing + k for k in share_order(devices)] for h in range(HALVES)]
     const = {name: jnp.asarray(value) for name, value in constants(steps).items()}
     groups = group_ids.reshape(1, channels)
-    order = [[k ^ order_mask(blocks) for k in range(blocks)]]
     limit = (16 if channels <= 512 else 56) * 2**20
     run = functools.partial(call, limit=limit)
     busy = pl.CostEstimate(flops=4_000_000_000, bytes_accessed=8_000_000, transcendentals=0)
@@ -928,12 +1027,12 @@
 
     send, restored_grad = run(
         functools.partial(send_kernel, own),
-        [((blocks * SEND, LANES), f32), ((channels, LANES), f32)],
+        [((blocks * 2 * KIND, LANES), f32), ((channels, LANES), f32)],
         hbm=(series, cotangent, mixing, groups),
         scratch=[pltpu.VMEM((channels, LANES), f32)],
         cost=brief,
     )
-    ahead, lines, mine, columns, masked, same, cot3, cot_sum = run(
+    ahead, lines, mine, columns, masked, same, cot, cot_send = run(
         functools.partial(table_kernel, own),
         [
             ((width, 2 * LANES), bf16),
@@ -942,8 +1041,8 @@
             ((channels, LANES), f32),
             ((2, channels, channels), bf16),
             ((channels, padded), f32),
-            ((padded, 3 * LANES), bf16),
-            ((8, padded), f32),
+            ((channels, LANES), f32),
+            ((channels * 3 // 4, LANES), f32),
         ],
         smem=(place,),
         hbm=(
@@ -963,17 +1062,18 @@
             const["scale"],
             const["later"],
         ),
-        scratch=[pltpu.VMEM((padded, LANES), f32), pltpu.VMEM((LANES, LANES), f32)],
+        scratch=[pltpu.VMEM((LANES, LANES), f32)],
         cost=busy,
     )
-    owned_rows = exchange(send, "seq", blocks, order)
+    owned_rows = exchange(send, "seq", all_of)
     rows = blocks * SLOT
     windows = blocks * steps // WINDOW
     send, *kept = run(
         functools.partial(forward_kernel, own, blocks, steps),
-        [((blocks * SEND, LANES), f32)]
+        [((sets * 3 * KIND, LANES), f32)]
         + [((rows, LANES), f32)] * 6
         + [((windows * SLOT, LANES), f32)],
+        smem=(place,),
         vmem=(
             owned_rows,
             mine,
@@ -982,40 +1082,47 @@
             const["to_modes"],
             const["earlier"],
         ),
-        scratch=[pltpu.VMEM((rows, LANES), f32)],
+        scratch=[pltpu.VMEM((blocks * 16, LANES), f32), pltpu.VMEM((sets * 24, LANES), f32)],
         cost=brief,
     )
-    there = exchange(send, "seq", blocks, order)
-    tiles, rest, each, rest_rows, misc_rows, extra = pieces(channels, devices)
+    there = exchange(send, "seq", halves_of)
+    cot_send, kept[0] = lax.optimization_barrier((cot_send, kept[0]))
+    cot_partner = lax.ppermute(cot_send, "seq", [(k, (k + sets) % blocks) for k in range(blocks)])
+    tiles, rest, each, rest_rows, misc_rows, extra = pieces(channels, sharing)
     slot = up(tiles * each + extra + 1, 8)
     misc, starts = run(
-        functools.partial(backward_kernel, own, blocks, steps),
-        [((up(misc_rows, 8), LANES), f32), ((blocks, LANES), f32)],
+        functools.partial(backward_kernel, own, blocks, steps, padded),
+        [
+            ((up(misc_rows, 8), LANES), f32),
+            ((sharing, LANES), f32),
+        ],
         smem=(place,),
-        vmem=(mine, *kept, lines, cot_sum),
+        vmem=(owned_rows, mine, *kept, lines),
         hbm=(const["turn"], const["weights_t"], const["earlier"]),
         cost=busy,
     )
     (send,) = run(
-        functools.partial(mix_kernel, own, devices, steps),
-        [((devices * slot, LANES), f32)],
-        vmem=(there, same, cot3, misc, starts),
+        functools.partial(mix_kernel, own, sharing, steps),
+        [((sharing * slot, LANES), f32)],
+        vmem=(there, same, cot, cot_partner, misc, starts),
         scratch=[
             pltpu.VMEM((padded, LANES), f32),
-            pltpu.VMEM((up(extra * devices, 8), LANES), f32),
+            pltpu.VMEM((padded, LANES), f32),
+            pltpu.VMEM((channels, LANES), f32),
+            pltpu.VMEM((up(extra * sharing, 8), LANES), f32),
         ],
         cost=brief,
     )
-    shares = exchange(send, ("seq", "rep"), devices)
+    shares = exchange(send, ("seq", "rep"), shares_of)
     (send,) = run(
-        functools.partial(sum_kernel, devices),
-        [((devices * slot, LANES), f32)],
+        functools.partial(sum_kernel, sharing),
+        [((sharing * slot, LANES), f32)],
         vmem=(shares,),
         cost=brief,
     )
-    sums = exchange(send, ("seq", "rep"), devices)
+    sums = exchange(send, ("seq", "rep"), shares_of)
     layer_out, series_grad = run(
-        functools.partial(steps_kernel, own, devices),
+        functools.partial(steps_kernel, own, sharing),
         [((1, channels, steps), f32), ((1, channels, steps), f32)],
         smem=(place,),
         vmem=(there, shares, restored_grad, columns, masked),
@@ -1024,7 +1131,7 @@
         cost=busy,
     )
     outs = run(
-        functools.partial(spread_kernel, devices),
+        functools.partial(spread_kernel, sharing),
         [
             ((1, channels), f32),
             ((1, channels), f32),
@@ -1036,7 +1143,7 @@
             ((1, channels), f32),
         ],
         vmem=(sums, const["endpoint"]),
-        scratch=[pltpu.VMEM((up(extra * devices, 8), LANES), f32)],
+        scratch=[pltpu.VMEM((up(extra * sharing, 8), LANES), f32)],
         cost=brief,
     )
     return (

time: 54.1 us -> 49.4 us (0.913)
  blocking collectives: 12.8 us -> 7.79 us
  starting transfers between devices: 18.6 us -> 20.8 us
  waiting for transfers between devices: 7.59 us -> 5.45 us
    all_to_all x1, blocking collectives: 12.8 us -> 7.79 us  [exchange(): lax.all_to_all(value.reshape(count, value.shape[0] // count, value.shape[...]
    all_to_all x3, waiting for transfers between devices: 7.59 us -> 4.5 us  [exchange(): lax.all_to_all(value.reshape(count, value.shape[0] // count, value.shape[...]
    ppermute x0 -> x1, starting transfers between devices: none -> 1.61 us  [body(): lax.ppermute(cot_send, 'seq', [(k, (k + sets) % blocks) for k in range(bl...]
    ppermute x0 -> x1, waiting for transfers between devices: none -> 0.95 us  [body(): lax.ppermute(cot_send, 'seq', [(k, (k + sets) % blocks) for k in range(bl...]
    all_to_all x3, starting transfers between devices: 18.6 us -> 19.2 us  [exchange(): lax.all_to_all(value.reshape(count, value.shape[0] // count, value.shape[...]
  transfers between devices with their start and end apart: 3 -> 4, of which waited for: 3 -> 3; matrix products, arithmetic and copies ran while one was open for 0% -> 0% of each run, Pallas kernels for 15% -> 16%
where the time goes in v4:
time: 49.4 us; the launch traced here: 48.9 us
  starting transfers between devices  20.8 us (42%)
  Pallas kernels  14.1 us (29%)
  blocking collectives  7.79 us (16%)
  waiting for transfers between devices  5.45 us (11%)
  between operations  0.72 us (1%)
    all_to_all x3, starting transfers between devices, exchange(): lax.all_to_all(value.reshape(count, value.shape[0] // count, value.shape[...  19.2 us
    pallas_call x8, Pallas kernels, call(): pl.pallas_call(kernel, out_shape=tuple((jax.ShapeDtypeStruct(shape, kind)...  14.1 us
    all_to_all x1, blocking collectives, exchange(): lax.all_to_all(value.reshape(count, value.shape[0] // count, value.shape[...  7.79 us
    all_to_all x3, waiting for transfers between devices, exchange(): lax.all_to_all(value.reshape(count, value.shape[0] // count, value.shape[...  4.5 us
    ppermute x1, starting transfers between devices, body(): lax.ppermute(cot_send, 'seq', [(k, (k + sets) % blocks) for k in range(bl...  1.61 us
  transfers between devices with their start and end apart: 4, of which 3 were waited for; matrix products, arithmetic and copies ran while one was open for 0% of the time, Pallas kernels for 16%

profile of v4, /device:TPU:0, one launch (start us, length us, event | category | flops | bytes accessed | tf_op | source)
XLA Modules:
  0.0 48.9 jit_solution(1534516334897812682)
XLA Ops:
  0.6 2.3 %shard_map.267 = (f32[512,128]{1,0:T(8,128)}, f32[160,128]{1,0:T(8,128)S(1)}) custom-call(f32[1,160,90]{2,1,0:T(8,128)} %series_hbm.3, f32[1,160,90]{2,1,0:T(8,128)} %cot_hbm.5, f32[160,160]{1,0:T(8,128)} %mixing_hbm.3, s32[1,160]{1,0:T(1,128)} %bitcast.30), custom_call_target="tpu_custom_call" | custom-call | flops 100000000 | bytes 1000000 | tf_op jit(solution)/shard_map/pallas_call | solution.py:973
  2.9 8.8 %all-to-all-start = ((f32[16,32,128]{2,1,0:T(8,128)}), f32[16,32,128]{2,1,0:T(8,128)S(1)}, u32[]{:S(2)}, u32[]{:S(2)}) async-start(f32[16,32,128]{2,1,0:T(8,128)} %bitcast.2), calls=%async_computation | async-start | bytes 524288 | tf_op jit(solution)/shard_map/all_to_all | solution.py:986
  11.7 0.0 copy-start
  11.7 0.0 copy-start.1
  11.8 0.0 copy-start.2
  11.8 3.1 %shard_map.268 = (bf16[1024,256]{1,0:T(8,128)(2,1)S(1)}, f32[32,1024]{1,0:T(8,128)S(1)}, f32[80,128]{1,0:T(8,128)S(1)}, f32[160,128]{1,0:T(8,128)S(1)}, bf16[2,1...) custom-call(s32[1]{0:T(128)} %bitcast.place_ref, ...), custom_call_target="tpu_custom_call" | custom-call | flops 4000000000 | bytes 8000000 | tf_op jit(solution)/shard_map/pallas_call | solution.py:973
  14.8 3.8 %all-to-all-done = f32[16,32,128]{2,1,0:T(8,128)S(1)} async-done(((f32[16,32,128]{2,1,0:T(8,128)}), f32[16,32,128]{2,1,0:T(8,128)S(1)}, u32[]{:S(2)}, u32[]{:S(2)}) %all-to-all-start) | async-done | bytes 262176 | tf_op jit(solution)/shard_map/all_to_all | solution.py:986
  18.6 0.0 copy-done
  18.6 0.0 copy-done.1
  18.6 0.0 copy-done.2
  18.6 1.9 %shard_map.269 = (f32[384,128]{1,0:T(8,128)}, f32[384,128]{1,0:T(8,128)S(1)}, f32[384,128]{1,0:T(8,128)S(1)}, f32[384,128]{1,0:T(8,128)S(1)}, f32[384,128]{1,0:T...) custom-call(s32[1]{0:T(128)} %bitcast.place_ref, f32[512,128]{1,0:T(8,128)S(1)} %bitcast.20, ...), custom_call_target="tpu_custom_call" | custom-call | flops 100000000 | bytes 1000000 | tf_op jit(solution)/shard_map/pallas_call | solution.py:973
  20.6 4.6 %all-to-all-start.1 = ((f32[8,48,128]{2,1,0:T(8,128)}), f32[8,48,128]{2,1,0:T(8,128)S(1)}, u32[]{:S(2)}, u32[]{:S(2)}) async-start(f32[8,48,128]{2,1,0:T(8,128)} %bitcast.9), calls=%async_computation.1 | async-start | bytes 393216 | tf_op jit(solution)/shard_map/all_to_all | solution.py:986
  25.1 1.6 %collective-permute-start = (f32[120,128]{1,0:T(8,128)S(1)}, f32[120,128]{1,0:T(8,128)S(1)}, u32[]{:S(2)}, u32[]{:S(2)}) collective-permute-start(f32[120,128]{1,0:T(8,128)S(1)} %get-tuple-element.50), channel_id=1, source_target_pairs={{0,16},{2,18},{4,20},{6,22},{8,24},{10,26},{12,28},{14,30},{16,0},... | collective-permute-start | bytes 184328 | tf_op jit(solution)/shard_map/ppermute | solution.py:1090
  26.7 2.6 %shard_map.270 = (f32[24,128]{1,0:T(8,128)S(1)}, f32[16,128]{1,0:T(8,128)S(1)}) custom-call(s32[1]{0:T(128)} %bitcast.place_ref, f32[512,128]{1,0:T(8,128)S(1)} %bitcast.21, f32[80,128]{1,0:T(8,128)S(1)} %get-tuple-element.43.own_ref, f32[384,128]{1,0:T(8,128)S(1)} %get-tuple-element.51.mean_ref, f32[384,128]{1,0:T(8,128)S(1)} %get-tuple-element.52.inverse_ref, ...), custom_call_target="tpu_custom_call" | custom-call | flops 4000000000 | bytes 8000000 | tf_op jit(solution)/shard_map/pallas_call | solution.py:973
  29.3 0.9 %collective-permute-done.cot_partner_ref = f32[120,128]{1,0:T(8,128)S(1)} collective-permute-done((f32[120,128]{1,0:T(8,128)S(1)}, f32[120,128]{1,0:T(8,128)S(1)}, u32[]{:S(2)}, u32[]{:S(2)}) %collective-permute-start) | collective-permute-done | bytes 61472 | tf_op jit(solution)/shard_map/ppermute | solution.py:1090
  30.2 0.0 all-to-all-done.1
  30.2 0.4 shard_map.271
  30.6 7.8 %all_to_all.20 = f32[16,16,128]{2,1,0:T(8,128)S(1)} all-to-all(f32[16,16,128]{2,1,0:T(8,128)S(1)} %bitcast.24), channel_id=1, replica_groups={{15,1,12,14,8,4,7,3,2,11,5,6,10,0,9,13},{31,17,28,30,24,20,23,19,18,27,..., dimensions={0} | all-to-all | bytes 262144 | tf_op jit(solution)/shard_map/all_to_all | solution.py:986
  38.4 0.7 %shard_map.273 = f32[256,128]{1,0:T(8,128)} custom-call(f32[256,128]{1,0:T(8,128)S(1)} %bitcast.26), custom_call_target="tpu_custom_call" | custom-call | flops 100000000 | bytes 1000000 | tf_op jit(solution)/shard_map/pallas_call | solution.py:973
  39.1 5.8 %all-to-all-start.3 = ((f32[16,16,128]{2,1,0:T(8,128)}), f32[16,16,128]{2,1,0:T(8,128)S(1)}, u32[]{:S(2)}, u32[]{:S(2)}) async-start(f32[16,16,128]{2,1,0:T(8,128)} %bitcast.13), calls=%async_computation.3 | async-start | bytes 262144 | tf_op jit(solution)/shard_map/all_to_all | solution.py:986
  44.9 2.4 %shard_map.272 = (f32[1,160,90]{2,1,0:T(8,128)}, f32[1,160,90]{2,1,0:T(8,128)}) custom-call(s32[1]{0:T(128)} %bitcast.place_ref, f32[384,128]{1,0:T(8,128)S(1)} %bitcast.23, f32[256,128]{1,0:T(8,128)S(1)} %bitcast.27, f32[160,128]{1,0:T(8,128)S(1)} %get-tuple-element.61.grad_ref, f32[160,128]{1,0:T(8,128)S(1)} %get-tuple-element.62.columns_ref, ...), custom_call_target="tpu_custom_call" | custom-call | flops 4000000000 | bytes 8000000 | tf_op jit(solution)/shard_map/pallas_call | solution.py:973
  47.4 0.0 copy-start.3
  47.4 0.7 %all-to-all-done.3 = f32[16,16,128]{2,1,0:T(8,128)S(1)} async-done(((f32[16,16,128]{2,1,0:T(8,128)}), f32[16,16,128]{2,1,0:T(8,128)S(1)}, u32[]{:S(2)}, u32[]{:S(2)}) %all-to-all-start.3) | async-done | bytes 131104 | tf_op jit(solution)/shard_map/all_to_all | solution.py:986
  48.1 0.0 copy-done.3
  48.1 0.8 %shard_map.274 = (f32[1,160]{1,0:T(1,128)}, f32[1,160]{1,0:T(1,128)}, f32[4,256]{1,0:T(4,128)}, f32[4,256]{1,0:T(4,128)}, f32[4,32]{1,0:T(4,128)}, /*index=5*/f3...) custom-call(f32[256,128]{1,0:T(8,128)S(1)} %bitcast.25, f32[1,256]{1,0:T(1,128)S(1)} %copy-done.3), custom_call_target="tpu_custom_call" | custom-call | flops 100000000 | bytes 1000000 | tf_op jit(solution)/shard_map/pallas_call | solution.py:973
Async XLA Ops:
  2.9 15.7 %all-to-all-start = ((f32[16,32,128]{2,1,0:T(8,128)}), f32[16,32,128]{2,1,0:T(8,128)S(1)}, u32[]{:S(2)}, u32[]{:S(2)}) async-start(f32[16,32,128]{2,1,0:T(8,128)} %bitcast.2), calls=%async_computation | async-start | bytes 524288 | tf_op jit(solution)/shard_map/all_to_all | solution.py:986
  11.7 6.9 %copy-start = (bf16[64,2048]{1,0:T(8,128)(2,1)S(1)}, bf16[64,2048]{1,0:T(8,128)(2,1)}, u32[]{:S(2)}) copy-start(bf16[64,2048]{1,0:T(8,128)(2,1)} %constant.34.clone.from_modes_ref) | copy-start | bytes 786436
  11.7 6.9 %copy-start.1 = (bf16[1024,128]{1,0:T(8,128)(2,1)S(1)}, bf16[1024,128]{1,0:T(8,128)(2,1)}, u32[]{:S(2)}) copy-start(bf16[1024,128]{1,0:T(8,128)(2,1)} %constant.33.clone.to_modes_ref) | copy-start | bytes 786436
  11.8 6.9 %copy-start.2 = (bf16[256,256]{1,0:T(8,128)(2,1)S(1)}, bf16[256,256]{1,0:T(8,128)(2,1)}, u32[]{:S(2)}) copy-start(bf16[256,256]{1,0:T(8,128)(2,1)} %constant.35.clone.earlier_ref.earlier_hbm) | copy-start | bytes 393220
  20.6 9.7 %all-to-all-start.1 = ((f32[8,48,128]{2,1,0:T(8,128)}), f32[8,48,128]{2,1,0:T(8,128)S(1)}, u32[]{:S(2)}, u32[]{:S(2)}) async-start(f32[8,48,128]{2,1,0:T(8,128)} %bitcast.9), calls=%async_computation.1 | async-start | bytes 393216 | tf_op jit(solution)/shard_map/all_to_all | solution.py:986
  25.1 5.1 %collective-permute-start = (f32[120,128]{1,0:T(8,128)S(1)}, f32[120,128]{1,0:T(8,128)S(1)}, u32[]{:S(2)}, u32[]{:S(2)}) collective-permute-start(f32[120,128]{1,0:T(8,128)S(1)} %get-tuple-element.50), channel_id=1, source_target_pairs={{0,16},{2,18},{4,20},{6,22},{8,24},{10,26},{12,28},{14,30},{16,0},... | collective-permute-start | bytes 184328 | tf_op jit(solution)/shard_map/ppermute | solution.py:1090
  39.1 9.0 %all-to-all-start.3 = ((f32[16,16,128]{2,1,0:T(8,128)}), f32[16,16,128]{2,1,0:T(8,128)S(1)}, u32[]{:S(2)}, u32[]{:S(2)}) async-start(f32[16,16,128]{2,1,0:T(8,128)} %bitcast.13), calls=%async_computation.3 | async-start | bytes 262144 | tf_op jit(solution)/shard_map/all_to_all | solution.py:986
  47.4 0.7 %copy-start.3 = (f32[1,256]{1,0:T(1,128)S(1)}, f32[1,256]{1,0:T(1,128)}, u32[]{:S(2)}) copy-start(f32[1,256]{1,0:T(1,128)} %constant.30.clone.endpoint_hbm.endpoint_ref) | copy-start | bytes 3076

commit v5 on v4

--- a/solution.py
+++ b/solution.py
@@ -160,7 +160,7 @@
 def share_order(devices):
     sharing = devices // HALVES
     if sharing == 16:
-        return [15, 1, 12, 14, 8, 4, 7, 3, 2, 11, 5, 6, 10, 0, 9, 13]
+        return [15, 1, 12, 8, 14, 4, 7, 3, 2, 11, 5, 6, 0, 10, 9, 13]
     return [int(k) for k in np.random.default_rng(0).permutation(sharing)]
 
 
@@ -261,22 +261,25 @@
         out = dot(jnp.concatenate([high, low], 0), both)
         part = out[:channels, :LANES] + out[:channels, LANES:] + out[channels:, :LANES]
         total = part if total is None else total + part
-    spot = lax.broadcasted_iota(jnp.int32, (channels, LANES), 1) == LANES - 2
+    lane = lax.broadcasted_iota(jnp.int32, (channels, LANES), 1)
+    spot = lane == LANES - 2
+    behind = (lane[:sets] >= steps) & (lane[:sets] < steps + EXTRA)
     sums = jnp.sum(pad_ref[...], axis=1, keepdims=True)
     grad_ref[...] = total
     ready(3)
     pad_ref[:, :steps] = series_ref[0]
     pad_ref[...] = jnp.where(spot, sums, pad_ref[...])
     for kind, ref in enumerate((pad_ref, grad_ref)):
-        for i in range(own):
+        for i in range(KIND):
             value = ref[sets * i : sets * (i + 1), :]
             if kind and i < own - KIND:
                 there = sets * (KIND + i)
                 value = jnp.where(spot[:sets], sums[there : there + sets], value)
-            if i < KIND:
-                send_ref[pl.ds(KIND * kind + i, sets, stride=rows), :] = value
-            else:
-                pack_extra(send_ref, value, i, kind, rows, steps)
+            there, p = sets * (KIND + i // 4), i % 4
+            if there < channels and p < 3:
+                extra = pltpu.roll(ref[there : there + sets, :], steps - EXTRA * p, 1)
+                value = jnp.where(behind, extra, value)
+            send_ref[pl.ds(KIND * kind + i, sets, stride=rows), :] = value
     for half in range(1, HALVES):
         send_ref[half * sets * rows : (half + 1) * sets * rows, :] = send_ref[0 : sets * rows, :]
 
@@ -353,6 +356,7 @@
     lines_ref[...] = jnp.zeros_like(lines_ref)
     turned_ref[...] = jnp.zeros_like(turned_ref)
     cot_pad_ref[...] = jnp.zeros_like(cot_pad_ref)
+    same_ref[...] = jnp.zeros_like(same_ref)
     ready(0, 1, 2, 3)
     kernel = lax.dot_general(
         mode_in_ref[...],

time: 49.4 us -> 48.8 us (0.988)
  transfers between devices with their start and end apart: 4 -> 4, of which waited for: 3 -> 3; matrix products, arithmetic and copies ran while one was open for 0% -> 0% of each run, Pallas kernels for 16% -> 17%
where the time goes in v5:
time: 48.8 us; the launch traced here: 48.3 us
  starting transfers between devices  20.4 us (42%)
  Pallas kernels  14 us (29%)
  blocking collectives  7.81 us (16%)
  waiting for transfers between devices  5.42 us (11%)
  between operations  0.72 us (1%)
    all_to_all x3, starting transfers between devices, exchange(): lax.all_to_all(value.reshape(count, value.shape[0] // count, value.shape[...  18.7 us
    pallas_call x8, Pallas kernels, call(): pl.pallas_call(kernel, out_shape=tuple((jax.ShapeDtypeStruct(shape, kind)...  14 us
    all_to_all x1, blocking collectives, exchange(): lax.all_to_all(value.reshape(count, value.shape[0] // count, value.shape[...  7.81 us
    all_to_all x3, waiting for transfers between devices, exchange(): lax.all_to_all(value.reshape(count, value.shape[0] // count, value.shape[...  4.47 us
    ppermute x1, starting transfers between devices, body(): lax.ppermute(cot_send, 'seq', [(k, (k + sets) % blocks) for k in range(bl...  1.61 us
  transfers between devices with their start and end apart: 4, of which 3 were waited for; matrix products, arithmetic and copies ran while one was open for 0% of the time, Pallas kernels for 17%

profile of v5, /device:TPU:0, one launch (start us, length us, event | category | flops | bytes accessed | tf_op | source)
XLA Modules:
  0.0 48.3 jit_solution(14050963796639935169)
XLA Ops:
  0.6 2.2 %shard_map.267 = (f32[512,128]{1,0:T(8,128)}, f32[160,128]{1,0:T(8,128)S(1)}) custom-call(f32[1,160,90]{2,1,0:T(8,128)} %series_hbm.3, f32[1,160,90]{2,1,0:T(8,128)} %cot_hbm.5, f32[160,160]{1,0:T(8,128)} %mixing_hbm.3, s32[1,160]{1,0:T(1,128)} %bitcast.30), custom_call_target="tpu_custom_call" | custom-call | flops 100000000 | bytes 1000000 | tf_op jit(solution)/shard_map/pallas_call | solution.py:977
  2.9 8.8 %all-to-all-start = ((f32[16,32,128]{2,1,0:T(8,128)}), f32[16,32,128]{2,1,0:T(8,128)S(1)}, u32[]{:S(2)}, u32[]{:S(2)}) async-start(f32[16,32,128]{2,1,0:T(8,128)} %bitcast.2), calls=%async_computation | async-start | bytes 524288 | tf_op jit(solution)/shard_map/all_to_all | solution.py:990
  11.7 0.0 copy-start
  11.7 0.0 copy-start.1
  11.7 0.0 copy-start.2
  11.7 3.1 %shard_map.268 = (bf16[1024,256]{1,0:T(8,128)(2,1)S(1)}, f32[32,1024]{1,0:T(8,128)S(1)}, f32[80,128]{1,0:T(8,128)S(1)}, f32[160,128]{1,0:T(8,128)S(1)}, bf16[2,1...) custom-call(s32[1]{0:T(128)} %bitcast.place_ref, ...), custom_call_target="tpu_custom_call" | custom-call | flops 4000000000 | bytes 8000000 | tf_op jit(solution)/shard_map/pallas_call | solution.py:977
  14.8 3.8 %all-to-all-done = f32[16,32,128]{2,1,0:T(8,128)S(1)} async-done(((f32[16,32,128]{2,1,0:T(8,128)}), f32[16,32,128]{2,1,0:T(8,128)S(1)}, u32[]{:S(2)}, u32[]{:S(2)}) %all-to-all-start) | async-done | bytes 262176 | tf_op jit(solution)/shard_map/all_to_all | solution.py:990
  18.6 0.0 copy-done
  18.6 0.0 copy-done.1
  18.6 0.0 copy-done.2
  18.6 1.9 %shard_map.269 = (f32[384,128]{1,0:T(8,128)}, f32[384,128]{1,0:T(8,128)S(1)}, f32[384,128]{1,0:T(8,128)S(1)}, f32[384,128]{1,0:T(8,128)S(1)}, f32[384,128]{1,0:T...) custom-call(s32[1]{0:T(128)} %bitcast.place_ref, f32[512,128]{1,0:T(8,128)S(1)} %bitcast.20, ...), custom_call_target="tpu_custom_call" | custom-call | flops 100000000 | bytes 1000000 | tf_op jit(solution)/shard_map/pallas_call | solution.py:977
  20.5 4.6 %all-to-all-start.1 = ((f32[8,48,128]{2,1,0:T(8,128)}), f32[8,48,128]{2,1,0:T(8,128)S(1)}, u32[]{:S(2)}, u32[]{:S(2)}) async-start(f32[8,48,128]{2,1,0:T(8,128)} %bitcast.9), calls=%async_computation.1 | async-start | bytes 393216 | tf_op jit(solution)/shard_map/all_to_all | solution.py:990
  25.0 1.6 %collective-permute-start = (f32[120,128]{1,0:T(8,128)S(1)}, f32[120,128]{1,0:T(8,128)S(1)}, u32[]{:S(2)}, u32[]{:S(2)}) collective-permute-start(f32[120,128]{1,0:T(8,128)S(1)} %get-tuple-element.50), channel_id=1, source_target_pairs={{0,16},{2,18},{4,20},{6,22},{8,24},{10,26},{12,28},{14,30},{16,0},... | collective-permute-start | bytes 184328 | tf_op jit(solution)/shard_map/ppermute | solution.py:1094
  26.6 2.6 %shard_map.270 = (f32[24,128]{1,0:T(8,128)S(1)}, f32[16,128]{1,0:T(8,128)S(1)}) custom-call(s32[1]{0:T(128)} %bitcast.place_ref, f32[512,128]{1,0:T(8,128)S(1)} %bitcast.21, f32[80,128]{1,0:T(8,128)S(1)} %get-tuple-element.43.own_ref, f32[384,128]{1,0:T(8,128)S(1)} %get-tuple-element.51.mean_ref, f32[384,128]{1,0:T(8,128)S(1)} %get-tuple-element.52.inverse_ref, ...), custom_call_target="tpu_custom_call" | custom-call | flops 4000000000 | bytes 8000000 | tf_op jit(solution)/shard_map/pallas_call | solution.py:977
  29.2 0.9 %collective-permute-done.cot_partner_ref = f32[120,128]{1,0:T(8,128)S(1)} collective-permute-done((f32[120,128]{1,0:T(8,128)S(1)}, f32[120,128]{1,0:T(8,128)S(1)}, u32[]{:S(2)}, u32[]{:S(2)}) %collective-permute-start) | collective-permute-done | bytes 61472 | tf_op jit(solution)/shard_map/ppermute | solution.py:1094
  30.2 0.0 all-to-all-done.1
  30.2 0.4 shard_map.271
  30.6 7.8 %all_to_all.20 = f32[16,16,128]{2,1,0:T(8,128)S(1)} all-to-all(f32[16,16,128]{2,1,0:T(8,128)S(1)} %bitcast.24), channel_id=1, replica_groups={{15,1,12,8,14,4,7,3,2,11,5,6,0,10,9,13},{31,17,28,24,30,20,23,19,18,27,..., dimensions={0} | all-to-all | bytes 262144 | tf_op jit(solution)/shard_map/all_to_all | solution.py:990
  38.4 0.7 %shard_map.273 = f32[256,128]{1,0:T(8,128)} custom-call(f32[256,128]{1,0:T(8,128)S(1)} %bitcast.26), custom_call_target="tpu_custom_call" | custom-call | flops 100000000 | bytes 1000000 | tf_op jit(solution)/shard_map/pallas_call | solution.py:977
  39.1 5.4 %all-to-all-start.3 = ((f32[16,16,128]{2,1,0:T(8,128)}), f32[16,16,128]{2,1,0:T(8,128)S(1)}, u32[]{:S(2)}, u32[]{:S(2)}) async-start(f32[16,16,128]{2,1,0:T(8,128)} %bitcast.13), calls=%async_computation.3 | async-start | bytes 262144 | tf_op jit(solution)/shard_map/all_to_all | solution.py:990
  44.4 2.4 %shard_map.272 = (f32[1,160,90]{2,1,0:T(8,128)}, f32[1,160,90]{2,1,0:T(8,128)}) custom-call(s32[1]{0:T(128)} %bitcast.place_ref, f32[384,128]{1,0:T(8,128)S(1)} %bitcast.23, f32[256,128]{1,0:T(8,128)S(1)} %bitcast.27, f32[160,128]{1,0:T(8,128)S(1)} %get-tuple-element.61.grad_ref, f32[160,128]{1,0:T(8,128)S(1)} %get-tuple-element.62.columns_ref, ...), custom_call_target="tpu_custom_call" | custom-call | flops 4000000000 | bytes 8000000 | tf_op jit(solution)/shard_map/pallas_call | solution.py:977
  46.9 0.0 copy-start.3
  46.9 0.7 %all-to-all-done.3 = f32[16,16,128]{2,1,0:T(8,128)S(1)} async-done(((f32[16,16,128]{2,1,0:T(8,128)}), f32[16,16,128]{2,1,0:T(8,128)S(1)}, u32[]{:S(2)}, u32[]{:S(2)}) %all-to-all-start.3) | async-done | bytes 131104 | tf_op jit(solution)/shard_map/all_to_all | solution.py:990
  47.6 0.0 copy-done.3
  47.6 0.8 %shard_map.274 = (f32[1,160]{1,0:T(1,128)}, f32[1,160]{1,0:T(1,128)}, f32[4,256]{1,0:T(4,128)}, f32[4,256]{1,0:T(4,128)}, f32[4,32]{1,0:T(4,128)}, /*index=5*/f3...) custom-call(f32[256,128]{1,0:T(8,128)S(1)} %bitcast.25, f32[1,256]{1,0:T(1,128)S(1)} %copy-done.3), custom_call_target="tpu_custom_call" | custom-call | flops 100000000 | bytes 1000000 | tf_op jit(solution)/shard_map/pallas_call | solution.py:977
Async XLA Ops:
  2.9 15.7 %all-to-all-start = ((f32[16,32,128]{2,1,0:T(8,128)}), f32[16,32,128]{2,1,0:T(8,128)S(1)}, u32[]{:S(2)}, u32[]{:S(2)}) async-start(f32[16,32,128]{2,1,0:T(8,128)} %bitcast.2), calls=%async_computation | async-start | bytes 524288 | tf_op jit(solution)/shard_map/all_to_all | solution.py:990
  11.7 6.9 %copy-start = (bf16[64,2048]{1,0:T(8,128)(2,1)S(1)}, bf16[64,2048]{1,0:T(8,128)(2,1)}, u32[]{:S(2)}) copy-start(bf16[64,2048]{1,0:T(8,128)(2,1)} %constant.34.clone.from_modes_ref) | copy-start | bytes 786436
  11.7 6.9 %copy-start.1 = (bf16[1024,128]{1,0:T(8,128)(2,1)S(1)}, bf16[1024,128]{1,0:T(8,128)(2,1)}, u32[]{:S(2)}) copy-start(bf16[1024,128]{1,0:T(8,128)(2,1)} %constant.33.clone.to_modes_ref) | copy-start | bytes 786436
  11.7 6.9 %copy-start.2 = (bf16[256,256]{1,0:T(8,128)(2,1)S(1)}, bf16[256,256]{1,0:T(8,128)(2,1)}, u32[]{:S(2)}) copy-start(bf16[256,256]{1,0:T(8,128)(2,1)} %constant.35.clone.earlier_ref.earlier_hbm) | copy-start | bytes 393220
  20.5 9.7 %all-to-all-start.1 = ((f32[8,48,128]{2,1,0:T(8,128)}), f32[8,48,128]{2,1,0:T(8,128)S(1)}, u32[]{:S(2)}, u32[]{:S(2)}) async-start(f32[8,48,128]{2,1,0:T(8,128)} %bitcast.9), calls=%async_computation.1 | async-start | bytes 393216 | tf_op jit(solution)/shard_map/all_to_all | solution.py:990
  25.0 5.1 %collective-permute-start = (f32[120,128]{1,0:T(8,128)S(1)}, f32[120,128]{1,0:T(8,128)S(1)}, u32[]{:S(2)}, u32[]{:S(2)}) collective-permute-start(f32[120,128]{1,0:T(8,128)S(1)} %get-tuple-element.50), channel_id=1, source_target_pairs={{0,16},{2,18},{4,20},{6,22},{8,24},{10,26},{12,28},{14,30},{16,0},... | collective-permute-start | bytes 184328 | tf_op jit(solution)/shard_map/ppermute | solution.py:1094
  39.1 8.5 %all-to-all-start.3 = ((f32[16,16,128]{2,1,0:T(8,128)}), f32[16,16,128]{2,1,0:T(8,128)S(1)}, u32[]{:S(2)}, u32[]{:S(2)}) async-start(f32[16,16,128]{2,1,0:T(8,128)} %bitcast.13), calls=%async_computation.3 | async-start | bytes 262144 | tf_op jit(solution)/shard_map/all_to_all | solution.py:990
  46.9 0.7 %copy-start.3 = (f32[1,256]{1,0:T(1,128)S(1)}, f32[1,256]{1,0:T(1,128)}, u32[]{:S(2)}) copy-start(f32[1,256]{1,0:T(1,128)} %constant.30.clone.endpoint_hbm.endpoint_ref) | copy-start | bytes 3076

commit v6 on v5

--- a/solution.py
+++ b/solution.py
@@ -160,7 +160,7 @@
 def share_order(devices):
     sharing = devices // HALVES
     if sharing == 16:
-        return [15, 1, 12, 8, 14, 4, 7, 3, 2, 11, 5, 6, 0, 10, 9, 13]
+        return [15, 1, 12, 8, 14, 11, 7, 3, 4, 2, 5, 6, 0, 10, 9, 13]
     return [int(k) for k in np.random.default_rng(0).permutation(sharing)]
 
 

time: 48.8 us -> 48.9 us (level)
  no operation moved by 1% of the time
where the time goes in v6:
time: 48.9 us; the launch traced here: 48.4 us
  starting transfers between devices  20.3 us (42%)
  Pallas kernels  14 us (29%)
  blocking collectives  7.84 us (16%)
  waiting for transfers between devices  5.45 us (11%)
  between operations  0.72 us (1%)
    all_to_all x3, starting transfers between devices, exchange(): lax.all_to_all(value.reshape(count, value.shape[0] // count, value.shape[...  18.7 us
    pallas_call x8, Pallas kernels, call(): pl.pallas_call(kernel, out_shape=tuple((jax.ShapeDtypeStruct(shape, kind)...  14 us
    all_to_all x1, blocking collectives, exchange(): lax.all_to_all(value.reshape(count, value.shape[0] // count, value.shape[...  7.84 us
    all_to_all x3, waiting for transfers between devices, exchange(): lax.all_to_all(value.reshape(count, value.shape[0] // count, value.shape[...  4.5 us
    ppermute x1, starting transfers between devices, body(): lax.ppermute(cot_send, 'seq', [(k, (k + sets) % blocks) for k in range(bl...  1.61 us
  transfers between devices with their start and end apart: 4, of which 3 were waited for; matrix products, arithmetic and copies ran while one was open for 0% of the time, Pallas kernels for 17%

profile of v6, /device:TPU:0, one launch (start us, length us, event | category | flops | bytes accessed | tf_op | source)
XLA Modules:
  0.0 48.4 jit_solution(16834059614442783888)
XLA Ops:
  0.6 2.2 %shard_map.267 = (f32[512,128]{1,0:T(8,128)}, f32[160,128]{1,0:T(8,128)S(1)}) custom-call(f32[1,160,90]{2,1,0:T(8,128)} %series_hbm.3, f32[1,160,90]{2,1,0:T(8,128)} %cot_hbm.5, f32[160,160]{1,0:T(8,128)} %mixing_hbm.3, s32[1,160]{1,0:T(1,128)} %bitcast.30), custom_call_target="tpu_custom_call" | custom-call | flops 100000000 | bytes 1000000 | tf_op jit(solution)/shard_map/pallas_call | solution.py:977
  2.9 8.8 %all-to-all-start = ((f32[16,32,128]{2,1,0:T(8,128)}), f32[16,32,128]{2,1,0:T(8,128)S(1)}, u32[]{:S(2)}, u32[]{:S(2)}) async-start(f32[16,32,128]{2,1,0:T(8,128)} %bitcast.2), calls=%async_computation | async-start | bytes 524288 | tf_op jit(solution)/shard_map/all_to_all | solution.py:990
  11.7 0.0 copy-start
  11.7 0.0 copy-start.1
  11.7 0.0 copy-start.2
  11.7 3.1 %shard_map.268 = (bf16[1024,256]{1,0:T(8,128)(2,1)S(1)}, f32[32,1024]{1,0:T(8,128)S(1)}, f32[80,128]{1,0:T(8,128)S(1)}, f32[160,128]{1,0:T(8,128)S(1)}, bf16[2,1...) custom-call(s32[1]{0:T(128)} %bitcast.place_ref, ...), custom_call_target="tpu_custom_call" | custom-call | flops 4000000000 | bytes 8000000 | tf_op jit(solution)/shard_map/pallas_call | solution.py:977
  14.8 3.8 %all-to-all-done = f32[16,32,128]{2,1,0:T(8,128)S(1)} async-done(((f32[16,32,128]{2,1,0:T(8,128)}), f32[16,32,128]{2,1,0:T(8,128)S(1)}, u32[]{:S(2)}, u32[]{:S(2)}) %all-to-all-start) | async-done | bytes 262176 | tf_op jit(solution)/shard_map/all_to_all | solution.py:990
  18.6 0.0 copy-done
  18.6 0.0 copy-done.1
  18.6 0.0 copy-done.2
  18.6 1.9 %shard_map.269 = (f32[384,128]{1,0:T(8,128)}, f32[384,128]{1,0:T(8,128)S(1)}, f32[384,128]{1,0:T(8,128)S(1)}, f32[384,128]{1,0:T(8,128)S(1)}, f32[384,128]{1,0:T...) custom-call(s32[1]{0:T(128)} %bitcast.place_ref, f32[512,128]{1,0:T(8,128)S(1)} %bitcast.20, ...), custom_call_target="tpu_custom_call" | custom-call | flops 100000000 | bytes 1000000 | tf_op jit(solution)/shard_map/pallas_call | solution.py:977
  20.5 4.6 %all-to-all-start.1 = ((f32[8,48,128]{2,1,0:T(8,128)}), f32[8,48,128]{2,1,0:T(8,128)S(1)}, u32[]{:S(2)}, u32[]{:S(2)}) async-start(f32[8,48,128]{2,1,0:T(8,128)} %bitcast.9), calls=%async_computation.1 | async-start | bytes 393216 | tf_op jit(solution)/shard_map/all_to_all | solution.py:990
  25.0 1.6 %collective-permute-start = (f32[120,128]{1,0:T(8,128)S(1)}, f32[120,128]{1,0:T(8,128)S(1)}, u32[]{:S(2)}, u32[]{:S(2)}) collective-permute-start(f32[120,128]{1,0:T(8,128)S(1)} %get-tuple-element.50), channel_id=1, source_target_pairs={{0,16},{2,18},{4,20},{6,22},{8,24},{10,26},{12,28},{14,30},{16,0},... | collective-permute-start | bytes 184328 | tf_op jit(solution)/shard_map/ppermute | solution.py:1094
  26.6 2.6 %shard_map.270 = (f32[24,128]{1,0:T(8,128)S(1)}, f32[16,128]{1,0:T(8,128)S(1)}) custom-call(s32[1]{0:T(128)} %bitcast.place_ref, f32[512,128]{1,0:T(8,128)S(1)} %bitcast.21, f32[80,128]{1,0:T(8,128)S(1)} %get-tuple-element.43.own_ref, f32[384,128]{1,0:T(8,128)S(1)} %get-tuple-element.51.mean_ref, f32[384,128]{1,0:T(8,128)S(1)} %get-tuple-element.52.inverse_ref, ...), custom_call_target="tpu_custom_call" | custom-call | flops 4000000000 | bytes 8000000 | tf_op jit(solution)/shard_map/pallas_call | solution.py:977
  29.2 0.9 %collective-permute-done.cot_partner_ref = f32[120,128]{1,0:T(8,128)S(1)} collective-permute-done((f32[120,128]{1,0:T(8,128)S(1)}, f32[120,128]{1,0:T(8,128)S(1)}, u32[]{:S(2)}, u32[]{:S(2)}) %collective-permute-start) | collective-permute-done | bytes 61472 | tf_op jit(solution)/shard_map/ppermute | solution.py:1094
  30.2 0.0 all-to-all-done.1
  30.2 0.4 shard_map.271
  30.6 7.8 %all_to_all.20 = f32[16,16,128]{2,1,0:T(8,128)S(1)} all-to-all(f32[16,16,128]{2,1,0:T(8,128)S(1)} %bitcast.24), channel_id=1, replica_groups={{15,1,12,8,14,11,7,3,4,2,5,6,0,10,9,13},{31,17,28,24,30,27,23,19,20,18,..., dimensions={0} | all-to-all | bytes 262144 | tf_op jit(solution)/shard_map/all_to_all | solution.py:990
  38.4 0.7 %shard_map.273 = f32[256,128]{1,0:T(8,128)} custom-call(f32[256,128]{1,0:T(8,128)S(1)} %bitcast.26), custom_call_target="tpu_custom_call" | custom-call | flops 100000000 | bytes 1000000 | tf_op jit(solution)/shard_map/pallas_call | solution.py:977
  39.1 5.4 %all-to-all-start.3 = ((f32[16,16,128]{2,1,0:T(8,128)}), f32[16,16,128]{2,1,0:T(8,128)S(1)}, u32[]{:S(2)}, u32[]{:S(2)}) async-start(f32[16,16,128]{2,1,0:T(8,128)} %bitcast.13), calls=%async_computation.3 | async-start | bytes 262144 | tf_op jit(solution)/shard_map/all_to_all | solution.py:990
  44.4 2.4 %shard_map.272 = (f32[1,160,90]{2,1,0:T(8,128)}, f32[1,160,90]{2,1,0:T(8,128)}) custom-call(s32[1]{0:T(128)} %bitcast.place_ref, f32[384,128]{1,0:T(8,128)S(1)} %bitcast.23, f32[256,128]{1,0:T(8,128)S(1)} %bitcast.27, f32[160,128]{1,0:T(8,128)S(1)} %get-tuple-element.61.grad_ref, f32[160,128]{1,0:T(8,128)S(1)} %get-tuple-element.62.columns_ref, ...), custom_call_target="tpu_custom_call" | custom-call | flops 4000000000 | bytes 8000000 | tf_op jit(solution)/shard_map/pallas_call | solution.py:977
  46.9 0.0 copy-start.3
  46.9 0.7 %all-to-all-done.3 = f32[16,16,128]{2,1,0:T(8,128)S(1)} async-done(((f32[16,16,128]{2,1,0:T(8,128)}), f32[16,16,128]{2,1,0:T(8,128)S(1)}, u32[]{:S(2)}, u32[]{:S(2)}) %all-to-all-start.3) | async-done | bytes 131104 | tf_op jit(solution)/shard_map/all_to_all | solution.py:990
  47.6 0.0 copy-done.3
  47.6 0.8 %shard_map.274 = (f32[1,160]{1,0:T(1,128)}, f32[1,160]{1,0:T(1,128)}, f32[4,256]{1,0:T(4,128)}, f32[4,256]{1,0:T(4,128)}, f32[4,32]{1,0:T(4,128)}, /*index=5*/f3...) custom-call(f32[256,128]{1,0:T(8,128)S(1)} %bitcast.25, f32[1,256]{1,0:T(1,128)S(1)} %copy-done.3), custom_call_target="tpu_custom_call" | custom-call | flops 100000000 | bytes 1000000 | tf_op jit(solution)/shard_map/pallas_call | solution.py:977
Async XLA Ops:
  2.9 15.7 %all-to-all-start = ((f32[16,32,128]{2,1,0:T(8,128)}), f32[16,32,128]{2,1,0:T(8,128)S(1)}, u32[]{:S(2)}, u32[]{:S(2)}) async-start(f32[16,32,128]{2,1,0:T(8,128)} %bitcast.2), calls=%async_computation | async-start | bytes 524288 | tf_op jit(solution)/shard_map/all_to_all | solution.py:990
  11.7 6.9 %copy-start = (bf16[64,2048]{1,0:T(8,128)(2,1)S(1)}, bf16[64,2048]{1,0:T(8,128)(2,1)}, u32[]{:S(2)}) copy-start(bf16[64,2048]{1,0:T(8,128)(2,1)} %constant.34.clone.from_modes_ref) | copy-start | bytes 786436
  11.7 6.9 %copy-start.1 = (bf16[1024,128]{1,0:T(8,128)(2,1)S(1)}, bf16[1024,128]{1,0:T(8,128)(2,1)}, u32[]{:S(2)}) copy-start(bf16[1024,128]{1,0:T(8,128)(2,1)} %constant.33.clone.to_modes_ref) | copy-start | bytes 786436
  11.7 6.9 %copy-start.2 = (bf16[256,256]{1,0:T(8,128)(2,1)S(1)}, bf16[256,256]{1,0:T(8,128)(2,1)}, u32[]{:S(2)}) copy-start(bf16[256,256]{1,0:T(8,128)(2,1)} %constant.35.clone.earlier_ref.earlier_hbm) | copy-start | bytes 393220
  20.5 9.7 %all-to-all-start.1 = ((f32[8,48,128]{2,1,0:T(8,128)}), f32[8,48,128]{2,1,0:T(8,128)S(1)}, u32[]{:S(2)}, u32[]{:S(2)}) async-start(f32[8,48,128]{2,1,0:T(8,128)} %bitcast.9), calls=%async_computation.1 | async-start | bytes 393216 | tf_op jit(solution)/shard_map/all_to_all | solution.py:990
  25.0 5.1 %collective-permute-start = (f32[120,128]{1,0:T(8,128)S(1)}, f32[120,128]{1,0:T(8,128)S(1)}, u32[]{:S(2)}, u32[]{:S(2)}) collective-permute-start(f32[120,128]{1,0:T(8,128)S(1)} %get-tuple-element.50), channel_id=1, source_target_pairs={{0,16},{2,18},{4,20},{6,22},{8,24},{10,26},{12,28},{14,30},{16,0},... | collective-permute-start | bytes 184328 | tf_op jit(solution)/shard_map/ppermute | solution.py:1094
  39.1 8.5 %all-to-all-start.3 = ((f32[16,16,128]{2,1,0:T(8,128)}), f32[16,16,128]{2,1,0:T(8,128)S(1)}, u32[]{:S(2)}, u32[]{:S(2)}) async-start(f32[16,16,128]{2,1,0:T(8,128)} %bitcast.13), calls=%async_computation.3 | async-start | bytes 262144 | tf_op jit(solution)/shard_map/all_to_all | solution.py:990
  46.9 0.7 %copy-start.3 = (f32[1,256]{1,0:T(1,128)S(1)}, f32[1,256]{1,0:T(1,128)}, u32[]{:S(2)}) copy-start(f32[1,256]{1,0:T(1,128)} %constant.30.clone.endpoint_hbm.endpoint_ref) | copy-start | bytes 3076

commit v7 on v6

--- a/solution.py
+++ b/solution.py
@@ -308,7 +308,7 @@
     columns_ref,
     masked_ref,
     same_ref,
-    cot_pad_ref,
+    cot3_ref,
     cot_send_ref,
     cot_ref,
     mixing_ref,
@@ -326,6 +326,7 @@
     scale_ref,
     later_ref,
     turned_ref,
+    cot_pad_ref,
     sems,
 ):
     ready = fetch(
@@ -355,7 +356,6 @@
     count = 2 * MODES
     lines_ref[...] = jnp.zeros_like(lines_ref)
     turned_ref[...] = jnp.zeros_like(turned_ref)
-    cot_pad_ref[...] = jnp.zeros_like(cot_pad_ref)
     same_ref[...] = jnp.zeros_like(same_ref)
     ready(0, 1, 2, 3)
     kernel = lax.dot_general(
@@ -427,7 +427,10 @@
     own_ref[SLOT : 2 * SLOT, :] = jnp.broadcast_to(bias, (SLOT, LANES))
     own_ref[2 * SLOT : 3 * SLOT, :] = jnp.broadcast_to(1.0 / gain, (SLOT, LANES))
     own_ref[3 * SLOT :, :] = jnp.broadcast_to(scale_ref[...], (8, LANES))
+    cot_pad_ref[...] = jnp.zeros_like(cot_pad_ref)
     cot_pad_ref[:, :steps] = cot_ref[0]
+    high, low = split(cot_pad_ref[...])
+    cot3_ref[...] = jnp.concatenate([high, high, low], 1)
     most = cot_send_ref.shape[0]
     lane = lax.broadcasted_iota(jnp.int32, (channels - most, LANES), 1)
     behind = (lane >= steps) & (lane < steps + EXTRA)
@@ -752,7 +755,7 @@
     steps,
     recv_ref,
     same_ref,
-    cot_ref,
+    cot3_ref,
     cot_partner_ref,
     misc_ref,
     starts_ref,
@@ -788,11 +791,8 @@
     chunk = channels if channels <= 512 else devices
     for start in range(0, channels, chunk):
         at = slice(start, start + chunk)
-        six = []
-        for ref in (cot_ref, cot_all_ref):
-            high, low = split(ref[at, :])
-            six += [high, high, low]
-        grad = dot_nt(jnp.concatenate(six, 1), three)
+        high, low = split(cot_all_ref[at, :])
+        grad = dot_nt(jnp.concatenate([cot3_ref[at, :], high, high, low], 1), three)
         for j in range(tiles):
             lanes = slice(j * LANES, (j + 1) * LANES)
             tile = grad[:, lanes] * same_ref[at, lanes]
@@ -1045,7 +1045,7 @@
             ((channels, LANES), f32),
             ((2, channels, channels), bf16),
             ((channels, padded), f32),
-            ((channels, LANES), f32),
+            ((channels, 3 * LANES), bf16),
             ((channels * 3 // 4, LANES), f32),
         ],
         smem=(place,),
@@ -1066,7 +1066,7 @@
             const["scale"],
             const["later"],
         ),
-        scratch=[pltpu.VMEM((LANES, LANES), f32)],
+        scratch=[pltpu.VMEM((LANES, LANES), f32), pltpu.VMEM((channels, LANES), f32)],
         cost=busy,
     )
     owned_rows = exchange(send, "seq", all_of)

time: 48.9 us -> 48.8 us (level)
  no operation moved by 1% of the time
where the time goes in v7:
time: 48.8 us; the launch traced here: 48.3 us
  starting transfers between devices  20.3 us (42%)
  Pallas kernels  14 us (29%)
  blocking collectives  7.84 us (16%)
  waiting for transfers between devices  5.45 us (11%)
  between operations  0.72 us (1%)
    all_to_all x3, starting transfers between devices, exchange(): lax.all_to_all(value.reshape(count, value.shape[0] // count, value.shape[...  18.7 us
    pallas_call x8, Pallas kernels, call(): pl.pallas_call(kernel, out_shape=tuple((jax.ShapeDtypeStruct(shape, kind)...  14 us
    all_to_all x1, blocking collectives, exchange(): lax.all_to_all(value.reshape(count, value.shape[0] // count, value.shape[...  7.84 us
    all_to_all x3, waiting for transfers between devices, exchange(): lax.all_to_all(value.reshape(count, value.shape[0] // count, value.shape[...  4.5 us
    ppermute x1, starting transfers between devices, body(): lax.ppermute(cot_send, 'seq', [(k, (k + sets) % blocks) for k in range(bl...  1.61 us
  transfers between devices with their start and end apart: 4, of which 3 were waited for; matrix products, arithmetic and copies ran while one was open for 0% of the time, Pallas kernels for 17%

profile of v7, /device:TPU:0, one launch (start us, length us, event | category | flops | bytes accessed | tf_op | source)
XLA Modules:
  0.0 48.3 jit_solution(10169071098173559339)
XLA Ops:
  0.6 2.2 %shard_map.267 = (f32[512,128]{1,0:T(8,128)}, f32[160,128]{1,0:T(8,128)S(1)}) custom-call(f32[1,160,90]{2,1,0:T(8,128)} %series_hbm.3, f32[1,160,90]{2,1,0:T(8,128)} %cot_hbm.5, f32[160,160]{1,0:T(8,128)} %mixing_hbm.3, s32[1,160]{1,0:T(1,128)} %bitcast.30), custom_call_target="tpu_custom_call" | custom-call | flops 100000000 | bytes 1000000 | tf_op jit(solution)/shard_map/pallas_call | solution.py:977
  2.9 8.8 %all-to-all-start = ((f32[16,32,128]{2,1,0:T(8,128)}), f32[16,32,128]{2,1,0:T(8,128)S(1)}, u32[]{:S(2)}, u32[]{:S(2)}) async-start(f32[16,32,128]{2,1,0:T(8,128)} %bitcast.2), calls=%async_computation | async-start | bytes 524288 | tf_op jit(solution)/shard_map/all_to_all | solution.py:990
  11.7 0.0 copy-start
  11.7 0.0 copy-start.1
  11.7 0.0 copy-start.2
  11.7 3.1 %shard_map.268 = (bf16[1024,256]{1,0:T(8,128)(2,1)S(1)}, f32[32,1024]{1,0:T(8,128)S(1)}, f32[80,128]{1,0:T(8,128)S(1)}, f32[160,128]{1,0:T(8,128)S(1)}, bf16[2,1...) custom-call(s32[1]{0:T(128)} %bitcast.place_ref, ...), custom_call_target="tpu_custom_call" | custom-call | flops 4000000000 | bytes 8000000 | tf_op jit(solution)/shard_map/pallas_call | solution.py:977
  14.8 3.8 %all-to-all-done = f32[16,32,128]{2,1,0:T(8,128)S(1)} async-done(((f32[16,32,128]{2,1,0:T(8,128)}), f32[16,32,128]{2,1,0:T(8,128)S(1)}, u32[]{:S(2)}, u32[]{:S(2)}) %all-to-all-start) | async-done | bytes 262176 | tf_op jit(solution)/shard_map/all_to_all | solution.py:990
  18.6 0.0 copy-done
  18.6 0.0 copy-done.1
  18.6 0.0 copy-done.2
  18.6 1.9 %shard_map.269 = (f32[384,128]{1,0:T(8,128)}, f32[384,128]{1,0:T(8,128)S(1)}, f32[384,128]{1,0:T(8,128)S(1)}, f32[384,128]{1,0:T(8,128)S(1)}, f32[384,128]{1,0:T...) custom-call(s32[1]{0:T(128)} %bitcast.place_ref, f32[512,128]{1,0:T(8,128)S(1)} %bitcast.20, ...), custom_call_target="tpu_custom_call" | custom-call | flops 100000000 | bytes 1000000 | tf_op jit(solution)/shard_map/pallas_call | solution.py:977
  20.5 4.5 %all-to-all-start.1 = ((f32[8,48,128]{2,1,0:T(8,128)}), f32[8,48,128]{2,1,0:T(8,128)S(1)}, u32[]{:S(2)}, u32[]{:S(2)}) async-start(f32[8,48,128]{2,1,0:T(8,128)} %bitcast.9), calls=%async_computation.1 | async-start | bytes 393216 | tf_op jit(solution)/shard_map/all_to_all | solution.py:990
  25.0 1.6 %collective-permute-start = (f32[120,128]{1,0:T(8,128)S(1)}, f32[120,128]{1,0:T(8,128)S(1)}, u32[]{:S(2)}, u32[]{:S(2)}) collective-permute-start(f32[120,128]{1,0:T(8,128)S(1)} %get-tuple-element.50), channel_id=1, source_target_pairs={{0,16},{2,18},{4,20},{6,22},{8,24},{10,26},{12,28},{14,30},{16,0},... | collective-permute-start | bytes 184328 | tf_op jit(solution)/shard_map/ppermute | solution.py:1094
  26.6 2.6 %shard_map.270 = (f32[24,128]{1,0:T(8,128)S(1)}, f32[16,128]{1,0:T(8,128)S(1)}) custom-call(s32[1]{0:T(128)} %bitcast.place_ref, f32[512,128]{1,0:T(8,128)S(1)} %bitcast.21, f32[80,128]{1,0:T(8,128)S(1)} %get-tuple-element.43.own_ref, f32[384,128]{1,0:T(8,128)S(1)} %get-tuple-element.51.mean_ref, f32[384,128]{1,0:T(8,128)S(1)} %get-tuple-element.52.inverse_ref, ...), custom_call_target="tpu_custom_call" | custom-call | flops 4000000000 | bytes 8000000 | tf_op jit(solution)/shard_map/pallas_call | solution.py:977
  29.2 0.9 %collective-permute-done.cot_partner_ref = f32[120,128]{1,0:T(8,128)S(1)} collective-permute-done((f32[120,128]{1,0:T(8,128)S(1)}, f32[120,128]{1,0:T(8,128)S(1)}, u32[]{:S(2)}, u32[]{:S(2)}) %collective-permute-start) | collective-permute-done | bytes 61472 | tf_op jit(solution)/shard_map/ppermute | solution.py:1094
  30.1 0.0 all-to-all-done.1
  30.1 0.4 shard_map.271
  30.5 7.8 %all_to_all.20 = f32[16,16,128]{2,1,0:T(8,128)S(1)} all-to-all(f32[16,16,128]{2,1,0:T(8,128)S(1)} %bitcast.24), channel_id=1, replica_groups={{15,1,12,8,14,11,7,3,4,2,5,6,0,10,9,13},{31,17,28,24,30,27,23,19,20,18,..., dimensions={0} | all-to-all | bytes 262144 | tf_op jit(solution)/shard_map/all_to_all | solution.py:990
  38.4 0.7 %shard_map.273 = f32[256,128]{1,0:T(8,128)} custom-call(f32[256,128]{1,0:T(8,128)S(1)} %bitcast.26), custom_call_target="tpu_custom_call" | custom-call | flops 100000000 | bytes 1000000 | tf_op jit(solution)/shard_map/pallas_call | solution.py:977
  39.1 5.4 %all-to-all-start.3 = ((f32[16,16,128]{2,1,0:T(8,128)}), f32[16,16,128]{2,1,0:T(8,128)S(1)}, u32[]{:S(2)}, u32[]{:S(2)}) async-start(f32[16,16,128]{2,1,0:T(8,128)} %bitcast.13), calls=%async_computation.3 | async-start | bytes 262144 | tf_op jit(solution)/shard_map/all_to_all | solution.py:990
  44.4 2.4 %shard_map.272 = (f32[1,160,90]{2,1,0:T(8,128)}, f32[1,160,90]{2,1,0:T(8,128)}) custom-call(s32[1]{0:T(128)} %bitcast.place_ref, f32[384,128]{1,0:T(8,128)S(1)} %bitcast.23, f32[256,128]{1,0:T(8,128)S(1)} %bitcast.27, f32[160,128]{1,0:T(8,128)S(1)} %get-tuple-element.61.grad_ref, f32[160,128]{1,0:T(8,128)S(1)} %get-tuple-element.62.columns_ref, ...), custom_call_target="tpu_custom_call" | custom-call | flops 4000000000 | bytes 8000000 | tf_op jit(solution)/shard_map/pallas_call | solution.py:977
  46.8 0.0 copy-start.3
  46.9 0.7 %all-to-all-done.3 = f32[16,16,128]{2,1,0:T(8,128)S(1)} async-done(((f32[16,16,128]{2,1,0:T(8,128)}), f32[16,16,128]{2,1,0:T(8,128)S(1)}, u32[]{:S(2)}, u32[]{:S(2)}) %all-to-all-start.3) | async-done | bytes 131104 | tf_op jit(solution)/shard_map/all_to_all | solution.py:990
  47.6 0.0 copy-done.3
  47.6 0.8 %shard_map.274 = (f32[1,160]{1,0:T(1,128)}, f32[1,160]{1,0:T(1,128)}, f32[4,256]{1,0:T(4,128)}, f32[4,256]{1,0:T(4,128)}, f32[4,32]{1,0:T(4,128)}, /*index=5*/f3...) custom-call(f32[256,128]{1,0:T(8,128)S(1)} %bitcast.25, f32[1,256]{1,0:T(1,128)S(1)} %copy-done.3), custom_call_target="tpu_custom_call" | custom-call | flops 100000000 | bytes 1000000 | tf_op jit(solution)/shard_map/pallas_call | solution.py:977
Async XLA Ops:
  2.9 15.7 %all-to-all-start = ((f32[16,32,128]{2,1,0:T(8,128)}), f32[16,32,128]{2,1,0:T(8,128)S(1)}, u32[]{:S(2)}, u32[]{:S(2)}) async-start(f32[16,32,128]{2,1,0:T(8,128)} %bitcast.2), calls=%async_computation | async-start | bytes 524288 | tf_op jit(solution)/shard_map/all_to_all | solution.py:990
  11.7 6.9 %copy-start = (bf16[64,2048]{1,0:T(8,128)(2,1)S(1)}, bf16[64,2048]{1,0:T(8,128)(2,1)}, u32[]{:S(2)}) copy-start(bf16[64,2048]{1,0:T(8,128)(2,1)} %constant.34.clone.from_modes_ref) | copy-start | bytes 786436
  11.7 6.9 %copy-start.1 = (bf16[1024,128]{1,0:T(8,128)(2,1)S(1)}, bf16[1024,128]{1,0:T(8,128)(2,1)}, u32[]{:S(2)}) copy-start(bf16[1024,128]{1,0:T(8,128)(2,1)} %constant.33.clone.to_modes_ref) | copy-start | bytes 786436
  11.7 6.9 %copy-start.2 = (bf16[256,256]{1,0:T(8,128)(2,1)S(1)}, bf16[256,256]{1,0:T(8,128)(2,1)}, u32[]{:S(2)}) copy-start(bf16[256,256]{1,0:T(8,128)(2,1)} %constant.35.clone.earlier_ref.earlier_hbm) | copy-start | bytes 393220
  20.5 9.7 %all-to-all-start.1 = ((f32[8,48,128]{2,1,0:T(8,128)}), f32[8,48,128]{2,1,0:T(8,128)S(1)}, u32[]{:S(2)}, u32[]{:S(2)}) async-start(f32[8,48,128]{2,1,0:T(8,128)} %bitcast.9), calls=%async_computation.1 | async-start | bytes 393216 | tf_op jit(solution)/shard_map/all_to_all | solution.py:990
  25.0 5.1 %collective-permute-start = (f32[120,128]{1,0:T(8,128)S(1)}, f32[120,128]{1,0:T(8,128)S(1)}, u32[]{:S(2)}, u32[]{:S(2)}) collective-permute-start(f32[120,128]{1,0:T(8,128)S(1)} %get-tuple-element.50), channel_id=1, source_target_pairs={{0,16},{2,18},{4,20},{6,22},{8,24},{10,26},{12,28},{14,30},{16,0},... | collective-permute-start | bytes 184328 | tf_op jit(solution)/shard_map/ppermute | solution.py:1094
  39.1 8.5 %all-to-all-start.3 = ((f32[16,16,128]{2,1,0:T(8,128)}), f32[16,16,128]{2,1,0:T(8,128)S(1)}, u32[]{:S(2)}, u32[]{:S(2)}) async-start(f32[16,16,128]{2,1,0:T(8,128)} %bitcast.13), calls=%async_computation.3 | async-start | bytes 262144 | tf_op jit(solution)/shard_map/all_to_all | solution.py:990
  46.8 0.7 %copy-start.3 = (f32[1,256]{1,0:T(1,128)S(1)}, f32[1,256]{1,0:T(1,128)}, u32[]{:S(2)}) copy-start(f32[1,256]{1,0:T(1,128)} %constant.30.clone.endpoint_hbm.endpoint_ref) | copy-start | bytes 3076

commit v8 on v6

--- a/solution.py
+++ b/solution.py
@@ -145,6 +145,8 @@
 
 
 def owner_order(half):
+    if half == 8:
+        return [1, 6, 4, 7, 2, 5, 3, 0]
     return [k ^ 1 for k in range(half)]
 
 

time: 48.9 us -> 48.8 us (level)
    all_to_all x3, starting transfers between devices: 18.7 us -> 18.1 us  [exchange(): lax.all_to_all(value.reshape(count, value.shape[0] // count, value.shape[...]
    all_to_all x3, waiting for transfers between devices: 4.5 us -> 5 us  [exchange(): lax.all_to_all(value.reshape(count, value.shape[0] // count, value.shape[...]
where the time goes in v8:
time: 48.8 us; the launch traced here: 48.3 us
  starting transfers between devices  19.9 us (41%)
  Pallas kernels  14 us (29%)
  blocking collectives  7.92 us (16%)
  waiting for transfers between devices  5.73 us (12%)
  between operations  0.72 us (1%)
    all_to_all x3, starting transfers between devices, exchange(): lax.all_to_all(value.reshape(count, value.shape[0] // count, value.shape[...  18.1 us
    pallas_call x8, Pallas kernels, call(): pl.pallas_call(kernel, out_shape=tuple((jax.ShapeDtypeStruct(shape, kind)...  14 us
    all_to_all x1, blocking collectives, exchange(): lax.all_to_all(value.reshape(count, value.shape[0] // count, value.shape[...  7.92 us
    all_to_all x3, waiting for transfers between devices, exchange(): lax.all_to_all(value.reshape(count, value.shape[0] // count, value.shape[...  5 us
    ppermute x1, starting transfers between devices, body(): lax.ppermute(cot_send, 'seq', [(k, (k + sets) % blocks) for k in range(bl...  1.83 us
  transfers between devices with their start and end apart: 4, of which 3 were waited for; matrix products, arithmetic and copies ran while one was open for 0% of the time, Pallas kernels for 17%

profile of v8, /device:TPU:0, one launch (start us, length us, event | category | flops | bytes accessed | tf_op | source)
XLA Modules:
  0.0 48.3 jit_solution(16506275879102484940)
XLA Ops:
  0.6 2.2 %shard_map.267 = (f32[512,128]{1,0:T(8,128)}, f32[160,128]{1,0:T(8,128)S(1)}) custom-call(f32[1,160,90]{2,1,0:T(8,128)} %series_hbm.3, f32[1,160,90]{2,1,0:T(8,128)} %cot_hbm.5, f32[160,160]{1,0:T(8,128)} %mixing_hbm.3, s32[1,160]{1,0:T(1,128)} %bitcast.30), custom_call_target="tpu_custom_call" | custom-call | flops 100000000 | bytes 1000000 | tf_op jit(solution)/shard_map/pallas_call | solution.py:979
  2.9 8.8 %all-to-all-start = ((f32[16,32,128]{2,1,0:T(8,128)}), f32[16,32,128]{2,1,0:T(8,128)S(1)}, u32[]{:S(2)}, u32[]{:S(2)}) async-start(f32[16,32,128]{2,1,0:T(8,128)} %bitcast.2), calls=%async_computation | async-start | bytes 524288 | tf_op jit(solution)/shard_map/all_to_all | solution.py:992
  11.7 0.0 copy-start
  11.7 0.0 copy-start.1
  11.7 0.0 copy-start.2
  11.7 3.1 %shard_map.268 = (bf16[1024,256]{1,0:T(8,128)(2,1)S(1)}, f32[32,1024]{1,0:T(8,128)S(1)}, f32[80,128]{1,0:T(8,128)S(1)}, f32[160,128]{1,0:T(8,128)S(1)}, bf16[2,1...) custom-call(s32[1]{0:T(128)} %bitcast.place_ref, ...), custom_call_target="tpu_custom_call" | custom-call | flops 4000000000 | bytes 8000000 | tf_op jit(solution)/shard_map/pallas_call | solution.py:979
  14.8 4.3 %all-to-all-done = f32[16,32,128]{2,1,0:T(8,128)S(1)} async-done(((f32[16,32,128]{2,1,0:T(8,128)}), f32[16,32,128]{2,1,0:T(8,128)S(1)}, u32[]{:S(2)}, u32[]{:S(2)}) %all-to-all-start) | async-done | bytes 262176 | tf_op jit(solution)/shard_map/all_to_all | solution.py:992
  19.1 0.0 copy-done
  19.1 0.0 copy-done.1
  19.1 0.0 copy-done.2
  19.1 1.9 %shard_map.269 = (f32[384,128]{1,0:T(8,128)}, f32[384,128]{1,0:T(8,128)S(1)}, f32[384,128]{1,0:T(8,128)S(1)}, f32[384,128]{1,0:T(8,128)S(1)}, f32[384,128]{1,0:T...) custom-call(s32[1]{0:T(128)} %bitcast.place_ref, f32[512,128]{1,0:T(8,128)S(1)} %bitcast.20, ...), custom_call_target="tpu_custom_call" | custom-call | flops 100000000 | bytes 1000000 | tf_op jit(solution)/shard_map/pallas_call | solution.py:979
  21.0 3.9 %all-to-all-start.1 = ((f32[8,48,128]{2,1,0:T(8,128)}), f32[8,48,128]{2,1,0:T(8,128)S(1)}, u32[]{:S(2)}, u32[]{:S(2)}) async-start(f32[8,48,128]{2,1,0:T(8,128)} %bitcast.9), calls=%async_computation.1 | async-start | bytes 393216 | tf_op jit(solution)/shard_map/all_to_all | solution.py:992
  24.9 1.8 %collective-permute-start = (f32[120,128]{1,0:T(8,128)S(1)}, f32[120,128]{1,0:T(8,128)S(1)}, u32[]{:S(2)}, u32[]{:S(2)}) collective-permute-start(f32[120,128]{1,0:T(8,128)S(1)} %get-tuple-element.50), channel_id=1, source_target_pairs={{0,16},{2,18},{4,20},{6,22},{8,24},{10,26},{12,28},{14,30},{16,0},... | collective-permute-start | bytes 184328 | tf_op jit(solution)/shard_map/ppermute | solution.py:1096
  26.7 2.6 %shard_map.270 = (f32[24,128]{1,0:T(8,128)S(1)}, f32[16,128]{1,0:T(8,128)S(1)}) custom-call(s32[1]{0:T(128)} %bitcast.place_ref, f32[512,128]{1,0:T(8,128)S(1)} %bitcast.21, f32[80,128]{1,0:T(8,128)S(1)} %get-tuple-element.43.own_ref, f32[384,128]{1,0:T(8,128)S(1)} %get-tuple-element.51.mean_ref, f32[384,128]{1,0:T(8,128)S(1)} %get-tuple-element.52.inverse_ref, ...), custom_call_target="tpu_custom_call" | custom-call | flops 4000000000 | bytes 8000000 | tf_op jit(solution)/shard_map/pallas_call | solution.py:979
  29.3 0.7 %collective-permute-done.cot_partner_ref = f32[120,128]{1,0:T(8,128)S(1)} collective-permute-done((f32[120,128]{1,0:T(8,128)S(1)}, f32[120,128]{1,0:T(8,128)S(1)}, u32[]{:S(2)}, u32[]{:S(2)}) %collective-permute-start) | collective-permute-done | bytes 61472 | tf_op jit(solution)/shard_map/ppermute | solution.py:1096
  30.0 0.0 all-to-all-done.1
  30.0 0.4 shard_map.271
  30.4 7.9 %all_to_all.20 = f32[16,16,128]{2,1,0:T(8,128)S(1)} all-to-all(f32[16,16,128]{2,1,0:T(8,128)S(1)} %bitcast.24), channel_id=1, replica_groups={{15,1,12,8,14,11,7,3,4,2,5,6,0,10,9,13},{31,17,28,24,30,27,23,19,20,18,..., dimensions={0} | all-to-all | bytes 262144 | tf_op jit(solution)/shard_map/all_to_all | solution.py:992
  38.3 0.7 %shard_map.273 = f32[256,128]{1,0:T(8,128)} custom-call(f32[256,128]{1,0:T(8,128)S(1)} %bitcast.26), custom_call_target="tpu_custom_call" | custom-call | flops 100000000 | bytes 1000000 | tf_op jit(solution)/shard_map/pallas_call | solution.py:979
  39.0 5.4 %all-to-all-start.3 = ((f32[16,16,128]{2,1,0:T(8,128)}), f32[16,16,128]{2,1,0:T(8,128)S(1)}, u32[]{:S(2)}, u32[]{:S(2)}) async-start(f32[16,16,128]{2,1,0:T(8,128)} %bitcast.13), calls=%async_computation.3 | async-start | bytes 262144 | tf_op jit(solution)/shard_map/all_to_all | solution.py:992
  44.4 2.4 %shard_map.272 = (f32[1,160,90]{2,1,0:T(8,128)}, f32[1,160,90]{2,1,0:T(8,128)}) custom-call(s32[1]{0:T(128)} %bitcast.place_ref, f32[384,128]{1,0:T(8,128)S(1)} %bitcast.23, f32[256,128]{1,0:T(8,128)S(1)} %bitcast.27, f32[160,128]{1,0:T(8,128)S(1)} %get-tuple-element.61.grad_ref, f32[160,128]{1,0:T(8,128)S(1)} %get-tuple-element.62.columns_ref, ...), custom_call_target="tpu_custom_call" | custom-call | flops 4000000000 | bytes 8000000 | tf_op jit(solution)/shard_map/pallas_call | solution.py:979
  46.8 0.0 copy-start.3
  46.8 0.7 %all-to-all-done.3 = f32[16,16,128]{2,1,0:T(8,128)S(1)} async-done(((f32[16,16,128]{2,1,0:T(8,128)}), f32[16,16,128]{2,1,0:T(8,128)S(1)}, u32[]{:S(2)}, u32[]{:S(2)}) %all-to-all-start.3) | async-done | bytes 131104 | tf_op jit(solution)/shard_map/all_to_all | solution.py:992
  47.5 0.0 copy-done.3
  47.5 0.8 %shard_map.274 = (f32[1,160]{1,0:T(1,128)}, f32[1,160]{1,0:T(1,128)}, f32[4,256]{1,0:T(4,128)}, f32[4,256]{1,0:T(4,128)}, f32[4,32]{1,0:T(4,128)}, /*index=5*/f3...) custom-call(f32[256,128]{1,0:T(8,128)S(1)} %bitcast.25, f32[1,256]{1,0:T(1,128)S(1)} %copy-done.3), custom_call_target="tpu_custom_call" | custom-call | flops 100000000 | bytes 1000000 | tf_op jit(solution)/shard_map/pallas_call | solution.py:979
Async XLA Ops:
  2.9 16.2 %all-to-all-start = ((f32[16,32,128]{2,1,0:T(8,128)}), f32[16,32,128]{2,1,0:T(8,128)S(1)}, u32[]{:S(2)}, u32[]{:S(2)}) async-start(f32[16,32,128]{2,1,0:T(8,128)} %bitcast.2), calls=%async_computation | async-start | bytes 524288 | tf_op jit(solution)/shard_map/all_to_all | solution.py:992
  11.7 7.4 %copy-start = (bf16[64,2048]{1,0:T(8,128)(2,1)S(1)}, bf16[64,2048]{1,0:T(8,128)(2,1)}, u32[]{:S(2)}) copy-start(bf16[64,2048]{1,0:T(8,128)(2,1)} %constant.34.clone.from_modes_ref) | copy-start | bytes 786436
  11.7 7.4 %copy-start.1 = (bf16[1024,128]{1,0:T(8,128)(2,1)S(1)}, bf16[1024,128]{1,0:T(8,128)(2,1)}, u32[]{:S(2)}) copy-start(bf16[1024,128]{1,0:T(8,128)(2,1)} %constant.33.clone.to_modes_ref) | copy-start | bytes 786436
  11.7 7.4 %copy-start.2 = (bf16[256,256]{1,0:T(8,128)(2,1)S(1)}, bf16[256,256]{1,0:T(8,128)(2,1)}, u32[]{:S(2)}) copy-start(bf16[256,256]{1,0:T(8,128)(2,1)} %constant.35.clone.earlier_ref.earlier_hbm) | copy-start | bytes 393220
  21.0 9.0 %all-to-all-start.1 = ((f32[8,48,128]{2,1,0:T(8,128)}), f32[8,48,128]{2,1,0:T(8,128)S(1)}, u32[]{:S(2)}, u32[]{:S(2)}) async-start(f32[8,48,128]{2,1,0:T(8,128)} %bitcast.9), calls=%async_computation.1 | async-start | bytes 393216 | tf_op jit(solution)/shard_map/all_to_all | solution.py:992
  24.9 5.1 %collective-permute-start = (f32[120,128]{1,0:T(8,128)S(1)}, f32[120,128]{1,0:T(8,128)S(1)}, u32[]{:S(2)}, u32[]{:S(2)}) collective-permute-start(f32[120,128]{1,0:T(8,128)S(1)} %get-tuple-element.50), channel_id=1, source_target_pairs={{0,16},{2,18},{4,20},{6,22},{8,24},{10,26},{12,28},{14,30},{16,0},... | collective-permute-start | bytes 184328 | tf_op jit(solution)/shard_map/ppermute | solution.py:1096
  39.0 8.5 %all-to-all-start.3 = ((f32[16,16,128]{2,1,0:T(8,128)}), f32[16,16,128]{2,1,0:T(8,128)S(1)}, u32[]{:S(2)}, u32[]{:S(2)}) async-start(f32[16,16,128]{2,1,0:T(8,128)} %bitcast.13), calls=%async_computation.3 | async-start | bytes 262144 | tf_op jit(solution)/shard_map/all_to_all | solution.py:992
  46.8 0.7 %copy-start.3 = (f32[1,256]{1,0:T(1,128)S(1)}, f32[1,256]{1,0:T(1,128)}, u32[]{:S(2)}) copy-start(f32[1,256]{1,0:T(1,128)} %constant.30.clone.endpoint_hbm.endpoint_ref) | copy-start | bytes 3076
